TPU v7x, 128 devices: a whole 4x4x4 slice. The times are simulated.
128 devices in a mesh: leaf: 128 (over z, y, x, core).
Axes of the slice: x: 4, y: 4, z: 4, core: 2. Of those that a mesh axis runs over, the one named last changes fastest.
Arguments:
- points: float32 [16, 524288], P(None, 'leaf'), may hold values from -6 to 6
- charges: float32 [16, 524288], P(None, 'leaf'), may hold values from -1.2 to 1.2
- leaf_basis: float32 [64, 524288], P(None, 'leaf'), may hold values from -0.5 to 0.5
- local_transfer: float32 [7936, 4096], P('leaf'), may hold values from -0.625 to 0.625
- local_anchors: float32 [8064, 1024], P('leaf'), may hold values from -6 to 6
- local_lists: int32 [8064, 8], P('leaf'), may hold values from -1 to 4095, as said below
- near_blocks: int32 [4096, 8], P('leaf'), may hold values from -1 to 4095, as said below
- top_transfer: float32 [254, 4096], replicated, may hold values from -0.625 to 0.625
- top_anchors: float32 [127, 1024], replicated, may hold values from -6 to 6
- top_lists: int32 [127, 8], replicated, may hold values from -1 to 63, as said below
Outputs:
- potential: float32 [16, 524288], P(None, 'leaf')
Inputs may be any that keep to these rules, and one draw needn't show every extreme that they name: `near_blocks`: entry 0 of row t is t itself; the other entries of a row are distinct leaves u != t with |u - t| <= 16, or -1 for no block. `local_lists`: the entries of a row are distinct; each is -1 (none) or a cluster p of the row's level with 2 <= |p - c| <= 6, where c is the row's cluster. `top_lists`: the entries of a row are distinct; each is -1 (none) or a cluster p of the row's level with 2 <= |p - c| <= 6, where c is the row's cluster.
All inputs are finite; a program needn't handle non-finite values.
Results may differ from a plain program's by a relative error of at most 0.0003.
Values sent between devices are 32-bit elements; how exact they have to be, the bound alone decides.
No kernel may reach another device: no remote copies, remote signals or barrier semaphores. Data moves between devices by JAX's collectives and lax.ppermute only.
A program may use at most 128 MiB of HBM per device.

v0:
```python
import jax
import jax.numpy as jnp
from jax import lax
from jax.sharding import PartitionSpec as P

DIM = 16
RHS = 16
LEAF = 128
RANK = 64
LEAVES_DEV = 32
NREACH = 16
REACH = 6


length_scale = 3.0
highest = lax.Precision.HIGHEST


def from_behind(value, axis, by):
    length = lax.axis_size(axis)
    pairs = [(i, i + by) for i in range(length) if 0 <= i + by < length]
    return lax.ppermute(value, axis, pairs)


def padded(block, sides, width):
    for axis, dim in sides:
        count = lax.axis_size(axis)
        forward = [(i, i + 1) for i in range(count - 1)]
        backward = [(target, source) for source, target in forward]
        low = lax.ppermute(
            lax.slice_in_dim(block, block.shape[dim] - width, None, axis=dim), axis, forward
        )
        high = lax.ppermute(lax.slice_in_dim(block, 0, width, axis=dim), axis, backward)
        block = jnp.concatenate([low, block, high], axis=dim)
    return block


def matern_block(row_points, column_points):
    cross = jnp.einsum("...ad,...bd->...ab", row_points, column_points, precision=highest)
    row_norms = jnp.sum(row_points * row_points, axis=-1)[..., :, None]
    column_norms = jnp.sum(column_points * column_points, axis=-1)[..., None, :]
    squared = jnp.maximum(row_norms + column_norms - 2.0 * cross, 0.0)
    scaled = jnp.sqrt(3.0 * squared) / length_scale
    return (1.0 + scaled) * jnp.exp(-scaled)


def far_field(own_anchors, lists, source_moments, source_anchors, first_index):
    clusters = lists.shape[0]
    block_size = min(clusters, 128)
    usable = lists >= 0
    located = jnp.clip(lists - first_index, 0, source_moments.shape[0] - 1)

    def far_one_block(inputs):
        anchors_block, located_block, usable_block = inputs
        partner_moments = jnp.where(
            usable_block[:, :, None, None], jnp.take(source_moments, located_block, axis=0), 0.0
        )
        partner_anchors = jnp.take(source_anchors, located_block, axis=0)
        own_block = jnp.broadcast_to(anchors_block[:, None], partner_anchors.shape)
        kernel = matern_block(own_block, partner_anchors)
        return jnp.einsum("cnab,cnbs->cas", kernel, partner_moments, precision=highest)

    blocks = clusters // block_size
    results = lax.map(
        far_one_block,
        (
            own_anchors.reshape((blocks, block_size) + own_anchors.shape[1:]),
            located.reshape(blocks, block_size, -1),
            usable.reshape(blocks, block_size, -1),
        ),
    )
    return results.reshape((clusters,) + results.shape[2:])


def near_field(target_leaves, source_leaves, source_charges, near_blocks, first_index):
    leaf_count = target_leaves.shape[0]
    block_size = min(leaf_count, 16)
    usable = near_blocks >= 0
    located = jnp.clip(near_blocks - first_index, 0, source_leaves.shape[0] - 1)

    def near_one_block(inputs):
        targets, located_block, usable_block = inputs
        partner_points = jnp.take(source_leaves, located_block, axis=0)
        partner_charges = jnp.where(
            usable_block[:, :, None, None], jnp.take(source_charges, located_block, axis=0), 0.0
        )
        own_block = jnp.broadcast_to(targets[:, None], partner_points.shape)
        kernel = matern_block(own_block, partner_points)
        return jnp.einsum("bnpq,bnqs->bps", kernel, partner_charges, precision=highest)

    blocks = leaf_count // block_size
    results = lax.map(
        near_one_block,
        (
            target_leaves.reshape((blocks, block_size) + target_leaves.shape[1:]),
            located.reshape(blocks, block_size, -1),
            usable.reshape(blocks, block_size, -1),
        ),
    )
    return results.reshape((leaf_count,) + results.shape[2:])


def upward(transfer, moments):
    lifted = jnp.einsum("cab,cas->cbs", transfer, moments, precision=highest)
    return lifted[0::2] + lifted[1::2]


def downward(transfer, parents):
    return jnp.einsum("cab,cbs->cas", transfer, jnp.repeat(parents, 2, axis=0), precision=highest)


def rim_shape(number):
    rim_width = min(number, REACH)
    reach_devices = -(-REACH // number)
    return (rim_width, reach_devices)


def pull_level(moments_part, anchors_part, stride):
    return from_behind((moments_part, anchors_part), "leaf", stride)


def on_device(
    points,
    charges,
    leaf_basis,
    local_transfer,
    local_anchors,
    local_lists,
    near_blocks,
    top_transfer,
    top_anchors,
    top_lists,
):
    devices = lax.axis_size("leaf")
    device = lax.axis_index("leaf")
    local_depth = LEAVES_DEV.bit_length() - 1
    top_depth = devices.bit_length() - 1
    basis_leaves = leaf_basis.reshape(RANK, LEAVES_DEV, LEAF)
    charge_leaves = charges.reshape(RHS, LEAVES_DEV, LEAF)
    stacked = jnp.concatenate([points, charges], axis=0)
    target_leaves = points.reshape(DIM, LEAVES_DEV, LEAF).transpose(1, 2, 0)
    extended = padded(stacked, (("leaf", 1),), NREACH * LEAF)
    source_leaves = extended.reshape(DIM + RHS, -1, LEAF).transpose(1, 2, 0)
    near_term = near_field(
        target_leaves,
        source_leaves[:, :, :DIM],
        source_leaves[:, :, DIM:],
        near_blocks,
        device * LEAVES_DEV - NREACH,
    )
    transfer_rows = local_transfer.reshape(-1, RANK, RANK)
    anchor_rows = local_anchors.reshape(-1, RANK, DIM)
    moments = [jnp.einsum("rtp,stp->trs", basis_leaves, charge_leaves, precision=highest)]
    anchors_by_level = []
    lists_by_level = []
    transfer_by_level = []
    for height in range(local_depth + 1):
        number = LEAVES_DEV >> height
        first_row = 2 * LEAVES_DEV - 2 * number
        anchors_by_level.append(anchor_rows[first_row : first_row + number])
        lists_by_level.append(local_lists[first_row : first_row + number])
        if height < local_depth:
            transfer_by_level.append(transfer_rows[first_row : first_row + number])
            moments.append(upward(transfer_by_level[-1], moments[-1]))
    leading = [[] for height in range(local_depth + 1)]
    trailing = [[] for height in range(local_depth + 1)]
    for height in range(local_depth + 1):
        number = LEAVES_DEV >> height
        rim_width, reach_devices = rim_shape(number)
        for stride in range(reach_devices, 0, -1):
            leading[height].append(
                pull_level(
                    moments[height][number - rim_width :],
                    anchors_by_level[height][number - rim_width :],
                    stride,
                )
            )
        for stride in range(1, reach_devices + 1):
            trailing[height].append(
                pull_level(
                    moments[height][:rim_width], anchors_by_level[height][:rim_width], -stride
                )
            )
    far_terms = []
    for height in range(local_depth + 1):
        number = LEAVES_DEV >> height
        rim_width, reach_devices = rim_shape(number)
        source_moments = jnp.concatenate(
            [piece[0] for piece in leading[height]]
            + [moments[height]]
            + [piece[0] for piece in trailing[height]],
            axis=0,
        )
        source_anchors = jnp.concatenate(
            [piece[1] for piece in leading[height]]
            + [anchors_by_level[height]]
            + [piece[1] for piece in trailing[height]],
            axis=0,
        )
        far_terms.append(
            far_field(
                anchors_by_level[height],
                lists_by_level[height],
                source_moments,
                source_anchors,
                device * number - reach_devices * rim_width,
            )
        )
    top_rows = top_transfer.reshape(-1, RANK, RANK)
    top_anchor_rows = top_anchors.reshape(-1, RANK, DIM)
    root_moments = moments[local_depth]
    upper_far = [None]
    level_moments = lax.all_gather(root_moments, "leaf", axis=0, tiled=True)
    for height in range(1, top_depth + 1):
        number_below = devices >> height - 1
        child_row = 2 * devices - 2 * number_below
        level_moments = upward(top_rows[child_row : child_row + number_below], level_moments)
        number = devices >> height
        first_row = devices - (devices >> height - 1)
        cluster = device // (1 << height)
        anchors_here = top_anchor_rows[first_row : first_row + number]
        own_anchor = lax.dynamic_slice_in_dim(anchors_here, cluster, 1, 0)
        own_list = lax.dynamic_slice_in_dim(
            top_lists[first_row : first_row + number], cluster, 1, 0
        )
        upper_far.append(far_field(own_anchor, own_list, level_moments, anchors_here, 0))
    expansion = upper_far[top_depth]
    for height in range(top_depth - 1, -1, -1):
        number = devices >> height
        first_row = 2 * devices - 2 * number
        cluster = device // (1 << height)
        own_transfer = lax.dynamic_slice_in_dim(top_rows, first_row + cluster, 1, 0)
        pushed = jnp.einsum("cab,cbs->cas", own_transfer, expansion, precision=highest)
        if height == 0:
            expansion = far_terms[local_depth] + pushed
        else:
            expansion = upper_far[height] + pushed
    for height in range(local_depth - 1, -1, -1):
        expansion = far_terms[height] + downward(transfer_by_level[height], expansion)
    far_points = jnp.einsum("rtp,trs->stp", basis_leaves, expansion, precision=highest).reshape(
        RHS, -1
    )
    near_points = near_term.transpose(2, 0, 1).reshape(RHS, -1)
    return near_points + far_points


def solution(mesh):
    in_specs = (
        P(None, "leaf"),
        P(None, "leaf"),
        P(None, "leaf"),
        P("leaf", None),
        P("leaf", None),
        P("leaf", None),
        P("leaf", None),
        P(),
        P(),
        P(),
    )
    out_specs = P(None, "leaf")
    return jax.shard_map(
        on_device, mesh=mesh, in_specs=in_specs, out_specs=out_specs, check_vma=False
    )
```

profile of v0, /device:TPU:32, one launch (start us, length us, event | category | flops | bytes accessed | tf_op | source)
XLA Modules:
  0.0 763.9 jit_solution(13047631103616169027)
XLA Ops:
  6.9 7.9 %collective-permute-start.16 = (f32[4,64,16]{2,1,0:T(8,128)}, f32[4,64,16]{2,1,0:T(8,128)}, u32[]{:S(2)}, u32[]{:S(2)}) collective-permute-start(f32[4,64,16]{2,1,0:T(8,128)} %broadcast_in_dim.633), channel_id=1, source_target_pairs={{1,0},{2,1},{3,2},{4,3},{5,4},{6,5},{7,6},{8,7},{9,8},{10,9},{11,1... | collective-permute-start | bytes 49160 | tf_op jit(solution)/shard_map/ppermute | solution.py:22
  55.9 40.6 %all_gather.3 = f32[128,64,16]{1,2,0:T(8,128)} all-gather(f32[1,64,16]{1,2,0:T(8,128)} %slice_add_fusion.11), channel_id=1, replica_groups=mesh['leaf'=128] {'leaf'}, dimensions={0}, use_global_device_ids=true | all-gather | bytes 528384 | tf_op jit(solution)/shard_map/all_gather | solution.py:213
  199.0 7.7 %dynamic-slice_reduce_fusion = (f32[64,64]{1,0:T(8,128)S(1)}, f32[64,64]{1,0:T(8,128)S(1)}, f32[64,64]{1,0:T(8,128)S(1)}, f32[64,64]{1,0:T(8,128)S(1)}, f32[64,6...) fusion(f32[254,64,64]{0,2,1:T(8,128)S(1)} %bitcast.464, s32[]{:T(128)S(6)} %select_n.321, ...), kind=kLoop, calls=%fused_computation.109 | loop fusion | bytes 229404 | tf_op jit(solution)/shard_map/dynamic_slice | solution.py:232
  250.4 7.7 %collective-permute-done.50 = f32[1,64,16]{1,2,0:T(8,128)S(1)} collective-permute-done((f32[1,64,16]{1,2,0:T(8,128)}, f32[1,64,16]{1,2,0:T(8,128)S(1)}, u32[]{:S(2)}, u32[]{:S(2)}) %collective-permute-start.50) | collective-permute-done | bytes 4128 | tf_op jit(solution)/shard_map/ppermute | solution.py:22
  260.0 7.5 collective-permute-done.51
  285.9 8.1 %collective-permute-done.36 = f32[1,64,16]{1,2,0:T(8,128)S(1)} collective-permute-done((f32[1,64,16]{1,2,0:T(8,128)S(1)}, f32[1,64,16]{1,2,0:T(8,128)S(1)}, u32[]{:S(2)}, u32[]{:S(2)}) %collective-permute-start.36) | collective-permute-done | bytes 4128 | tf_op jit(solution)/shard_map/ppermute | solution.py:22
  296.0 7.5 collective-permute-done.37
  305.4 7.8 %collective-permute-done.38 = f32[1,64,16]{1,2,0:T(8,128)S(1)} collective-permute-done((f32[1,64,16]{1,2,0:T(8,128)S(1)}, f32[1,64,16]{1,2,0:T(8,128)S(1)}, u32[]{:S(2)}, u32[]{:S(2)}) %collective-permute-start.38) | collective-permute-done | bytes 4128 | tf_op jit(solution)/shard_map/ppermute | solution.py:22
  315.2 7.2 collective-permute-done.39
  339.0 7.8 %collective-permute-start.43 = (f32[1,64,16]{1,2,0:T(8,128)S(1)}, f32[1,64,16]{1,2,0:T(8,128)S(1)}, u32[]{:S(2)}, u32[]{:S(2)}) collective-permute-start(f32[1,64,16]{1,2,0:T(8,128)S(1)} %copy.346), channel_id=1, source_target_pairs={{4,0},{5,1},{6,2},{7,3},{8,4},{9,5},{10,6},{11,7},{12,8},{13,9},{1... | collective-permute-start | bytes 12296 | tf_op jit(solution)/shard_map/ppermute | solution.py:22
  356.5 8.1 %collective-permute-start.45 = (f32[1,64,16]{1,2,0:T(8,128)S(1)}, f32[1,64,16]{1,2,0:T(8,128)S(1)}, u32[]{:S(2)}, u32[]{:S(2)}) collective-permute-start(f32[1,64,16]{1,2,0:T(8,128)S(1)} %copy.346), channel_id=1, source_target_pairs={{6,0},{7,1},{8,2},{9,3},{10,4},{11,5},{12,6},{13,7},{14,8},{15,9},... | collective-permute-start | bytes 12296 | tf_op jit(solution)/shard_map/ppermute | solution.py:22
  365.9 9.9 %collective-permute-start.52 = (f32[1,64,16]{1,2,0:T(8,128)}, f32[1,64,16]{1,2,0:T(8,128)S(1)}, u32[]{:S(2)}, u32[]{:S(2)}) collective-permute-start(f32[1,64,16]{1,2,0:T(8,128)} %slice_add_fusion.11), channel_id=1, source_target_pairs={{1,0},{2,1},{3,2},{4,3},{5,4},{6,5},{7,6},{8,7},{9,8},{10,9},{11,1... | collective-permute-start | bytes 12296 | tf_op jit(solution)/shard_map/ppermute | solution.py:22
  391.1 7.8 %collective-permute-start.55 = (f32[1,64,16]{1,2,0:T(8,128)}, f32[1,64,16]{1,2,0:T(8,128)S(1)}, u32[]{:S(2)}, u32[]{:S(2)}) collective-permute-start(f32[1,64,16]{1,2,0:T(8,128)} %slice_add_fusion.11), channel_id=1, source_target_pairs={{4,0},{5,1},{6,2},{7,3},{8,4},{9,5},{10,6},{11,7},{12,8},{13,9},{1... | collective-permute-start | bytes 12296 | tf_op jit(solution)/shard_map/ppermute | solution.py:22
  409.0 8.1 %collective-permute-start.57 = (f32[1,64,16]{1,2,0:T(8,128)}, f32[1,64,16]{1,2,0:T(8,128)S(1)}, u32[]{:S(2)}, u32[]{:S(2)}) collective-permute-start(f32[1,64,16]{1,2,0:T(8,128)} %slice_add_fusion.11), channel_id=1, source_target_pairs={{6,0},{7,1},{8,2},{9,3},{10,4},{11,5},{12,6},{13,7},{14,8},{15,9},... | collective-permute-start | bytes 12296 | tf_op jit(solution)/shard_map/ppermute | solution.py:22
  440.0 7.3 collective-permute-done.30
  449.3 8.1 %collective-permute-done.22 = f32[2,64,16]{2,1,0:T(8,128)S(1)} collective-permute-done((f32[2,64,16]{2,1,0:T(8,128)S(1)}, f32[2,64,16]{2,1,0:T(8,128)S(1)}, u32[]{:S(2)}, u32[]{:S(2)}) %collective-permute-start.22) | collective-permute-done | bytes 8224 | tf_op jit(solution)/shard_map/ppermute | solution.py:22
  459.4 8.4 %collective-permute-done.23 = f32[2,64,16]{2,1,0:T(8,128)S(1)} collective-permute-done((f32[2,64,16]{2,1,0:T(8,128)S(1)}, f32[2,64,16]{2,1,0:T(8,128)S(1)}, u32[]{:S(2)}, u32[]{:S(2)}) %collective-permute-start.23) | collective-permute-done | bytes 8224 | tf_op jit(solution)/shard_map/ppermute | solution.py:22
  469.8 7.8 %collective-permute-done.24 = f32[2,64,16]{2,1,0:T(8,128)S(1)} collective-permute-done((f32[2,64,16]{2,1,0:T(8,128)S(1)}, f32[2,64,16]{2,1,0:T(8,128)S(1)}, u32[]{:S(2)}, u32[]{:S(2)}) %collective-permute-start.24) | collective-permute-done | bytes 8224 | tf_op jit(solution)/shard_map/ppermute | solution.py:22
  495.9 12.7 %collective-permute-start.31 = (f32[2,64,16]{1,2,0:T(8,128)S(1)}, f32[2,64,16]{1,2,0:T(8,128)S(1)}, u32[]{:S(2)}, u32[]{:S(2)}) collective-permute-start(f32[2,64,16]{1,2,0:T(8,128)S(1)} %copy-done.60), channel_id=1, source_target_pairs={{1,0},{2,1},{3,2},{4,3},{5,4},{6,5},{7,6},{8,7},{9,8},{10,9},{11,1... | collective-permute-start | bytes 24584 | tf_op jit(solution)/shard_map/ppermute | solution.py:22
  555.3 7.6 collective-permute-start.5
  573.2 7.4 collective-permute-start.7
  583.8 16.7 %fusion.91 = f32[32,8,64,64]{3,2,1,0:T(8,128)} fusion(f32[32,8,64,16]{2,3,1,0:T(8,128)S(1)} %bitcast.466, f32[32,64,16]{1,2,0:T(8,128)} %copy-done.18, pred[32,8]{1,0:T(8,128)(4,1)S(1)} %copy.288), kind=kOutput, calls=%fused_computation.131 | convolution fusion | flops 201588736 | bytes 5374208 | tf_op jit(solution)/shard_map/while/body/eval_jaxpr/...ad,...bd->...ab/dot_general | solution.py:39
  601.9 7.8 %collective-permute-start.11 = (f32[6,64,16]{2,1,0:T(8,128)}, f32[6,64,16]{2,1,0:T(8,128)S(1)}, u32[]{:S(2)}, u32[]{:S(2)}) collective-permute-start(f32[6,64,16]{2,1,0:T(8,128)} %slice.351), channel_id=1, source_target_pairs={{1,0},{2,1},{3,2},{4,3},{5,4},{6,5},{7,6},{8,7},{9,8},{10,9},{11,1... | collective-permute-start | bytes 73736 | tf_op jit(solution)/shard_map/ppermute | solution.py:22
  614.9 8.5 %fusion.182 = f32[16,8,64,64]{3,2,1,0:T(8,128)} fusion(f32[16,8,64,16]{2,3,1,0:T(8,128)S(1)} %bitcast.468, f32[16,64,16]{1,2,0:T(8,128)S(1)} %copy-done.26, pred[16,8]{1,0:T(8,128)(4,1)S(1)} %copy.300), kind=kOutput, calls=%fused_computation.264 | convolution fusion | flops 100794368 | bytes 2687104 | tf_op jit(solution)/shard_map/while/body/eval_jaxpr/...ad,...bd->...ab/dot_general | solution.py:39
  625.9 7.9 %collective-permute-start.9 = (f32[6,64,16]{1,2,0:T(8,128)S(1)}, f32[6,64,16]{1,2,0:T(8,128)S(1)}, u32[]{:S(2)}, u32[]{:S(2)}) collective-permute-start(f32[6,64,16]{1,2,0:T(8,128)S(1)} %copy-done.64), channel_id=1, source_target_pairs={{1,0},{2,1},{3,2},{4,3},{5,4},{6,5},{7,6},{8,7},{9,8},{10,9},{11,1... | collective-permute-start | bytes 73736 | tf_op jit(solution)/shard_map/ppermute | solution.py:22
  642.2 7.9 %collective-permute-start.13 = (f32[6,64,16]{1,2,0:T(8,128)S(1)}, f32[6,64,16]{1,2,0:T(8,128)S(1)}, u32[]{:S(2)}, u32[]{:S(2)}) collective-permute-start(f32[6,64,16]{1,2,0:T(8,128)S(1)} %copy-done.62), channel_id=1, source_target_pairs={{1,0},{2,1},{3,2},{4,3},{5,4},{6,5},{7,6},{8,7},{9,8},{10,9},{11,1... | collective-permute-start | bytes 73736 | tf_op jit(solution)/shard_map/ppermute | solution.py:22
  673.5 12.8 %fusion.146 = f32[32,64,16]{1,2,0:T(8,128)S(1)} fusion(f32[32,8,64,16]{2,3,1,0:T(8,128)S(1)} %bitcast.470, f32[32,8,64,64]{3,2,1,0:T(8,128)S(1)} %bitcast.476, f32[32,8,64]{2,1,0:T(8,128)S(1)} %copy-done.46, f32[32,64]{1,0:T(8,128)S(1)} %copy-done.70, pred[32,8]{1,0:T(8,128)(4,1)S(1)} %copy.288, pred[32,8]{1,0:T(8,128)(4,1)S(1)} %copy-done.94), kind=kOutput, calls=%fused_computation.202 | convolution fusion | flops 211288064 | bytes 5448192 | tf_op jit(solution)/shard_map/while/body/eval_jaxpr/cnab,cnbs->cas/dot_general | solution.py:61
  690.9 70.0 %while.2 = (s32[]{:T(128)}, f32[2,16,128,16]{2,3,1,0:T(8,128)}, f32[2,16,128,16]{2,3,1,0:T(8,128)S(1)}, s32[2,16,8]{1,0,2:T(2,128)}, f32[64,128,16]{1,2,0:T(8,12...) while((s32[]{:T(128)}, f32[2,16,128,16]{2,3,1,0:T(8,128)}, ...), condition=%wide.region_3.5_spmd, body=%wide.region_0.4_spmd.sunk | while | flops 825802880 | bytes 24801800 | solution.py:92
  694.1 15.5 %fusion.499 = f32[16,8,128,128]{3,2,1,0:T(8,128)} fusion(f32[16,8,128,16]{2,3,1,0:T(8,128)S(1)} %bitcast.461, f32[16,128,16]{1,2,0:T(8,128)S(1)} %get-tuple-element.493, pred[16,8]{1,0:T(8,128)(4,1)S(1)} %copy.450), kind=kOutput, calls=%fused_computation.49.clone.1 | convolution fusion | flops 402915328 | bytes 9568384 | tf_op jit(solution)/shard_map/while/body/eval_jaxpr/...ad,...bd->...ab/dot_general | solution.py:39
  710.9 15.2 %fusion.500 = f32[2,16,128,16]{2,3,1,0:T(8,128)} fusion(f32[2,16,128,16]{2,3,1,0:T(8,128)} %get-tuple-element.504, s32[]{:T(128)S(6)} %copy.456, f32[16,8,128,128]{3,2,1,0:T(8,128)} %fusion.499, f32[16,8,128]{2,1,0:T(8,128)S(1)} %multiply_reduce_fusion.30, f32[16,128]{1,0:T(8,128)S(1)} %get-tuple-element.494, f32[16,8,128,16]{2,3,1,0:T(8,128)S(1)} %bitcast.463, ...), kind=kOutput, calls=%fused_computation.46.clone.1 | convolution fusion | flops 422051840 | bytes 9642244 | tf_op jit(solution)/shard_map/while/body/eval_jaxpr/bnpq,bnqs->bps/dot_general | solution.py:89
  729.0 15.5 %fusion.499 = f32[16,8,128,128]{3,2,1,0:T(8,128)} fusion(f32[16,8,128,16]{2,3,1,0:T(8,128)S(1)} %bitcast.461, f32[16,128,16]{1,2,0:T(8,128)S(1)} %get-tuple-element.493, pred[16,8]{1,0:T(8,128)(4,1)S(1)} %copy.450), kind=kOutput, calls=%fused_computation.49.clone.1 | convolution fusion | flops 402915328 | bytes 9568384 | tf_op jit(solution)/shard_map/while/body/eval_jaxpr/...ad,...bd->...ab/dot_general | solution.py:39
  745.8 15.2 %fusion.500 = f32[2,16,128,16]{2,3,1,0:T(8,128)} fusion(f32[2,16,128,16]{2,3,1,0:T(8,128)} %get-tuple-element.504, s32[]{:T(128)S(6)} %copy.456, f32[16,8,128,128]{3,2,1,0:T(8,128)} %fusion.499, f32[16,8,128]{2,1,0:T(8,128)S(1)} %multiply_reduce_fusion.30, f32[16,128]{1,0:T(8,128)S(1)} %get-tuple-element.494, f32[16,8,128,16]{2,3,1,0:T(8,128)S(1)} %bitcast.463, ...), kind=kOutput, calls=%fused_computation.46.clone.1 | convolution fusion | flops 422051840 | bytes 9642244 | tf_op jit(solution)/shard_map/while/body/eval_jaxpr/bnpq,bnqs->bps/dot_general | solution.py:89
  (732 shorter events, 433.8 us)
Async XLA Ops:
  1.6 543.3 %collective-permute-start.14 = (f32[4,64,16]{2,1,0:T(8,128)}, f32[4,64,16]{2,1,0:T(8,128)}, u32[]{:S(2)}, u32[]{:S(2)}) collective-permute-start(f32[4,64,16]{2,1,0:T(8,128)} %broadcast_in_dim.633), channel_id=1, source_target_pairs={{0,2},{1,3},{2,4},{3,5},{4,6},{5,7},{6,8},{7,9},{8,10},{9,11},{10,... | collective-permute-start | bytes 49160 | tf_op jit(solution)/shard_map/ppermute | solution.py:22
  5.0 543.9 %collective-permute-start.15 = (f32[4,64,16]{2,1,0:T(8,128)}, f32[4,64,16]{2,1,0:T(8,128)}, u32[]{:S(2)}, u32[]{:S(2)}) collective-permute-start(f32[4,64,16]{2,1,0:T(8,128)} %broadcast_in_dim.633), channel_id=1, source_target_pairs={{0,1},{1,2},{2,3},{3,4},{4,5},{5,6},{6,7},{7,8},{8,9},{9,10},{10,1... | collective-permute-start | bytes 49160 | tf_op jit(solution)/shard_map/ppermute | solution.py:22
  6.9 545.1 %collective-permute-start.16 = (f32[4,64,16]{2,1,0:T(8,128)}, f32[4,64,16]{2,1,0:T(8,128)}, u32[]{:S(2)}, u32[]{:S(2)}) collective-permute-start(f32[4,64,16]{2,1,0:T(8,128)} %broadcast_in_dim.633), channel_id=1, source_target_pairs={{1,0},{2,1},{3,2},{4,3},{5,4},{6,5},{7,6},{8,7},{9,8},{10,9},{11,1... | collective-permute-start | bytes 49160 | tf_op jit(solution)/shard_map/ppermute | solution.py:22
  14.8 540.5 %collective-permute-start.17 = (f32[4,64,16]{2,1,0:T(8,128)}, f32[4,64,16]{2,1,0:T(8,128)}, u32[]{:S(2)}, u32[]{:S(2)}) collective-permute-start(f32[4,64,16]{2,1,0:T(8,128)} %broadcast_in_dim.633), channel_id=1, source_target_pairs={{2,0},{3,1},{4,2},{5,3},{6,4},{7,5},{8,6},{9,7},{10,8},{11,9},{12,... | collective-permute-start | bytes 49160 | tf_op jit(solution)/shard_map/ppermute | solution.py:22
  31.5 188.5 %collective-permute-start.46 = (f32[1,64,16]{1,2,0:T(8,128)}, f32[1,64,16]{1,2,0:T(8,128)}, u32[]{:S(2)}, u32[]{:S(2)}) collective-permute-start(f32[1,64,16]{1,2,0:T(8,128)} %slice_add_fusion.11), channel_id=1, source_target_pairs={{0,6},{1,7},{2,8},{3,9},{4,10},{5,11},{6,12},{7,13},{8,14},{9,15},... | collective-permute-start | bytes 12296 | tf_op jit(solution)/shard_map/ppermute | solution.py:22
  228.2 10.3 %collective-permute-start.48 = (f32[1,64,16]{1,2,0:T(8,128)}, f32[1,64,16]{1,2,0:T(8,128)S(1)}, u32[]{:S(2)}, u32[]{:S(2)}) collective-permute-start(f32[1,64,16]{1,2,0:T(8,128)} %slice_add_fusion.11), channel_id=1, source_target_pairs={{0,4},{1,5},{2,6},{3,7},{4,8},{5,9},{6,10},{7,11},{8,12},{9,13},{1... | collective-permute-start | bytes 12296 | tf_op jit(solution)/shard_map/ppermute | solution.py:22
  238.4 9.7 %collective-permute-start.49 = (f32[1,64,16]{1,2,0:T(8,128)}, f32[1,64,16]{1,2,0:T(8,128)S(1)}, u32[]{:S(2)}, u32[]{:S(2)}) collective-permute-start(f32[1,64,16]{1,2,0:T(8,128)} %slice_add_fusion.11), channel_id=1, source_target_pairs={{0,3},{1,4},{2,5},{3,6},{4,7},{5,8},{6,9},{7,10},{8,11},{9,12},{10... | collective-permute-start | bytes 12296 | tf_op jit(solution)/shard_map/ppermute | solution.py:22
  248.1 10.0 %collective-permute-start.50 = (f32[1,64,16]{1,2,0:T(8,128)}, f32[1,64,16]{1,2,0:T(8,128)S(1)}, u32[]{:S(2)}, u32[]{:S(2)}) collective-permute-start(f32[1,64,16]{1,2,0:T(8,128)} %slice_add_fusion.11), channel_id=1, source_target_pairs={{0,2},{1,3},{2,4},{3,5},{4,6},{5,7},{6,8},{7,9},{8,10},{9,11},{10,... | collective-permute-start | bytes 12296 | tf_op jit(solution)/shard_map/ppermute | solution.py:22
  284.0 10.0 %collective-permute-start.36 = (f32[1,64,16]{1,2,0:T(8,128)S(1)}, f32[1,64,16]{1,2,0:T(8,128)S(1)}, u32[]{:S(2)}, u32[]{:S(2)}) collective-permute-start(f32[1,64,16]{1,2,0:T(8,128)S(1)} %copy.346), channel_id=1, source_target_pairs={{0,4},{1,5},{2,6},{3,7},{4,8},{5,9},{6,10},{7,11},{8,12},{9,13},{1... | collective-permute-start | bytes 12296 | tf_op jit(solution)/shard_map/ppermute | solution.py:22
  303.5 9.8 %collective-permute-start.38 = (f32[1,64,16]{1,2,0:T(8,128)S(1)}, f32[1,64,16]{1,2,0:T(8,128)S(1)}, u32[]{:S(2)}, u32[]{:S(2)}) collective-permute-start(f32[1,64,16]{1,2,0:T(8,128)S(1)} %copy.346), channel_id=1, source_target_pairs={{0,2},{1,3},{2,4},{3,5},{4,6},{5,7},{6,8},{7,9},{8,10},{9,11},{10,... | collective-permute-start | bytes 12296 | tf_op jit(solution)/shard_map/ppermute | solution.py:22
  365.9 11.5 %collective-permute-start.52 = (f32[1,64,16]{1,2,0:T(8,128)}, f32[1,64,16]{1,2,0:T(8,128)S(1)}, u32[]{:S(2)}, u32[]{:S(2)}) collective-permute-start(f32[1,64,16]{1,2,0:T(8,128)} %slice_add_fusion.11), channel_id=1, source_target_pairs={{1,0},{2,1},{3,2},{4,3},{5,4},{6,5},{7,6},{8,7},{9,8},{10,9},{11,1... | collective-permute-start | bytes 12296 | tf_op jit(solution)/shard_map/ppermute | solution.py:22
  409.0 9.7 %collective-permute-start.57 = (f32[1,64,16]{1,2,0:T(8,128)}, f32[1,64,16]{1,2,0:T(8,128)S(1)}, u32[]{:S(2)}, u32[]{:S(2)}) collective-permute-start(f32[1,64,16]{1,2,0:T(8,128)} %slice_add_fusion.11), channel_id=1, source_target_pairs={{6,0},{7,1},{8,2},{9,3},{10,4},{11,5},{12,6},{13,7},{14,8},{15,9},... | collective-permute-start | bytes 12296 | tf_op jit(solution)/shard_map/ppermute | solution.py:22
  428.3 9.8 %collective-permute-start.29 = (f32[2,64,16]{1,2,0:T(8,128)S(1)}, f32[2,64,16]{1,2,0:T(8,128)S(1)}, u32[]{:S(2)}, u32[]{:S(2)}) collective-permute-start(f32[2,64,16]{1,2,0:T(8,128)S(1)} %copy-done.60), channel_id=1, source_target_pairs={{0,2},{1,3},{2,4},{3,5},{4,6},{5,7},{6,8},{7,9},{8,10},{9,11},{10,... | collective-permute-start | bytes 24584 | tf_op jit(solution)/shard_map/ppermute | solution.py:22
  447.4 10.1 %collective-permute-start.22 = (f32[2,64,16]{2,1,0:T(8,128)S(1)}, f32[2,64,16]{2,1,0:T(8,128)S(1)}, u32[]{:S(2)}, u32[]{:S(2)}) collective-permute-start(f32[2,64,16]{2,1,0:T(8,128)S(1)} %copy-done.32), channel_id=1, source_target_pairs={{0,3},{1,4},{2,5},{3,6},{4,7},{5,8},{6,9},{7,10},{8,11},{9,12},{10... | collective-permute-start | bytes 24584 | tf_op jit(solution)/shard_map/ppermute | solution.py:22
  457.4 10.4 %collective-permute-start.23 = (f32[2,64,16]{2,1,0:T(8,128)S(1)}, f32[2,64,16]{2,1,0:T(8,128)S(1)}, u32[]{:S(2)}, u32[]{:S(2)}) collective-permute-start(f32[2,64,16]{2,1,0:T(8,128)S(1)} %copy-done.32), channel_id=1, source_target_pairs={{0,2},{1,3},{2,4},{3,5},{4,6},{5,7},{6,8},{7,9},{8,10},{9,11},{10,... | collective-permute-start | bytes 24584 | tf_op jit(solution)/shard_map/ppermute | solution.py:22
  467.8 9.8 %collective-permute-start.24 = (f32[2,64,16]{2,1,0:T(8,128)S(1)}, f32[2,64,16]{2,1,0:T(8,128)S(1)}, u32[]{:S(2)}, u32[]{:S(2)}) collective-permute-start(f32[2,64,16]{2,1,0:T(8,128)S(1)} %copy-done.32), channel_id=1, source_target_pairs={{0,1},{1,2},{2,3},{3,4},{4,5},{5,6},{6,7},{7,8},{8,9},{9,10},{10,1... | collective-permute-start | bytes 24584 | tf_op jit(solution)/shard_map/ppermute | solution.py:22
  495.9 14.1 %collective-permute-start.31 = (f32[2,64,16]{1,2,0:T(8,128)S(1)}, f32[2,64,16]{1,2,0:T(8,128)S(1)}, u32[]{:S(2)}, u32[]{:S(2)}) collective-permute-start(f32[2,64,16]{1,2,0:T(8,128)S(1)} %copy-done.60), channel_id=1, source_target_pairs={{1,0},{2,1},{3,2},{4,3},{5,4},{6,5},{7,6},{8,7},{9,8},{10,9},{11,1... | collective-permute-start | bytes 24584 | tf_op jit(solution)/shard_map/ppermute | solution.py:22
  523.5 10.0 %collective-permute-start.18 = (f32[4,64,16]{1,2,0:T(8,128)S(1)}, f32[4,64,16]{1,2,0:T(8,128)S(1)}, u32[]{:S(2)}, u32[]{:S(2)}) collective-permute-start(f32[4,64,16]{1,2,0:T(8,128)S(1)} %copy-done.58), channel_id=1, source_target_pairs={{0,2},{1,3},{2,4},{3,5},{4,6},{5,7},{6,8},{7,9},{8,10},{9,11},{10,... | collective-permute-start | bytes 49160 | tf_op jit(solution)/shard_map/ppermute | solution.py:22
  543.0 21.0 %collective-permute-start.20 = (f32[4,64,16]{1,2,0:T(8,128)S(1)}, f32[4,64,16]{1,2,0:T(8,128)S(1)}, u32[]{:S(2)}, u32[]{:S(2)}) collective-permute-start(f32[4,64,16]{1,2,0:T(8,128)S(1)} %copy-done.58), channel_id=1, source_target_pairs={{1,0},{2,1},{3,2},{4,3},{5,4},{6,5},{7,6},{8,7},{9,8},{10,9},{11,1... | collective-permute-start | bytes 49160 | tf_op jit(solution)/shard_map/ppermute | solution.py:22
  544.9 21.6 %collective-permute-start.21 = (f32[4,64,16]{1,2,0:T(8,128)S(1)}, f32[4,64,16]{1,2,0:T(8,128)S(1)}, u32[]{:S(2)}, u32[]{:S(2)}) collective-permute-start(f32[4,64,16]{1,2,0:T(8,128)S(1)} %copy-done.58), channel_id=1, source_target_pairs={{2,0},{3,1},{4,2},{5,3},{6,4},{7,5},{8,6},{9,7},{10,8},{11,9},{12,... | collective-permute-start | bytes 49160 | tf_op jit(solution)/shard_map/ppermute | solution.py:22
  549.0 139.9 %collective-permute-start.1 = (f32[32,2048]{1,0:T(8,128)}, f32[32,2048]{1,0:T(8,128)}, u32[]{:S(2)}, u32[]{:S(2)}) collective-permute-start(f32[32,2048]{1,0:T(8,128)} %get-tuple-element.417), channel_id=1, source_target_pairs={{1,0},{2,1},{3,2},{4,3},{5,4},{6,5},{7,6},{8,7},{9,8},{10,9},{11,1... | collective-permute-start | bytes 786440 | tf_op jit(solution)/shard_map/ppermute | solution.py:33
  552.0 136.8 %collective-permute-start = (f32[32,2048]{1,0:T(8,128)}, f32[32,2048]{1,0:T(8,128)}, u32[]{:S(2)}, u32[]{:S(2)}) collective-permute-start(f32[32,2048]{1,0:T(8,128)} %get-tuple-element.416), channel_id=1, source_target_pairs={{0,1},{1,2},{2,3},{3,4},{4,5},{5,6},{6,7},{7,8},{8,9},{9,10},{10,1... | collective-permute-start | bytes 786440 | tf_op jit(solution)/shard_map/ppermute | solution.py:30
  555.3 84.9 %collective-permute-start.5 = (f32[6,64,16]{1,2,0:T(8,128)}, f32[6,64,16]{1,2,0:T(8,128)}, u32[]{:S(2)}, u32[]{:S(2)}) collective-permute-start(f32[6,64,16]{1,2,0:T(8,128)} %get-tuple-element.427), channel_id=1, source_target_pairs={{1,0},{2,1},{3,2},{4,3},{5,4},{6,5},{7,6},{8,7},{9,8},{10,9},{11,1... | collective-permute-start | bytes 73736 | tf_op jit(solution)/shard_map/ppermute | solution.py:22
  566.5 14.1 %collective-permute-start.2 = (f32[6,64,16]{1,2,0:T(8,128)S(1)}, f32[6,64,16]{1,2,0:T(8,128)S(1)}, u32[]{:S(2)}, u32[]{:S(2)}) collective-permute-start(f32[6,64,16]{1,2,0:T(8,128)S(1)} %copy.289), channel_id=1, source_target_pairs={{0,1},{1,2},{2,3},{3,4},{4,5},{5,6},{6,7},{7,8},{8,9},{9,10},{10,1... | collective-permute-start | bytes 73736 | tf_op jit(solution)/shard_map/ppermute | solution.py:22
  573.2 28.6 %collective-permute-start.7 = (f32[6,64,16]{2,1,0:T(8,128)}, f32[6,64,16]{2,1,0:T(8,128)}, u32[]{:S(2)}, u32[]{:S(2)}) collective-permute-start(f32[6,64,16]{2,1,0:T(8,128)} %slice.339), channel_id=1, source_target_pairs={{1,0},{2,1},{3,2},{4,3},{5,4},{6,5},{7,6},{8,7},{9,8},{10,9},{11,1... | collective-permute-start | bytes 73736 | tf_op jit(solution)/shard_map/ppermute | solution.py:22
  580.6 30.1 %collective-permute-start.6 = (f32[6,64,16]{2,1,0:T(8,128)}, f32[6,64,16]{2,1,0:T(8,128)}, u32[]{:S(2)}, u32[]{:S(2)}) collective-permute-start(f32[6,64,16]{2,1,0:T(8,128)} %slice.337), channel_id=1, source_target_pairs={{0,1},{1,2},{2,3},{3,4},{4,5},{5,6},{6,7},{7,8},{8,9},{9,10},{10,1... | collective-permute-start | bytes 73736 | tf_op jit(solution)/shard_map/ppermute | solution.py:22
  601.9 21.9 %collective-permute-start.11 = (f32[6,64,16]{2,1,0:T(8,128)}, f32[6,64,16]{2,1,0:T(8,128)S(1)}, u32[]{:S(2)}, u32[]{:S(2)}) collective-permute-start(f32[6,64,16]{2,1,0:T(8,128)} %slice.351), channel_id=1, source_target_pairs={{1,0},{2,1},{3,2},{4,3},{5,4},{6,5},{7,6},{8,7},{9,8},{10,9},{11,1... | collective-permute-start | bytes 73736 | tf_op jit(solution)/shard_map/ppermute | solution.py:22
  610.7 15.2 %collective-permute-start.10 = (f32[6,64,16]{2,1,0:T(8,128)}, f32[6,64,16]{2,1,0:T(8,128)S(1)}, u32[]{:S(2)}, u32[]{:S(2)}) collective-permute-start(f32[6,64,16]{2,1,0:T(8,128)} %slice.349), channel_id=1, source_target_pairs={{0,1},{1,2},{2,3},{3,4},{4,5},{5,6},{6,7},{7,8},{8,9},{9,10},{10,1... | collective-permute-start | bytes 73736 | tf_op jit(solution)/shard_map/ppermute | solution.py:22
  623.8 18.4 %collective-permute-start.4 = (f32[6,64,16]{1,2,0:T(8,128)S(1)}, f32[6,64,16]{1,2,0:T(8,128)S(1)}, u32[]{:S(2)}, u32[]{:S(2)}) collective-permute-start(f32[6,64,16]{1,2,0:T(8,128)S(1)} %copy-done.65), channel_id=1, source_target_pairs={{0,1},{1,2},{2,3},{3,4},{4,5},{5,6},{6,7},{7,8},{8,9},{9,10},{10,1... | collective-permute-start | bytes 73736 | tf_op jit(solution)/shard_map/ppermute | solution.py:22
  625.9 25.0 %collective-permute-start.9 = (f32[6,64,16]{1,2,0:T(8,128)S(1)}, f32[6,64,16]{1,2,0:T(8,128)S(1)}, u32[]{:S(2)}, u32[]{:S(2)}) collective-permute-start(f32[6,64,16]{1,2,0:T(8,128)S(1)} %copy-done.64), channel_id=1, source_target_pairs={{1,0},{2,1},{3,2},{4,3},{5,4},{6,5},{7,6},{8,7},{9,8},{10,9},{11,1... | collective-permute-start | bytes 73736 | tf_op jit(solution)/shard_map/ppermute | solution.py:22
  640.2 13.1 %collective-permute-start.8 = (f32[6,64,16]{1,2,0:T(8,128)S(1)}, f32[6,64,16]{1,2,0:T(8,128)S(1)}, u32[]{:S(2)}, u32[]{:S(2)}) collective-permute-start(f32[6,64,16]{1,2,0:T(8,128)S(1)} %copy-done.63), channel_id=1, source_target_pairs={{0,1},{1,2},{2,3},{3,4},{4,5},{5,6},{6,7},{7,8},{8,9},{9,10},{10,1... | collective-permute-start | bytes 73736 | tf_op jit(solution)/shard_map/ppermute | solution.py:22
  642.2 14.3 %collective-permute-start.13 = (f32[6,64,16]{1,2,0:T(8,128)S(1)}, f32[6,64,16]{1,2,0:T(8,128)S(1)}, u32[]{:S(2)}, u32[]{:S(2)}) collective-permute-start(f32[6,64,16]{1,2,0:T(8,128)S(1)} %copy-done.62), channel_id=1, source_target_pairs={{1,0},{2,1},{3,2},{4,3},{5,4},{6,5},{7,6},{8,7},{9,8},{10,9},{11,1... | collective-permute-start | bytes 73736 | tf_op jit(solution)/shard_map/ppermute | solution.py:22
  (169 other events, 5086.8 us)
where the time goes:
time: 773 us; the launch traced here: 764 us
  starting transfers between devices  239 us (31%)
  waiting for transfers between devices  161 us (21%)
  matrix products  156 us (20%)
  local copies, waits for them, and re-layouts  114 us (15%)
  other arithmetic  49.6 us (6%)
  blocking collectives  40.6 us (5%)
    ppermute x56, starting transfers between devices, from_behind(): return lax.ppermute(value, axis, pairs)  235 us
    ppermute x56, waiting for transfers between devices, from_behind(): return lax.ppermute(value, axis, pairs)  161 us
    dot_general x15, matrix products, matern_block(): jnp.einsum('...ad,...bd->...ab', row_points, column_points, precision=hig...  70.7 us
    all_gather x1, blocking collectives, on_device(): level_moments = lax.all_gather(root_moments, 'leaf', axis=0, tiled=True)  40.6 us
    dot_general x2, matrix products, near_one_block(): jnp.einsum('bnpq,bnqs->bps', kernel, partner_charges, precision=highest)  30.3 us
    dot_general x13, matrix products, far_one_block(): jnp.einsum('cnab,cnbs->cas', kernel, partner_moments, precision=highest)  27.7 us
    reduce_sum x15, other arithmetic, matern_block(): row_norms = jnp.sum(row_points * row_points, axis=-1)[..., :, None]  17.9 us
    dot_general x12, matrix products, upward(): lifted = jnp.einsum('cab,cas->cbs', transfer, moments, precision=highest)  16.6 us
  transfers between devices with their start and end apart: 58, of which 38 were waited for; matrix products, arithmetic and copies ran while one was open for 32% of the time, Pallas kernels for 0%

commit v1 on v0

v1 whole, which is shorter than its diff:
```python
import math

import jax
import jax.numpy as jnp
import numpy as np
from jax import lax
from jax.experimental import pallas as pl
from jax.experimental.pallas import tpu as pltpu
from jax.sharding import PartitionSpec as P

DIM = 16
RHS = 16
LEAF = 128
RANK = 64
LEAVES_DEV = 32
NREACH = 16
REACH = 6
DEVICES = 128
TOP = 7
SHARED = 6
SLOTS = 4

bf16 = jnp.bfloat16
f32 = jnp.float32
SCALE = math.log2(math.e) / math.sqrt(3.0)
LN2 = math.log(2.0)
TINY = 1e-30

COLUMN = [0, 2048, 3072, 3584, 3840, 3968]
ROW = [0, 32, 48, 56, 60]
RIM = [0, 384, 768, 1152, 1408, 1536]
RIM_WIDTH = 1664
LOW_PIECES = [(0, 384), (2048, 2432), (3072, 3456), (3584, 4096)]
HIGH_PIECES = [(1664, 2048), (2688, 3072), (3200, 4096)]
VMEM = pl.BlockSpec(memory_space=pltpu.VMEM)
SMEM = pl.BlockSpec(memory_space=pltpu.SMEM)


def relevant(first, second, level):
    return 2 <= abs((first >> level) - (second >> level)) <= REACH


def slot_tables():
    sent = np.full((DEVICES, DEVICES, SLOTS), TOP, np.int32)
    held = np.zeros((DEVICES, SHARED, DEVICES), np.int32)
    for first in range(DEVICES):
        for second in range(DEVICES):
            levels = [level for level in range(SHARED) if relevant(first, second, level)]
            for slot, level in enumerate(levels):
                sent[first, second, slot] = level
                held[first, level, second] = slot
            sent[first, second, SLOTS - 1] = SHARED
    return np.concatenate([sent.reshape(DEVICES, -1), held.reshape(DEVICES, -1)], axis=1)


SENT = DEVICES * SLOTS


def split(x):
    high = x.astype(bf16)
    return high, (x - high.astype(f32)).astype(bf16)


def lanes(*parts):
    return jnp.concatenate(parts, axis=1)


def rows(*parts):
    return jnp.concatenate(parts, axis=0)


def dot(a, b):
    return jnp.dot(a, b, preferred_element_type=f32)


def dot_nt(a, b):
    return lax.dot_general(a, b, (((1,), (1,)), ((), ())), preferred_element_type=f32)


def narrow(x):
    high, low = split(x)
    return rows(lanes(high, high), lanes(low, low))


def folded(x):
    return x[:16] + x[16:]


def sides(x):
    x = x * SCALE
    high = x.astype(bf16).astype(f32)
    low = (x - high).astype(bf16).astype(f32)
    norm = jnp.sum(high * (high + 2.0 * low), axis=0, keepdims=True)
    norm_high = norm.astype(bf16).astype(f32)
    norm_middle = (norm - norm_high).astype(bf16).astype(f32)
    norm_low = norm - norm_high - norm_middle
    row = lax.broadcasted_iota(jnp.int32, x.shape, 0)
    parts = jnp.where(row % 3 == 0, norm_high, jnp.where(row % 3 == 1, norm_middle, norm_low))
    return high, low, parts, row


def source_side(x):
    high, low, parts, row = sides(x)
    tail = jnp.where(row < 3, 1.0, jnp.where(row < 6, parts, 0.0))
    return rows(high, high, low, tail)


def target_sides(x):
    high, low, parts, row = sides(x)
    tail = jnp.where(row < 3, parts, jnp.where(row < 6, 1.0, 0.0))
    factors = rows(-2.0 * high, -2.0 * low, -2.0 * high, tail)
    first = rows(factors, jnp.zeros_like(factors)).T
    return first.astype(bf16), pltpu.roll(first, RANK, 1).astype(bf16)


def matern(squared):
    squared = jnp.maximum(squared, TINY)
    distance = squared * lax.rsqrt(squared)
    return (1.0 + LN2 * distance) * jnp.exp2(-distance)


def pick(parts):
    lane = lax.broadcasted_iota(jnp.int32, parts[0].shape, 1)
    result = parts[3]
    for j in (2, 1, 0):
        result = jnp.where(lane < 32 * (j + 1), parts[j], result)
    return result


def interact(targets, sources, weights):
    kernel = matern(dot(targets, sources))
    high, low = split(kernel)
    size = kernel.shape[0]
    result = dot(rows(high, low), weights)
    quarter = size // 4
    return pick(
        [
            result[quarter * j : quarter * (j + 1)]
            + result[size + quarter * j : size + quarter * (j + 1)]
            for j in range(4)
        ]
    )


def weight_turns(slabs):
    parts = []
    for slab in slabs:
        high = slab.astype(bf16).astype(f32)
        parts += [high, slab - high]
    columns = rows(*parts).T
    return [
        (columns if turn == 0 else pltpu.roll(columns, 32 * turn, 1)).astype(bf16)
        for turn in range(4)
    ]


def halves(first, second):
    lane = lax.broadcasted_iota(jnp.int32, first.shape, 1)
    return jnp.where(lane < RANK, first, second)


def moments_kernel(
    tables, basis, charges, transfer, path, moments, low_rim, high_rim, outgoing, blocks
):
    def two_leaves(q, carry):
        parts = []
        for leaf in range(2):
            columns = pl.ds(pl.multiple_of(q * 256 + leaf * 128, 128), 128)
            high, low = split(basis[:, columns])
            parts.append(folded(dot_nt(narrow(charges[:, columns]), lanes(high, low))))
        moments[:, pl.ds(pl.multiple_of(q * 128, 128), 128)] = lanes(*parts)
        return carry

    lax.fori_loop(0, LEAVES_DEV // 2, two_leaves, 0, unroll=8)

    def lifted(slab, matrices):
        high, low = split(matrices)
        return folded(dot(narrow(slab), rows(high, low)))

    for height in range(5):
        number = LEAVES_DEV >> height
        parents = []
        for q in range(number // 2):
            start = (ROW[height] + 2 * q) * RANK
            slab = moments[:, COLUMN[height] + 128 * q : COLUMN[height] + 128 * (q + 1)]
            parents.append(lifted(slab, transfer[start : start + 128, :]))
        if height == 4:
            parents.append(jnp.zeros((16, RANK), f32))
        for q in range(len(parents) // 2):
            start = COLUMN[height + 1] + 128 * q
            moments[:, start : start + 128] = lanes(parents[2 * q], parents[2 * q + 1])

    for rim, pieces in ((low_rim, LOW_PIECES), (high_rim, HIGH_PIECES)):
        start = 0
        for first, last in pieces:
            rim[:, start : start + last - first] = moments[:, first:last]
            start += last - first

    value = moments[:, COLUMN[5] : COLUMN[5] + RANK]
    for level in range(SHARED + 1):
        blocks[level] = lanes(value[:8], value[8:])
        if level < SHARED:
            value = lifted(value, path[RANK * level : RANK * (level + 1), :])
    blocks[TOP] = jnp.zeros((8, 128), f32)

    def one_device(other, carry):
        for slot in range(SLOTS - 1):
            outgoing[other, 8 * slot : 8 * (slot + 1), :] = blocks[tables[other * SLOTS + slot]]
        outgoing[other, 8 * (SLOTS - 1) : 8 * SLOTS, :] = blocks[SHARED]
        return carry

    lax.fori_loop(0, DEVICES, one_device, 0, unroll=8)


def moments_call(tables, basis, charges, transfer, path):
    shape = jax.ShapeDtypeStruct
    return pl.pallas_call(
        moments_kernel,
        out_shape=(
            shape((16, 4096), f32),
            shape((16, RIM_WIDTH), f32),
            shape((16, RIM_WIDTH), f32),
            shape((DEVICES, 8 * SLOTS, 128), f32),
        ),
        in_specs=[SMEM, VMEM, VMEM, VMEM, VMEM],
        out_specs=(VMEM, VMEM, VMEM, VMEM),
        scratch_shapes=[pltpu.VMEM((8, 8, 128), f32)],
        compiler_params=pltpu.CompilerParams(vmem_limit_bytes=48 * 2**20),
        cost_estimate=pl.CostEstimate(flops=10**9, bytes_accessed=2**22, transcendentals=0),
        name="moments",
    )(tables, basis, charges, transfer, path)


def near_kernel(device, near_blocks, points, charges, low, high, out, factors, weights):
    def prepare(point_ref, charge_ref, charge_row, first):
        def four_leaves(i, carry):
            columns = pl.ds(pl.multiple_of(i * 512, 512), 512)
            side = source_side(point_ref[:DIM, columns]).astype(bf16)
            charge = charge_ref[charge_row : charge_row + RHS, columns]
            slabs = []
            for m in range(4):
                factors[(first + i) * 4 + m] = side[:, 128 * m : 128 * (m + 1)]
                slabs.append(charge[:, 128 * m : 128 * (m + 1)])
            for turn, value in enumerate(weight_turns(slabs)):
                weights[turn, first + i] = value
            return carry

        return four_leaves

    lax.fori_loop(0, 4, prepare(low, low, DIM, 0), 0, unroll=2)
    lax.fori_loop(0, 8, prepare(points, charges, 0, 4), 0, unroll=2)
    lax.fori_loop(0, 4, prepare(high, high, DIM, 12), 0, unroll=2)
    factors[64] = jnp.zeros((64, 128), bf16)
    for turn in range(4):
        weights[turn, 16] = jnp.zeros((128, 128), bf16)
    first_leaf = device[0] * LEAVES_DEV - NREACH

    def one_leaf(t, carry):
        columns = pl.ds(pl.multiple_of(t * 128, 128), 128)
        front, back = target_sides(points[:, columns])
        empty = jnp.zeros_like(front)
        targets = rows(
            lanes(front, empty), lanes(back, empty), lanes(empty, front), lanes(empty, back)
        )
        located = []
        for j in range(8):
            block = near_blocks[t, j]
            inside = jnp.minimum(jnp.maximum(block - first_leaf, 0), 63)
            located.append(jnp.where(block < 0, 64, inside))
        sources = rows(
            *[lanes(factors[located[2 * j]], factors[located[2 * j + 1]]) for j in range(4)]
        )
        weight = rows(
            *[
                pick([weights[(j - located[2 * j + h]) & 3, located[2 * j + h] >> 2] for j in range(4)])
                for h in range(2)
            ]
        )
        total = interact(targets, sources, weight).T
        out[:, columns] = sum(total[16 * g : 16 * (g + 1)] for g in range(8))
        return carry

    lax.fori_loop(0, LEAVES_DEV, one_leaf, 0, unroll=8)


def near_call(device, near_blocks, points, charges, low, high):
    return pl.pallas_call(
        near_kernel,
        out_shape=jax.ShapeDtypeStruct((RHS, LEAVES_DEV * LEAF), f32),
        in_specs=[SMEM, SMEM, VMEM, VMEM, VMEM, VMEM],
        out_specs=VMEM,
        scratch_shapes=[
            pltpu.VMEM((65, 64, 128), bf16),
            pltpu.VMEM((4, 17, 128, 128), bf16),
        ],
        compiler_params=pltpu.CompilerParams(vmem_limit_bytes=48 * 2**20),
        cost_estimate=pl.CostEstimate(flops=10**10, bytes_accessed=2**22, transcendentals=0),
        name="near",
    )(device, near_blocks, points, charges, low, high)


def prepare_factors(anchors, factors, groups):
    def four_slabs(i, carry):
        side = source_side(anchors[:, pl.ds(pl.multiple_of(i * 512, 512), 512)])
        for m in range(4):
            slab = side[:, 128 * m : 128 * (m + 1)]
            turned = pltpu.roll(slab, RANK, 1)
            factors[(i * 4 + m) * 2] = halves(slab, turned).astype(bf16)
            factors[(i * 4 + m) * 2 + 1] = halves(turned, slab).astype(bf16)
        return carry

    lax.fori_loop(0, groups, four_slabs, 0, unroll=2)


def prepare_weights(moments, weights, groups):
    def four_slabs(i, carry):
        value = moments[:, pl.ds(pl.multiple_of(i * 512, 512), 512)]
        turns = weight_turns([value[:, 128 * m : 128 * (m + 1)] for m in range(4)])
        for turn in range(4):
            weights[turn, i, 0] = turns[turn][:RANK]
            weights[turn, i, 1] = turns[turn][RANK:]
        return carry

    lax.fori_loop(0, groups, four_slabs, 0, unroll=2)


def two_targets(anchors):
    front, back = target_sides(anchors)
    empty = jnp.zeros((RANK, 128), bf16)
    return rows(
        lanes(front[:RANK], empty),
        lanes(back[:RANK], empty),
        lanes(empty, front[RANK:]),
        lanes(empty, back[RANK:]),
    )


def four_sources(factors, located):
    return lanes(
        halves(factors[located[0]], factors[located[1]]),
        halves(factors[located[2]], factors[located[3]]),
    )


def placed(weights, index, slot):
    pair = index >> 1
    return weights[(slot - pair) & 3, pair >> 2, index & 1]


def two_clusters(anchors, factors, weights, located):
    sources = rows(*[four_sources(factors, located[4 * slot : 4 * slot + 4]) for slot in range(4)])
    weight = rows(
        *[pick([placed(weights, located[4 * slot + m], slot) for slot in range(4)]) for m in range(4)]
    )
    return cluster_sums(interact(two_targets(anchors), sources, weight))


def cluster_sums(total):
    total = total.T
    return lanes(
        total[:16] + total[16:32] + total[32:48] + total[48:64],
        total[64:80] + total[80:96] + total[96:112] + total[112:],
    )


def locate(entry, first, last, base, empty):
    inside = jnp.minimum(jnp.maximum(entry - first, 0), last)
    return jnp.where(entry < 0, empty, base + inside)


FINE_BASE = [0, 44, 72]
FINE_EMPTY = 92


def fine_kernel(
    device,
    lists,
    anchors,
    moments,
    low_anchors,
    high_anchors,
    low_moments,
    high_moments,
    far,
    held_anchors,
    held_moments,
    factors,
    weights,
):
    start = 0
    for height in range(3):
        width = (LEAVES_DEV >> height) * RANK
        rim = slice(RIM[height], RIM[height] + REACH * RANK)
        own = slice(COLUMN[height], COLUMN[height] + width)
        for held, parts in (
            (
                held_anchors,
                (low_anchors[2 * DIM : 3 * DIM, rim], anchors[:, own], high_anchors[2 * DIM : 3 * DIM, rim]),
            ),
            (held_moments, (low_moments[:, rim], moments[:, own], high_moments[:, rim])),
        ):
            at = start
            for part in parts:
                held[:, at : at + part.shape[1]] = part
                at += part.shape[1]
        start = at
    held_anchors[:, start:] = jnp.zeros((DIM, 48 * 128 - start), f32)
    held_moments[:, start:] = jnp.zeros((DIM, 48 * 128 - start), f32)
    prepare_factors(held_anchors, factors, 12)
    prepare_weights(held_moments, weights, 12)

    for height in range(3):
        number = LEAVES_DEV >> height

        def one_pair(q, carry, height=height, number=number):
            first = device[0] * number - REACH
            located = []
            for cluster in range(2):
                for j in range(8):
                    entry = lists[2 * LEAVES_DEV - 2 * number + 2 * q + cluster, j]
                    located.append(
                        locate(entry, first, number + 2 * REACH - 1, FINE_BASE[height], FINE_EMPTY)
                    )
            columns = pl.ds(pl.multiple_of(COLUMN[height] + q * 128, 128), 128)
            far[:, columns] = two_clusters(anchors[:, columns], factors, weights, located)
            return carry

        lax.fori_loop(0, number // 2, one_pair, 0, unroll=4)


def fine_call(device, lists, anchors, moments, low, high, low_moments, high_moments):
    return pl.pallas_call(
        fine_kernel,
        out_shape=jax.ShapeDtypeStruct((RHS, 56 * RANK), f32),
        in_specs=[SMEM, SMEM] + [VMEM] * 6,
        out_specs=VMEM,
        scratch_shapes=[
            pltpu.VMEM((DIM, 48 * 128), f32),
            pltpu.VMEM((RHS, 48 * 128), f32),
            pltpu.VMEM((96, 64, 128), bf16),
            pltpu.VMEM((4, 12, 2, 64, 128), bf16),
        ],
        compiler_params=pltpu.CompilerParams(vmem_limit_bytes=48 * 2**20),
        cost_estimate=pl.CostEstimate(flops=5 * 10**9, bytes_accessed=2**22, transcendentals=0),
        name="fine",
    )(device, lists, anchors, moments, low, high, low_moments, high_moments)


COARSE_EMPTY = 30


def coarse_kernel(
    device,
    tables,
    lists,
    top_lists,
    anchors,
    moments,
    low_anchors,
    high_anchors,
    low_moments,
    high_moments,
    low_second,
    high_second,
    low_third,
    high_third,
    incoming,
    top_anchors,
    path,
    transfer,
    basis,
    far,
    near,
    out,
    held_anchors,
    held_moments,
    factors,
    weights,
    expansion,
):
    me = device[0]
    a = slice(0, DIM)
    m = slice(DIM, 2 * DIM)
    e = slice(2 * DIM, 3 * DIM)

    def at(column):
        return slice(column, column + 128)

    slabs = [
        (low_second[a, at(0)], low_second[m, at(0)]),
        (low_anchors[e, at(1152)], low_moments[:, at(1152)]),
        (low_anchors[e, at(1280)], low_moments[:, at(1280)]),
        (anchors[:, at(3584)], moments[:, at(3584)]),
        (anchors[:, at(3712)], moments[:, at(3712)]),
        (high_anchors[e, at(1152)], high_moments[:, at(1152)]),
        (high_anchors[e, at(1280)], high_moments[:, at(1280)]),
        (high_second[a, at(0)], high_second[m, at(0)]),
        (low_third[a, at(0)], low_third[m, at(0)]),
        (low_second[a, at(128)], low_second[m, at(128)]),
        (low_anchors[e, at(1408)], low_moments[:, at(1408)]),
        (anchors[:, at(3840)], moments[:, at(3840)]),
        (high_anchors[e, at(1408)], high_moments[:, at(1408)]),
        (high_second[a, at(128)], high_second[m, at(128)]),
        (high_third[a, at(0)], high_third[m, at(0)]),
        (low_third[a, at(256)], None),
        (low_third[a, at(128)], None),
        (low_second[a, at(256)], None),
        (low_anchors[e, at(1536)], None),
        (anchors[:, at(3968)], None),
        (high_anchors[e, at(1536)], None),
        (high_second[a, at(256)], None),
        (high_third[a, at(128)], None),
        (high_third[a, at(256)], None),
    ]
    for index, (anchor_slab, moment_slab) in enumerate(slabs):
        held_anchors[:, at(128 * index)] = anchor_slab
        if moment_slab is not None:
            held_moments[:, at(128 * index)] = moment_slab
    held_moments[:, at(128 * 15)] = jnp.zeros((RHS, 128), f32)
    prepare_factors(held_anchors, factors, 6)
    prepare_weights(held_moments, weights, 4)

    def local_pair(height, q, base):
        number = LEAVES_DEV >> height
        located = []
        for cluster in range(2):
            for j in range(8):
                entry = lists[2 * LEAVES_DEV - 2 * number + 2 * q + cluster, j]
                located.append(
                    locate(entry, me * number - REACH, number + 2 * REACH - 1, base, COARSE_EMPTY)
                )
        return two_clusters(
            anchors[:, at(COLUMN[height] + 128 * q)], factors, weights, located
        )

    far_third = [local_pair(3, q, 0) for q in range(2)]
    far_fourth = local_pair(4, 0, 16)

    lane = lax.broadcasted_iota(jnp.int32, (8, 128), 1)

    def two_blocks(first, second):
        return rows(
            jnp.where(lane < RANK, first, pltpu.roll(second, RANK, 1)),
            jnp.where(lane < RANK, pltpu.roll(first, RANK, 1), second),
        )

    def lifted(slab, matrices):
        high, low = split(matrices)
        return folded(dot(narrow(slab), rows(high, low)))

    sixth = [
        jnp.sum(incoming[64 * c : 64 * (c + 1), 8 * (SLOTS - 1) : 8 * SLOTS, :], axis=0)
        for c in range(2)
    ]
    seventh = lifted(two_blocks(*sixth), path[RANK * 7 : RANK * 9, :])
    seventh = lanes(seventh[:8], seventh[8:])

    entries = [[lists[62, j] for j in range(8)]]
    for level in range(1, TOP + 1):
        row = DEVICES - (DEVICES >> (level - 1)) + (me >> level)
        entries.append([top_lists[row, j] for j in range(8)])

    def block(level, entry):
        if level == TOP:
            return jnp.where(entry == 0, seventh, 0.0)
        if level == SHARED:
            return jnp.where(entry == 0, sixth[0], jnp.where(entry == 1, sixth[1], 0.0))
        first = jnp.maximum(entry, 0) << level

        def add(i, total):
            slot = tables[SENT + level * DEVICES + first + i]
            return total + incoming[first + i, pl.ds(pl.multiple_of(slot * 8, 8), 8), :]

        count = jnp.where(entry < 0, 0, 1 << level)
        return lax.fori_loop(0, count, add, jnp.zeros((8, 128), f32))

    far_chain = []
    for unit in range(4):
        pairs = []
        for level in (2 * unit, 2 * unit + 1):
            held = [block(level, entry) for entry in entries[level]]
            pairs += [two_blocks(held[2 * j], held[2 * j + 1]) for j in range(4)]
        weight = []
        for h in range(2):
            parts = []
            for slot in range(4):
                high = pairs[2 * slot + h].astype(bf16).astype(f32)
                parts += [high, pairs[2 * slot + h] - high]
            weight.append(rows(*parts).T.astype(bf16))
        own = top_anchors[:, at(128 * unit)]
        sources = []
        for level in (2 * unit, 2 * unit + 1):
            for h in range(2):
                if level == 0:
                    located = []
                    for j in range(4):
                        shift = entries[0][4 * h + j] - me + REACH
                        shift = jnp.minimum(jnp.maximum(shift, 0), 2 * REACH)
                        place = shift + sum(
                            (shift >= edge).astype(jnp.int32) for edge in (1, 6, 7, 8)
                        )
                        located.append(30 + place)
                    sources.append(four_sources(factors, located))
                else:
                    start = 512 * level + 256 * h
                    sources.append(source_side(top_anchors[:, start : start + 256]).astype(bf16))
        if unit == 0:
            own = halves(anchors[:, at(COLUMN[5])], own)
        result = cluster_sums(interact(two_targets(own), rows(*sources), rows(*weight)))
        far_chain += [result[:, :RANK], result[:, RANK:]]

    def pushed(value, matrices):
        high, low = split(matrices)
        return folded(dot_nt(narrow(value), lanes(high, low)))

    value = far_chain[TOP]
    for level in range(TOP - 1, -1, -1):
        value = far_chain[level] + pushed(value, path[RANK * level : RANK * (level + 1), :])

    def children(parent, height, q):
        start = (ROW[height] + 2 * q) * RANK
        return pushed(parent, transfer[start : start + 128, :])

    upper = [far_fourth + children(value, 4, 0)]
    for height in (3, 2, 1, 0):
        lower = []
        for q, slab in enumerate(upper):
            for side in range(2):
                parent = slab[:, RANK * side : RANK * (side + 1)]
                index = 2 * q + side
                if height == 3:
                    own = far_third[index]
                else:
                    own = far[:, at(COLUMN[height] + 128 * index)]
                lower.append(own + children(parent, height, index))
        upper = lower
    for q, slab in enumerate(upper):
        expansion[:, at(128 * q)] = slab

    def two_leaves(q, carry):
        slab = expansion[:, pl.ds(pl.multiple_of(q * 128, 128), 128)]
        for leaf in range(2):
            columns = pl.ds(pl.multiple_of(q * 256 + leaf * 128, 128), 128)
            high, low = split(basis[:, columns])
            own = slab[:, RANK * leaf : RANK * (leaf + 1)]
            out[:, columns] = near[:, columns] + folded(dot(narrow(own), rows(high, low)))
        return carry

    lax.fori_loop(0, LEAVES_DEV // 2, two_leaves, 0, unroll=8)


def coarse_call(*arguments):
    return pl.pallas_call(
        coarse_kernel,
        out_shape=jax.ShapeDtypeStruct((RHS, LEAVES_DEV * LEAF), f32),
        in_specs=[SMEM] * 4 + [VMEM] * 17,
        out_specs=VMEM,
        scratch_shapes=[
            pltpu.VMEM((DIM, 24 * 128), f32),
            pltpu.VMEM((RHS, 16 * 128), f32),
            pltpu.VMEM((48, 64, 128), bf16),
            pltpu.VMEM((4, 4, 2, 64, 128), bf16),
            pltpu.VMEM((RHS, 2048), f32),
        ],
        compiler_params=pltpu.CompilerParams(vmem_limit_bytes=48 * 2**20),
        cost_estimate=pl.CostEstimate(flops=10**9, bytes_accessed=2**23, transcendentals=0),
        name="coarse",
    )(*arguments)


def shifted(value, by):
    return lax.ppermute(value, "leaf", [(i, (i + by) % DEVICES) for i in range(DEVICES)])


def as_columns(anchor_rows):
    return anchor_rows.reshape(-1, DIM).T


def pieces(array, parts):
    return jnp.concatenate([array[:, first:last] for first, last in parts], axis=1)


def on_device(
    points,
    charges,
    leaf_basis,
    local_transfer,
    local_anchors,
    local_lists,
    near_blocks,
    top_transfer,
    top_anchors,
    top_lists,
):
    index = lax.axis_index("leaf")
    device = index.reshape(1)
    half = NREACH * LEAF
    anchors = as_columns(jnp.pad(local_anchors, ((0, 1), (0, 0))))

    def rim(columns, parts):
        held = jnp.pad(pieces(anchors, parts), ((0, 0), (0, half - RIM_WIDTH)))
        return jnp.concatenate([points[:, columns], charges[:, columns], held], axis=0)

    low = shifted(rim(slice(half, None), HIGH_PIECES), 1)
    high = shifted(rim(slice(0, half), LOW_PIECES), -1)

    tables = lax.dynamic_index_in_dim(jnp.asarray(slot_tables()), index, 0, keepdims=False)
    levels = jnp.arange(TOP, dtype=jnp.int32)
    own_rows = 2 * DEVICES - (2 * DEVICES >> levels) + (index >> levels)
    path_rows = jnp.concatenate([own_rows, jnp.array([252, 253], jnp.int32)])
    path = jnp.take(top_transfer, path_rows, axis=0, mode="clip").reshape(-1, RANK)
    transfer = local_transfer.reshape(-1, RANK)
    moments, low_rim, high_rim, outgoing = moments_call(
        tables, leaf_basis, charges, transfer, path
    )
    incoming = lax.all_to_all(outgoing, "leaf", 0, 0)
    low_moments = shifted(high_rim, 1)
    high_moments = shifted(low_rim, -1)

    upper = levels + 1
    first_rows = DEVICES - (DEVICES >> (upper - 1))
    chain_rows = first_rows + (index >> upper)
    chain_lists = jnp.take(top_lists, chain_rows, axis=0, mode="clip")
    partner_rows = first_rows[:, None] + jnp.maximum(chain_lists, 0)
    wanted = jnp.concatenate([chain_rows[:1], chain_rows, partner_rows.reshape(-1)])
    chain_anchors = as_columns(jnp.take(top_anchors, wanted, axis=0, mode="clip"))

    def roots(array):
        return array[2 * DIM :, RIM[5] : RIM[5] + RANK]

    own_root = anchors[:, COLUMN[5] : COLUMN[5] + RANK]

    def second(columns, root_pair):
        held = jnp.concatenate([anchors[:, columns], anchors[:, 3840:3968]] + root_pair, axis=1)
        sent = jnp.concatenate([moments[:, columns], moments[:, 3840:4096]], axis=1)
        return jnp.concatenate([held, sent], axis=0)

    low_second = shifted(second(slice(3712, 3840), [roots(low), own_root]), 2)
    high_second = shifted(second(slice(3584, 3712), [own_root, roots(high)]), -2)

    near = near_call(device, near_blocks, points, charges, low, high)

    def third(parts):
        held = jnp.concatenate([anchors[:, 3840:3968]] + parts + [own_root], axis=1)
        sent = jnp.concatenate([moments[:, 3840:4096], moments[:, 3968:4096]], axis=1)
        return jnp.concatenate([held, sent], axis=0)

    near, low_second, high_second = lax.optimization_barrier((near, low_second, high_second))
    low_roots = low_second[:DIM, 256:384]
    high_roots = high_second[:DIM, 256:384]
    low_third = shifted(third([low_roots[:, RANK:], roots(low), low_roots[:, :RANK]]), 3)
    high_third = shifted(third([roots(high), high_roots[:, :RANK], high_roots[:, RANK:]]), -3)
    far = fine_call(device, local_lists, anchors, moments, low, high, low_moments, high_moments)
    return coarse_call(
        device,
        tables,
        local_lists,
        top_lists,
        anchors,
        moments,
        low,
        high,
        low_moments,
        high_moments,
        low_second,
        high_second,
        low_third,
        high_third,
        incoming,
        chain_anchors,
        path,
        transfer,
        leaf_basis,
        far,
        near,
    )


def solution(mesh):
    in_specs = (
        P(None, "leaf"),
        P(None, "leaf"),
        P(None, "leaf"),
        P("leaf", None),
        P("leaf", None),
        P("leaf", None),
        P("leaf", None),
        P(),
        P(),
        P(),
    )
    out_specs = P(None, "leaf")
    return jax.shard_map(
        on_device, mesh=mesh, in_specs=in_specs, out_specs=out_specs, check_vma=False
    )
```

time: 773 us -> 119 us (0.15)
  the two profiles are of different devices: /device:TPU:32 before, /device:TPU:0 now
where the time goes in v1:
time: 119 us; the launch traced here: 117 us
  Pallas kernels  43.4 us (36%)
  local copies, waits for them, and re-layouts  39.5 us (33%)
  starting transfers between devices  30.6 us (26%)
  other arithmetic  3.71 us (3%)
    ppermute x8, starting transfers between devices, shifted(): lax.ppermute(value, 'leaf', [(i, (i + by) % DEVICES) for i in range(DEVIC...  24.6 us
    unnamed x59, local copies, waits for them, and re-layouts  17 us
    pallas_call x1, Pallas kernels, near_call(): pl.pallas_call(near_kernel, out_shape=jax.ShapeDtypeStruct((RHS, LEAVES_D...  14.9 us
    pallas_call x1, Pallas kernels, coarse_call(): pl.pallas_call(coarse_kernel, out_shape=jax.ShapeDtypeStruct((RHS, LEAVES...  12 us
    pallas_call x1, Pallas kernels, fine_call(): pl.pallas_call(fine_kernel, out_shape=jax.ShapeDtypeStruct((RHS, 56 * RAN...  11.8 us
    reshape x4, local copies, waits for them, and re-layouts, as_columns(): return anchor_rows.reshape(-1, DIM).T  8.54 us
    all_to_all x1, starting transfers between devices, on_device(): incoming = lax.all_to_all(outgoing, 'leaf', 0, 0)  5.93 us
    pallas_call x1, Pallas kernels, moments_call(): pl.pallas_call(moments_kernel, out_shape=(shape((16, 4096), f32), shape((...  4.68 us
  transfers between devices with their start and end apart: 9, of which 0 were waited for; matrix products, arithmetic and copies ran while one was open for 17% of the time, Pallas kernels for 27%

profile of v1, /device:TPU:0, one launch (start us, length us, event | category | flops | bytes accessed | tf_op | source)
XLA Modules:
  0.0 117.4 jit_solution(9459614864097244266)
XLA Ops:
  0.0 1.0 pad.11
  1.0 2.1 %reshape.47 = f32[4096,16]{1,0:T(8,128)} reshape(f32[64,1024]{1,0:T(8,128)S(1)} %pad.11) | data formatting | bytes 524288 | tf_op jit(solution)/shard_map/reshape | solution.py:676
  3.1 2.2 %copy.18 = f32[4096,16]{0,1:T(8,128)S(1)} copy(f32[4096,16]{1,0:T(8,128)} %reshape.47) | data formatting | bytes 524288 | tf_op jit(solution)/shard_map/reshape | solution.py:676
  6.3 0.8 pad_maximum_fusion.1
  7.1 8.2 %collective-permute-start.1 = (f32[48,2048]{1,0:T(8,128)}, f32[48,2048]{1,0:T(8,128)}, u32[]{:S(2)}, u32[]{:S(2)}) collective-permute-start(f32[48,2048]{1,0:T(8,128)} %pad_maximum_fusion.1), channel_id=1, source_target_pairs={{0,127},{1,0},{2,1},{3,2},{4,3},{5,4},{6,5},{7,6},{8,7},{9,8},{10,... | collective-permute-start | bytes 1179656 | tf_op jit(solution)/shard_map/ppermute | solution.py:672
  15.4 2.9 %gather_fusion = f32[9,4096]{1,0:T(8,128)S(1)} fusion(f32[254,4096]{1,0:T(8,128)} %param.19, s32[1024]{0:T(1024)S(1)} %pad_clamp_fusion.2), kind=kCustom, calls=%fused_computation | custom fusion | bytes 294948 | tf_op jit(solution)/shard_map/jit(_take)/gather | solution.py:711
  18.4 2.0 %reshape.48.transfer = f32[3968,64]{1,0:T(8,128)S(1)} reshape(f32[62,4096]{1,0:T(8,128)} %param.15) | data formatting | bytes 2031616 | tf_op jit(solution)/shard_map/reshape | solution.py:712
  20.3 0.8 dynamic-slice_reduce_fusion.tables
  21.2 1.2 %copy-done.2 = f32[64,4096]{1,0:T(8,128)S(1)} copy-done((f32[64,4096]{1,0:T(8,128)S(1)}, f32[64,4096]{1,0:T(8,128)}, u32[]{:S(2)}) %copy-start.2) | copy-done | bytes 1048600
  22.4 0.9 copy-done.10
  23.3 4.7 %moments.1 = (f32[16,4096]{1,0:T(8,128)S(1)}, f32[16,1664]{1,0:T(8,128)}, f32[16,1664]{1,0:T(8,128)}, f32[128,32,128]{2,1,0:T(8,128)S(1)}) custom-call(s32[1280]{0:T(1024)S(1)} %dynamic-slice_reduce_fusion.tables, f32[64,4096]{1,0:T(8,128)S(1)} %copy-done.2, f32[16,4096]{1,0:T(8,128)S(1)} %copy-done.10, f32[3968,64]{1,0:T(8,128)S(1)} %reshape.48.transfer, ...), custom_call_target="tpu_custom_call" | custom-call | flops 1000000000 | bytes 4194304 | tf_op jit(solution)/shard_map/moments/pallas_call | solution.py:217
  28.0 1.3 %copy-done.1 = f32[128,32,128]{2,1,0:T(8,128)} copy-done((f32[128,32,128]{2,1,0:T(8,128)}, f32[128,32,128]{2,1,0:T(8,128)S(1)}, u32[]{:S(2)}) %copy-start.1) | copy-done | bytes 2097176
  29.3 5.9 %all-to-all-start = ((f32[128,32,128]{2,1,0:T(8,128)}), f32[128,32,128]{2,1,0:T(8,128)}, u32[]{:S(2)}, u32[]{:S(2)}) async-start(f32[128,32,128]{2,1,0:T(8,128)} %copy-done.1), calls=%async_computation | async-start | bytes 4194304 | tf_op jit(solution)/shard_map/all_to_all | solution.py:716
  35.4 7.2 %collective-permute-start.3 = (f32[16,1664]{1,0:T(8,128)}, f32[16,1664]{1,0:T(8,128)}, u32[]{:S(2)}, u32[]{:S(2)}) collective-permute-start(f32[16,1664]{1,0:T(8,128)} %get-tuple-element.14), channel_id=1, source_target_pairs={{0,127},{1,0},{2,1},{3,2},{4,3},{5,4},{6,5},{7,6},{8,7},{9,8},{10,... | collective-permute-start | bytes 319496 | tf_op jit(solution)/shard_map/ppermute | solution.py:672
  46.8 2.1 %reshape.50 = f32[4096,16]{1,0:T(8,128)} reshape(f32[64,1024]{1,0:T(8,128)S(1)} %gather_fusion.2) | data formatting | bytes 524288 | tf_op jit(solution)/shard_map/reshape | solution.py:676
  48.9 2.2 %copy.21 = f32[4096,16]{0,1:T(8,128)S(1)} copy(f32[4096,16]{1,0:T(8,128)} %reshape.50) | data formatting | bytes 524288 | tf_op jit(solution)/shard_map/reshape | solution.py:676
  53.1 0.8 maximum_maximum_fusion
  54.0 7.4 %collective-permute-start.5 = (f32[32,384]{1,0:T(8,128)S(1)}, f32[32,384]{1,0:T(8,128)S(1)}, u32[]{:S(2)}, u32[]{:S(2)}) collective-permute-start(f32[32,384]{1,0:T(8,128)S(1)} %maximum_maximum_fusion), channel_id=1, source_target_pairs={{0,126},{1,127},{2,0},{3,1},{4,2},{5,3},{6,4},{7,5},{8,6},{9,7},{1... | collective-permute-start | bytes 147464 | tf_op jit(solution)/shard_map/ppermute | solution.py:672
  61.4 0.9 copy-done.11
  62.4 0.9 copy-done.13
  63.3 14.9 %near.1 = f32[16,4096]{1,0:T(8,128)S(1)} custom-call(s32[1]{0:T(128)} %bitcast.device, s32[32,8]{1,0:T(8,128)S(1)} %copy.19.near_blocks, f32[16,4096]{1,0:T(8,128)S(1)} %copy-done.13, f32[16,4096]{1,0:T(8,128)S(1)} %copy-done.11, f32[48,2048]{1,0:T(8,128)} %collective-permute-done.low.low_anchors, f32[48,2048]{1,0:T(8,128)} %collective-permute-done.1.high.high_anchors), custom_call_target="tpu_custom_call" | custom-call | flops 10000000000 | bytes 4194304 | tf_op jit(solution)/shard_map/near/pallas_call | solution.py:287
  80.2 1.4 %concatenate.66 = f32[16,384]{1,0:T(8,128)} concatenate(f32[16,128]{1,0:T(8,128)} %get-tuple-element.19, f32[16,64]{1,0:T(8,128)} %get-tuple-element.33, f32[16,64]{1,0:T(8,128)} %copy-done.23, f32[16,64]{1,0:T(8,128)S(1)} %get-tuple-element.32, f32[16,64]{1,0:T(8,128)S(1)} %slice.135), dimensions={1} | concatenate | bytes 49152 | tf_op jit(solution)/shard_map/concatenate | solution.py:744
  81.6 0.9 fusion.1
  82.5 1.7 %collective-permute-start.6 = (f32[32,384]{1,0:T(8,128)S(1)}, f32[32,384]{1,0:T(8,128)S(1)}, u32[]{:S(2)}, u32[]{:S(2)}) collective-permute-start(f32[32,384]{1,0:T(8,128)S(1)} %get-tuple-element.35), channel_id=1, source_target_pairs={{0,3},{1,4},{2,5},{3,6},{4,7},{5,8},{6,9},{7,10},{8,11},{9,12},{10... | collective-permute-start | bytes 147464 | tf_op jit(solution)/shard_map/ppermute | solution.py:672
  84.3 0.9 copy-done.5
  85.2 11.8 %fine.1.far = f32[16,3584]{1,0:T(8,128)S(1)} custom-call(s32[1]{0:T(128)} %bitcast.device, s32[63,8]{1,0:T(8,128)S(1)} %copy.23.lists, f32[16,4096]{1,0:T(8,128)S(1)} %bitcast.13, f32[16,4096]{1,0:T(8,128)S(1)} %copy-done.5, f32[48,2048]{1,0:T(8,128)} %collective-permute-done.low.low_anchors, f32[48,2048]{1,0:T(8,128)} %collective-permute-done.1.high.high_anchors, ...), custom_call_target="tpu_custom_call" | custom-call | flops 5000000000 | bytes 4194304 | tf_op jit(solution)/shard_map/fine/pallas_call | solution.py:432
  99.0 1.2 %copy-done.3 = f32[64,4096]{1,0:T(8,128)S(1)} copy-done((f32[64,4096]{1,0:T(8,128)S(1)}, f32[64,4096]{1,0:T(8,128)}, u32[]{:S(2)}) %copy-start.3) | copy-done | bytes 1048600
  100.2 0.9 copy-done.6
  101.2 0.9 copy-done.8
  102.1 0.9 copy-done.15
  103.1 0.8 copy-done.17
  105.5 12.0 %coarse.1 = f32[16,4096]{1,0:T(8,128)} custom-call(s32[1]{0:T(128)} %bitcast.device, s32[1280]{0:T(1024)S(1)} %dynamic-slice_reduce_fusion.tables, s32[63,8]{1,0:T(8,128)S(1)} %copy.23.lists, s32[127,8]{1,0:T(8,128)S(1)} %copy.24.top_lists, f32[16,4096]{1,0:T(8,128)S(1)} %bitcast.14, f32[16,4096]{1,0:T(8,128)S(1)} %copy-done.6, ...), custom_call_target="tpu_custom_call" | custom-call | flops 1000000000 | bytes 8388608 | tf_op jit(solution)/shard_map/coarse/pallas_call | solution.py:653
  (94 shorter events, 13.1 us)
Async XLA Ops:
  0.0 46.1 %copy-start = (f32[127,1024]{1,0:T(8,128)S(1)}, f32[127,1024]{1,0:T(8,128)}, u32[]{:S(2)}) copy-start(f32[127,1024]{1,0:T(8,128)} %param.20) | copy-start | bytes 1560580
  1.0 4.3 %copy-start.12 = (f32[16,4096]{1,0:T(8,128)S(1)}, f32[16,4096]{1,0:T(8,128)}, u32[]{:S(2)}) copy-start(f32[16,4096]{1,0:T(8,128)} %points.1) | copy-start | bytes 786436
  3.1 2.3 %copy-start.9 = (f32[16,4096]{1,0:T(8,128)S(1)}, f32[16,4096]{1,0:T(8,128)}, u32[]{:S(2)}) copy-start(f32[16,4096]{1,0:T(8,128)} %charges.3) | copy-start | bytes 786436
  5.3 10.0 %copy-start.27 = (s32[2]{0:T(128)S(1)}, s32[2]{0:T(128)}, u32[]{:S(2)}) copy-start(s32[2]{0:T(128)} %constant.27.clone) | copy-start | bytes 28
  6.2 44.8 %collective-permute-start = (f32[48,2048]{1,0:T(8,128)}, f32[48,2048]{1,0:T(8,128)}, u32[]{:S(2)}, u32[]{:S(2)}) collective-permute-start(f32[48,2048]{1,0:T(8,128)} %pad_maximum_fusion), channel_id=1, source_target_pairs={{0,1},{1,2},{2,3},{3,4},{4,5},{5,6},{6,7},{7,8},{8,9},{9,10},{10,1... | collective-permute-start | bytes 1179656 | tf_op jit(solution)/shard_map/ppermute | solution.py:672
  7.1 45.3 %collective-permute-start.1 = (f32[48,2048]{1,0:T(8,128)}, f32[48,2048]{1,0:T(8,128)}, u32[]{:S(2)}, u32[]{:S(2)}) collective-permute-start(f32[48,2048]{1,0:T(8,128)} %pad_maximum_fusion.1), channel_id=1, source_target_pairs={{0,127},{1,0},{2,1},{3,2},{4,3},{5,4},{6,5},{7,6},{8,7},{9,8},{10,... | collective-permute-start | bytes 1179656 | tf_op jit(solution)/shard_map/ppermute | solution.py:672
  21.2 1.2 %copy-start.2 = (f32[64,4096]{1,0:T(8,128)S(1)}, f32[64,4096]{1,0:T(8,128)}, u32[]{:S(2)}) copy-start(f32[64,4096]{1,0:T(8,128)} %basis.3) | copy-start | bytes 3145732
  22.4 0.9 copy-start.10
  28.0 1.3 %copy-start.1 = (f32[128,32,128]{2,1,0:T(8,128)}, f32[128,32,128]{2,1,0:T(8,128)S(1)}, u32[]{:S(2)}) copy-start(f32[128,32,128]{2,1,0:T(8,128)S(1)} %get-tuple-element.17) | copy-start | bytes 6291460
  29.3 16.4 %copy-start.4 = (f32[16,4096]{1,0:T(8,128)}, f32[16,4096]{1,0:T(8,128)S(1)}, u32[]{:S(2)}) copy-start(f32[16,4096]{1,0:T(8,128)S(1)} %get-tuple-element.12.moments) | copy-start | bytes 786436
  29.3 13.8 %copy-start.24 = (s32[127,8]{0,1:T(8,128)S(1)}, s32[127,8]{0,1:T(8,128)}, u32[]{:S(2)}) copy-start(s32[127,8]{0,1:T(8,128)} %param.21) | copy-start | bytes 12196
  29.3 16.4 %copy-start.25 = (s32[32,8]{0,1:T(8,128)S(1)}, s32[32,8]{0,1:T(8,128)}, u32[]{:S(2)}) copy-start(s32[32,8]{0,1:T(8,128)} %param.18) | copy-start | bytes 3076
  29.3 16.5 %copy-start.26 = (s32[63,8]{0,1:T(8,128)S(1)}, s32[63,8]{0,1:T(8,128)}, u32[]{:S(2)}) copy-start(s32[63,8]{0,1:T(8,128)} %param.17) | copy-start | bytes 6052
  29.3 69.6 %all-to-all-start = ((f32[128,32,128]{2,1,0:T(8,128)}), f32[128,32,128]{2,1,0:T(8,128)}, u32[]{:S(2)}, u32[]{:S(2)}) async-start(f32[128,32,128]{2,1,0:T(8,128)} %copy-done.1), calls=%async_computation | async-start | bytes 4194304 | tf_op jit(solution)/shard_map/all_to_all | solution.py:716
  35.3 49.0 %collective-permute-start.2 = (f32[16,1664]{1,0:T(8,128)}, f32[16,1664]{1,0:T(8,128)}, u32[]{:S(2)}, u32[]{:S(2)}) collective-permute-start(f32[16,1664]{1,0:T(8,128)} %get-tuple-element.13), channel_id=1, source_target_pairs={{0,1},{1,2},{2,3},{3,4},{4,5},{5,6},{6,7},{7,8},{8,9},{9,10},{10,1... | collective-permute-start | bytes 319496 | tf_op jit(solution)/shard_map/ppermute | solution.py:672
  35.4 48.9 %collective-permute-start.3 = (f32[16,1664]{1,0:T(8,128)}, f32[16,1664]{1,0:T(8,128)}, u32[]{:S(2)}, u32[]{:S(2)}) collective-permute-start(f32[16,1664]{1,0:T(8,128)} %get-tuple-element.14), channel_id=1, source_target_pairs={{0,127},{1,0},{2,1},{3,2},{4,3},{5,4},{6,5},{7,6},{8,7},{9,8},{10,... | collective-permute-start | bytes 319496 | tf_op jit(solution)/shard_map/ppermute | solution.py:672
  52.4 26.5 %collective-permute-start.4 = (f32[32,384]{1,0:T(8,128)S(1)}, f32[32,384]{1,0:T(8,128)S(1)}, u32[]{:S(2)}, u32[]{:S(2)}) collective-permute-start(f32[32,384]{1,0:T(8,128)S(1)} %fusion), channel_id=1, source_target_pairs={{0,2},{1,3},{2,4},{3,5},{4,6},{5,7},{6,8},{7,9},{8,10},{9,11},{10,... | collective-permute-start | bytes 147464 | tf_op jit(solution)/shard_map/ppermute | solution.py:672
  53.1 8.3 %copy-start.22 = (f32[16,64]{1,0:T(8,128)}, f32[16,64]{1,0:T(8,128)S(1)}, u32[]{:S(2)}) copy-start(f32[16,64]{1,0:T(8,128)S(1)} %slice.138) | copy-start | bytes 12292
  54.0 25.0 %collective-permute-start.5 = (f32[32,384]{1,0:T(8,128)S(1)}, f32[32,384]{1,0:T(8,128)S(1)}, u32[]{:S(2)}, u32[]{:S(2)}) collective-permute-start(f32[32,384]{1,0:T(8,128)S(1)} %maximum_maximum_fusion), channel_id=1, source_target_pairs={{0,126},{1,127},{2,0},{3,1},{4,2},{5,3},{6,4},{7,5},{8,6},{9,7},{1... | collective-permute-start | bytes 147464 | tf_op jit(solution)/shard_map/ppermute | solution.py:672
  61.4 1.0 copy-start.11
  62.4 0.9 copy-start.13
  78.2 0.7 copy-start.7
  82.5 15.2 %collective-permute-start.7 = (f32[32,384]{1,0:T(8,128)S(1)}, f32[32,384]{1,0:T(8,128)S(1)}, u32[]{:S(2)}, u32[]{:S(2)}) collective-permute-start(f32[32,384]{1,0:T(8,128)S(1)} %get-tuple-element.34), channel_id=1, source_target_pairs={{0,125},{1,126},{2,127},{3,0},{4,1},{5,2},{6,3},{7,4},{8,5},{9,6},... | collective-permute-start | bytes 147464 | tf_op jit(solution)/shard_map/ppermute | solution.py:672
  82.5 15.8 %collective-permute-start.6 = (f32[32,384]{1,0:T(8,128)S(1)}, f32[32,384]{1,0:T(8,128)S(1)}, u32[]{:S(2)}, u32[]{:S(2)}) collective-permute-start(f32[32,384]{1,0:T(8,128)S(1)} %get-tuple-element.35), channel_id=1, source_target_pairs={{0,3},{1,4},{2,5},{3,6},{4,7},{5,8},{6,9},{7,10},{8,11},{9,12},{10... | collective-permute-start | bytes 147464 | tf_op jit(solution)/shard_map/ppermute | solution.py:672
  84.3 1.0 copy-start.5
  99.0 1.2 %copy-start.3 = (f32[64,4096]{1,0:T(8,128)S(1)}, f32[64,4096]{1,0:T(8,128)}, u32[]{:S(2)}) copy-start(f32[64,4096]{1,0:T(8,128)} %basis.3) | copy-start | bytes 3145732
  100.2 0.9 copy-start.6
  101.2 0.9 copy-start.8
  102.1 0.9 copy-start.15
  103.1 0.8 copy-start.17
  103.9 0.8 copy-start.19
  104.7 0.8 copy-start.21
  (5 other events, 3.1 us)

commit v2 on v1

v2 whole, which is shorter than its diff:
```python
import math

import jax
import jax.numpy as jnp
import numpy as np
from jax import lax
from jax.experimental import pallas as pl
from jax.experimental.pallas import tpu as pltpu
from jax.sharding import PartitionSpec as P

DIM = 16
RHS = 16
LEAF = 128
RANK = 64
LEAVES_DEV = 32
NREACH = 16
REACH = 6
DEVICES = 128
TOP = 7
SHARED = 6
SLOTS = 4
NOTHING = 7
ANCHORS = 8
FORMED = (-6, -5, 5, 6)
LOCAL = 62
MATRICES = LOCAL + 13

bf16 = jnp.bfloat16
f32 = jnp.float32
SCALE = math.log2(math.e) / math.sqrt(3.0)
LN2 = math.log(2.0)
TINY = 1e-30

COLUMN = [0, 2048, 3072, 3584, 3840, 3968]
ROW = [0, 32, 48, 56, 60]
RIM = [0, 384, 768, 1152, 1408, 1536]
RIM_WIDTH = 1664
LOW_PIECES = [(0, 384), (2048, 2432), (3072, 3456), (3584, 4096)]
HIGH_PIECES = [(1664, 2048), (2688, 3072), (3200, 4096)]
VMEM_LIMIT = 60 * 2**20
VMEM = pl.BlockSpec(memory_space=pltpu.VMEM)
SMEM = pl.BlockSpec(memory_space=pltpu.SMEM)
HBM = pl.BlockSpec(memory_space=pltpu.HBM)


def relevant(first, second, level):
    return 2 <= abs((first >> level) - (second >> level)) <= REACH


def slot_tables():
    sent = np.full((DEVICES, DEVICES, SLOTS), NOTHING, np.int32)
    held = np.zeros((DEVICES, SHARED + 1, DEVICES), np.int32)
    for first in range(DEVICES):
        for second in range(DEVICES):
            levels = [level for level in range(SHARED) if relevant(first, second, level)]
            if levels and levels[0] == 0:
                if len(levels) == 3:
                    levels.pop()
                    held[first, 2, second] = SLOTS + FORMED.index(second - first)
                levels.append(ANCHORS)
            for slot, level in enumerate(levels):
                sent[first, second, slot] = level
                held[first, SHARED if level == ANCHORS else level, second] = slot
            sent[first, second, SLOTS - 1] = SHARED
    tables = np.concatenate([sent.reshape(DEVICES, -1), held.reshape(DEVICES, -1)], axis=1)
    return tables.reshape(DEVICES, -1, 128)


SENT = DEVICES * SLOTS
TABLE = (SENT + (SHARED + 1) * DEVICES) // 128


def started(semaphores, *pairs):
    copies = []
    for index, (source, target) in enumerate(pairs):
        copy = pltpu.make_async_copy(source, target, semaphores.at[index])
        copy.start()
        copies.append(copy)
    return copies


def split(x):
    high = x.astype(bf16)
    return high, (x - high.astype(f32)).astype(bf16)


def lanes(*parts):
    return jnp.concatenate(parts, axis=1)


def rows(*parts):
    return jnp.concatenate(parts, axis=0)


def dot(a, b):
    return jnp.dot(a, b, preferred_element_type=f32)


def dot_nt(a, b):
    return lax.dot_general(a, b, (((1,), (1,)), ((), ())), preferred_element_type=f32)


def narrow(x):
    high, low = split(x)
    return rows(lanes(high, high), lanes(low, low))


def folded(x):
    return x[:16] + x[16:]


def sides(x):
    x = x * SCALE
    high = x.astype(bf16).astype(f32)
    low = (x - high).astype(bf16).astype(f32)
    norm = jnp.sum(high * (high + 2.0 * low), axis=0, keepdims=True)
    norm_high = norm.astype(bf16).astype(f32)
    norm_middle = (norm - norm_high).astype(bf16).astype(f32)
    norm_low = norm - norm_high - norm_middle
    row = lax.broadcasted_iota(jnp.int32, x.shape, 0)
    parts = jnp.where(row % 3 == 0, norm_high, jnp.where(row % 3 == 1, norm_middle, norm_low))
    return high, low, parts, row


def source_side(x):
    high, low, parts, row = sides(x)
    tail = jnp.where(row < 3, 1.0, jnp.where(row < 6, parts, 0.0))
    return rows(high, high, low, tail)


def target_sides(x):
    high, low, parts, row = sides(x)
    tail = jnp.where(row < 3, parts, jnp.where(row < 6, 1.0, 0.0))
    factors = rows(-2.0 * high, -2.0 * low, -2.0 * high, tail)
    first = rows(factors, jnp.zeros_like(factors)).T
    return first.astype(bf16), pltpu.roll(first, RANK, 1).astype(bf16)


def matern(squared):
    squared = jnp.maximum(squared, TINY)
    distance = squared * lax.rsqrt(squared)
    return (1.0 + LN2 * distance) * jnp.exp2(-distance)


def pick(parts):
    lane = lax.broadcasted_iota(jnp.int32, parts[0].shape, 1)
    result = parts[3]
    for j in (2, 1, 0):
        result = jnp.where(lane < 32 * (j + 1), parts[j], result)
    return result


def interact(targets, sources, weights):
    kernel = matern(dot(targets, sources))
    high, low = split(kernel)
    size = kernel.shape[0]
    result = dot(rows(high, low), weights)
    quarter = size // 4
    return pick(
        [
            result[quarter * j : quarter * (j + 1)]
            + result[size + quarter * j : size + quarter * (j + 1)]
            for j in range(4)
        ]
    )


def weight_turns(slabs):
    parts = []
    for slab in slabs:
        high = slab.astype(bf16).astype(f32)
        parts += [high, slab - high]
    columns = rows(*parts).T
    return [
        (columns if turn == 0 else pltpu.roll(columns, 32 * turn, 1)).astype(bf16)
        for turn in range(4)
    ]


def halves(first, second):
    lane = lax.broadcasted_iota(jnp.int32, first.shape, 1)
    return jnp.where(lane < RANK, first, second)


def regrouped(load, staged, count, width):
    for c in range(count):
        value = load(c)
        for i in range(width):
            staged[8 * i + c : 8 * i + c + 1, :] = value[:, 128 * i : 128 * (i + 1)]


def tile(staged, c, width):
    return staged[pl.ds(c, width, stride=8), :]


def store_matrix(staged, c, matrices, index):
    value = tile(staged, c, 32)
    matrices[pl.ds(RANK * index, 32, stride=2), :] = value[:, :RANK]
    matrices[pl.ds(RANK * index + 1, 32, stride=2), :] = value[:, RANK:]


def eight_anchors(tiles):
    group = lax.broadcasted_iota(jnp.int32, (8, 128), 1) // 16
    for bit in (1, 2, 4):
        turned = list(tiles)
        for p in range(8):
            if p & bit == 0:
                first, second = tiles[p], tiles[p | bit]
                turned[p] = jnp.where(group & bit == 0, first, pltpu.roll(second, 16 * bit, 1))
                turned[p | bit] = jnp.where(
                    group & bit == 0, pltpu.roll(first, 128 - 16 * bit, 1), second
                )
        tiles = turned
    held = rows(*tiles).T
    slabs = [lanes(held[32 * q : 32 * q + 16], held[32 * q + 16 : 32 * q + 32]) for q in range(4)]
    value = rows(*slabs)
    high = value.astype(bf16)
    rest = value - high.astype(f32)
    middle = rest.astype(bf16)
    low = (rest - middle.astype(f32)).astype(bf16)
    row = lax.broadcasted_iota(jnp.int32, (128, 128), 0)
    column = lax.broadcasted_iota(jnp.int32, (128, 128), 1)
    order = (row & RANK) + 8 * (row & 7) + ((row & 63) >> 3)
    order = jnp.where(order == column, 1.0, 0.0).astype(bf16)
    value = dot(rows(high, middle, low), order)
    value = value[:64] + (value[64:128] + value[128:])
    return [value[16 * q : 16 * (q + 1)] for q in range(4)]


def lifted(slab, matrices):
    high, low = split(matrices)
    return folded(dot(narrow(slab), rows(high, low)))


def as_block(value):
    return lanes(value[:8], value[8:])


def moments_kernel(
    device,
    tables_hbm,
    basis_hbm,
    charges_hbm,
    transfer_hbm,
    anchors_hbm,
    top_hbm,
    moments_out,
    anchors_out,
    inner_out,
    outer_out,
    third,
    outgoing_out,
    matrices_out,
    tables,
    basis,
    charges,
    transfer,
    anchor_rows,
    top_transfer,
    moments,
    anchors,
    inner,
    outer,
    outgoing,
    matrices,
    blocks,
    staged,
    staged_anchors,
    semaphores,
):
    me = device[0]
    quarters = [slice(1024 * i, 1024 * (i + 1)) for i in range(4)]
    loads = started(
        semaphores,
        (charges_hbm, charges),
        *[(basis_hbm.at[:, part], basis.at[:, part]) for part in quarters],
        (transfer_hbm, transfer),
        (top_hbm, top_transfer),
        (anchors_hbm, anchor_rows),
        (tables_hbm.at[me], tables),
    )
    loads[0].wait()

    def two_leaves(q, carry):
        parts = []
        for leaf in range(2):
            columns = pl.ds(pl.multiple_of(q * 256 + leaf * 128, 128), 128)
            high, low = split(basis[:, columns])
            parts.append(folded(dot_nt(narrow(charges[:, columns]), lanes(high, low))))
        moments[:, pl.ds(pl.multiple_of(q * 128, 128), 128)] = lanes(*parts)
        return carry

    for part in range(4):
        loads[1 + part].wait()
        lax.fori_loop(4 * part, 4 * part + 4, two_leaves, 0, unroll=4)

    loads[5].wait()
    for group in range(8):
        count = min(8, LOCAL - 8 * group)
        for i in range(32):
            staged[group % 2, 8 * i : 8 * i + count, :] = transfer[
                8 * group : 8 * group + count, 128 * i : 128 * (i + 1)
            ]
        for c in range(count):
            store_matrix(staged.at[group % 2], c, matrices, 8 * group + c)
    loads[6].wait()
    chain = [2 * DEVICES - (2 * DEVICES >> level) + (me >> level) for level in range(TOP)]
    chain += [252, 253]
    for shift in FORMED:
        other = jnp.minimum(jnp.maximum(me + shift, 0), DEVICES - 1)
        chain.append(DEVICES + (other >> 1))
    for group in range(2):
        part = chain[8 * group : 8 * group + 8]
        regrouped(lambda c: top_transfer[pl.ds(part[c], 1), :], staged.at[group], len(part), 32)
        for c in range(len(part)):
            store_matrix(staged.at[group], c, matrices, LOCAL + 8 * group + c)
    stores = started(semaphores.at[9:], (matrices, matrices_out))

    loads[7].wait()
    for group in range(8):
        count = min(8, 63 - 8 * group)
        for i in range(8):
            staged_anchors[group % 2, 8 * i : 8 * i + count, :] = anchor_rows[
                8 * group : 8 * group + count, 128 * i : 128 * (i + 1)
            ]
        tiles = [tile(staged_anchors.at[group % 2], c, 8) for c in range(count)]
        tiles += [jnp.zeros((8, 128), f32)] * (8 - count)
        for q, slab in enumerate(eight_anchors(tiles)):
            anchors[:, 512 * group + 128 * q : 512 * group + 128 * (q + 1)] = slab

    for height in range(5):
        number = LEAVES_DEV >> height
        parents = []
        for q in range(number // 2):
            start = (ROW[height] + 2 * q) * RANK
            slab = moments[:, COLUMN[height] + 128 * q : COLUMN[height] + 128 * (q + 1)]
            parents.append(lifted(slab, matrices[start : start + 128, :]))
        if height == 4:
            parents.append(jnp.zeros((16, RANK), f32))
        for q in range(len(parents) // 2):
            start = COLUMN[height + 1] + 128 * q
            moments[:, start : start + 128] = lanes(parents[2 * q], parents[2 * q + 1])

    even = (me & 1) == 0

    def fill(low_rim, high_rim):
        for row, value in ((slice(0, DIM), anchors), (slice(DIM, 2 * DIM), moments)):
            for rim, parts in ((low_rim, LOW_PIECES), (high_rim, HIGH_PIECES)):
                start = 0
                for first, last in parts:
                    rim[row, start : start + last - first] = value[:, first:last]
                    start += last - first

    @pl.when(even)
    def _():
        fill(outer, inner)

    @pl.when(jnp.logical_not(even))
    def _():
        fill(inner, outer)

    third[:DIM, :] = anchors[:, 3840:3968]
    third[DIM:, :] = moments[:, 3840:3968]
    stores += started(
        semaphores.at[10:],
        (inner, inner_out),
        (outer, outer_out),
        (moments, moments_out),
        (anchors, anchors_out),
    )

    value = moments[:, COLUMN[5] : COLUMN[5] + RANK]
    for level in range(SHARED + 1):
        blocks[level] = as_block(value)
        if level < SHARED:
            start = RANK * (LOCAL + level)
            value = lifted(value, matrices[start : start + RANK, :])
    blocks[NOTHING] = jnp.zeros((8, 128), f32)
    blocks[ANCHORS] = as_block(anchors[:, COLUMN[5] : COLUMN[5] + RANK])

    def one_device(other, carry):
        for slot in range(SLOTS - 1):
            kind = tables[other // 32, (other % 32) * SLOTS + slot]
            outgoing[other, 8 * slot : 8 * (slot + 1), :] = blocks[kind]
        outgoing[other, 8 * (SLOTS - 1) : 8 * SLOTS, :] = blocks[SHARED]
        return carry

    loads[8].wait()
    for part in range(4):
        lax.fori_loop(32 * part, 32 * part + 32, one_device, 0, unroll=8)
        own = slice(32 * part, 32 * part + 32)
        stores += started(semaphores.at[14 + part :], (outgoing.at[own], outgoing_out.at[own]))
    for copy in stores:
        copy.wait()


def moments_call(*arguments):
    shape = jax.ShapeDtypeStruct
    return pl.pallas_call(
        moments_kernel,
        out_shape=(
            shape((16, 4096), f32),
            shape((16, 4096), f32),
            shape((32, RIM_WIDTH), f32),
            shape((32, RIM_WIDTH), f32),
            shape((32, 128), f32),
            shape((DEVICES, 8 * SLOTS, 128), f32),
            shape((MATRICES * RANK, RANK), f32),
        ),
        in_specs=[SMEM] + [HBM] * 6,
        out_specs=(HBM, HBM, HBM, HBM, VMEM, HBM, HBM),
        scratch_shapes=[
            pltpu.SMEM((TABLE, 128), jnp.int32),
            pltpu.VMEM((RANK, 4096), f32),
            pltpu.VMEM((RHS, 4096), f32),
            pltpu.VMEM((LOCAL, RANK * RANK), f32),
            pltpu.VMEM((63, RANK * DIM), f32),
            pltpu.VMEM((254, RANK * RANK), f32),
            pltpu.VMEM((RHS, 4096), f32),
            pltpu.VMEM((DIM, 4096), f32),
            pltpu.VMEM((32, RIM_WIDTH), f32),
            pltpu.VMEM((32, RIM_WIDTH), f32),
            pltpu.VMEM((DEVICES, 8 * SLOTS, 128), f32),
            pltpu.VMEM((MATRICES * RANK, RANK), f32),
            pltpu.VMEM((9, 8, 128), f32),
            pltpu.VMEM((2, 256, 128), f32),
            pltpu.VMEM((2, 64, 128), f32),
            pltpu.SemaphoreType.DMA((18,)),
        ],
        compiler_params=pltpu.CompilerParams(vmem_limit_bytes=VMEM_LIMIT),
        cost_estimate=pl.CostEstimate(flops=10**9, bytes_accessed=2**22, transcendentals=0),
        name="moments",
    )(*arguments)


def near_kernel(
    device,
    near_blocks,
    points_hbm,
    charges_hbm,
    inner_hbm,
    outer_hbm,
    out_hbm,
    points,
    charges,
    inner,
    outer,
    out,
    factors,
    weights,
    semaphores,
):
    me = device[0]
    loads = started(
        semaphores,
        (points_hbm, points),
        (charges_hbm, charges),
        (inner_hbm, inner),
        (outer_hbm, outer),
    )

    def prepare(point_ref, charge_ref, charge_row, first):
        def four_leaves(i, carry):
            columns = pl.ds(pl.multiple_of(i * 512, 512), 512)
            side = source_side(point_ref[:DIM, columns]).astype(bf16)
            charge = charge_ref[charge_row : charge_row + RHS, columns]
            slabs = []
            for m in range(4):
                factors[(first + i) * 4 + m] = side[:, 128 * m : 128 * (m + 1)]
                slabs.append(charge[:, 128 * m : 128 * (m + 1)])
            for turn, value in enumerate(weight_turns(slabs)):
                weights[turn, first + i] = value
            return carry

        return four_leaves

    loads[0].wait()
    loads[1].wait()
    lax.fori_loop(0, 8, prepare(points, charges, 0, 4), 0, unroll=2)
    side = (me & 1) * 12
    loads[2].wait()
    lax.fori_loop(0, 4, prepare(inner, inner, DIM, 12 - side), 0, unroll=2)
    loads[3].wait()
    lax.fori_loop(0, 4, prepare(outer, outer, DIM, side), 0, unroll=2)
    factors[64] = jnp.zeros((64, 128), bf16)
    for turn in range(4):
        weights[turn, 16] = jnp.zeros((128, 128), bf16)
    first_leaf = me * LEAVES_DEV - NREACH

    def one_leaf(t, carry):
        columns = pl.ds(pl.multiple_of(t * 128, 128), 128)
        front, back = target_sides(points[:, columns])
        empty = jnp.zeros_like(front)
        targets = rows(
            lanes(front, empty), lanes(back, empty), lanes(empty, front), lanes(empty, back)
        )
        located = []
        for j in range(8):
            block = near_blocks[t, j]
            inside = jnp.minimum(jnp.maximum(block - first_leaf, 0), 63)
            located.append(jnp.where(block < 0, 64, inside))
        sources = rows(
            *[lanes(factors[located[2 * j]], factors[located[2 * j + 1]]) for j in range(4)]
        )
        weight = rows(
            *[
                pick([weights[(j - located[2 * j + h]) & 3, located[2 * j + h] >> 2] for j in range(4)])
                for h in range(2)
            ]
        )
        total = interact(targets, sources, weight).T
        out[:, columns] = sum(total[16 * g : 16 * (g + 1)] for g in range(8))
        return carry

    stores = []
    for part in range(2):
        lax.fori_loop(16 * part, 16 * part + 16, one_leaf, 0, unroll=8)
        own = slice(2048 * part, 2048 * part + 2048)
        stores += started(semaphores.at[4 + part :], (out.at[:, own], out_hbm.at[:, own]))
    for copy in stores:
        copy.wait()


def near_call(*arguments):
    return pl.pallas_call(
        near_kernel,
        out_shape=jax.ShapeDtypeStruct((RHS, LEAVES_DEV * LEAF), f32),
        in_specs=[SMEM, SMEM] + [HBM] * 4,
        out_specs=HBM,
        scratch_shapes=[
            pltpu.VMEM((DIM, LEAVES_DEV * LEAF), f32),
            pltpu.VMEM((RHS, LEAVES_DEV * LEAF), f32),
            pltpu.VMEM((DIM + RHS, NREACH * LEAF), f32),
            pltpu.VMEM((DIM + RHS, NREACH * LEAF), f32),
            pltpu.VMEM((RHS, LEAVES_DEV * LEAF), f32),
            pltpu.VMEM((65, 64, 128), bf16),
            pltpu.VMEM((4, 17, 128, 128), bf16),
            pltpu.SemaphoreType.DMA((6,)),
        ],
        compiler_params=pltpu.CompilerParams(vmem_limit_bytes=VMEM_LIMIT),
        cost_estimate=pl.CostEstimate(flops=10**10, bytes_accessed=2**22, transcendentals=0),
        name="near",
    )(*arguments)


def prepare_factors(anchors, factors, groups):
    def four_slabs(i, carry):
        side = source_side(anchors[:, pl.ds(pl.multiple_of(i * 512, 512), 512)])
        for m in range(4):
            slab = side[:, 128 * m : 128 * (m + 1)]
            turned = pltpu.roll(slab, RANK, 1)
            factors[(i * 4 + m) * 2] = halves(slab, turned).astype(bf16)
            factors[(i * 4 + m) * 2 + 1] = halves(turned, slab).astype(bf16)
        return carry

    lax.fori_loop(0, groups, four_slabs, 0, unroll=2)


def prepare_weights(moments, weights, groups):
    def four_slabs(i, carry):
        value = moments[:, pl.ds(pl.multiple_of(i * 512, 512), 512)]
        turns = weight_turns([value[:, 128 * m : 128 * (m + 1)] for m in range(4)])
        for turn in range(4):
            weights[turn, i, 0] = turns[turn][:RANK]
            weights[turn, i, 1] = turns[turn][RANK:]
        return carry

    lax.fori_loop(0, groups, four_slabs, 0, unroll=2)


def two_targets(anchors):
    front, back = target_sides(anchors)
    empty = jnp.zeros((RANK, 128), bf16)
    return rows(
        lanes(front[:RANK], empty),
        lanes(back[:RANK], empty),
        lanes(empty, front[RANK:]),
        lanes(empty, back[RANK:]),
    )


def four_sources(factors, located):
    return lanes(
        halves(factors[located[0]], factors[located[1]]),
        halves(factors[located[2]], factors[located[3]]),
    )


def placed(weights, index, slot):
    pair = index >> 1
    return weights[(slot - pair) & 3, pair >> 2, index & 1]


def two_clusters(anchors, factors, weights, located):
    sources = rows(*[four_sources(factors, located[4 * slot : 4 * slot + 4]) for slot in range(4)])
    weight = rows(
        *[pick([placed(weights, located[4 * slot + m], slot) for slot in range(4)]) for m in range(4)]
    )
    return cluster_sums(interact(two_targets(anchors), sources, weight))


def cluster_sums(total):
    total = total.T
    return lanes(
        total[:16] + total[16:32] + total[32:48] + total[48:64],
        total[64:80] + total[80:96] + total[96:112] + total[112:],
    )


def locate(entry, first, last, base, empty):
    inside = jnp.minimum(jnp.maximum(entry - first, 0), last)
    return jnp.where(entry < 0, empty, base + inside)


FINE_BASE = [0, 44, 72]
FINE_EMPTY = 92


def fine_kernel(
    device,
    lists,
    anchors_hbm,
    moments_hbm,
    inner_hbm,
    outer_hbm,
    far_hbm,
    anchors,
    moments,
    inner,
    outer,
    far,
    held_anchors,
    held_moments,
    factors,
    weights,
    semaphores,
):
    me = device[0]
    loads = started(
        semaphores,
        (anchors_hbm, anchors),
        (moments_hbm, moments),
        (inner_hbm, inner),
        (outer_hbm, outer),
    )
    for copy in loads:
        copy.wait()
    odd = (me & 1) == 1
    start = 0
    for height in range(3):
        width = (LEAVES_DEV >> height) * RANK
        wide = REACH * RANK
        rim = slice(RIM[height], RIM[height] + wide)
        own = slice(COLUMN[height], COLUMN[height] + width)
        far_end = start + wide + width
        for held, whole, row in (
            (held_anchors, anchors, slice(0, DIM)),
            (held_moments, moments, slice(DIM, 2 * DIM)),
        ):
            held[:, start + wide : far_end] = whole[:, own]
            inner_at = pl.multiple_of(jnp.where(odd, start, far_end), 128)
            outer_at = pl.multiple_of(jnp.where(odd, far_end, start), 128)
            held[:, pl.ds(inner_at, wide)] = inner[row, rim]
            held[:, pl.ds(outer_at, wide)] = outer[row, rim]
        start = far_end + wide
    held_anchors[:, start:] = jnp.zeros((DIM, 48 * 128 - start), f32)
    held_moments[:, start:] = jnp.zeros((DIM, 48 * 128 - start), f32)
    prepare_factors(held_anchors, factors, 12)
    prepare_weights(held_moments, weights, 12)

    for height in range(3):
        number = LEAVES_DEV >> height

        def one_pair(q, carry, height=height, number=number):
            first = me * number - REACH
            located = []
            for cluster in range(2):
                for j in range(8):
                    entry = lists[2 * LEAVES_DEV - 2 * number + 2 * q + cluster, j]
                    located.append(
                        locate(entry, first, number + 2 * REACH - 1, FINE_BASE[height], FINE_EMPTY)
                    )
            columns = pl.ds(pl.multiple_of(COLUMN[height] + q * 128, 128), 128)
            far[:, columns] = two_clusters(anchors[:, columns], factors, weights, located)
            return carry

        lax.fori_loop(0, number // 2, one_pair, 0, unroll=4)
    for copy in started(semaphores, (far, far_hbm)):
        copy.wait()


def fine_call(*arguments):
    return pl.pallas_call(
        fine_kernel,
        out_shape=jax.ShapeDtypeStruct((RHS, 56 * RANK), f32),
        in_specs=[SMEM, SMEM] + [HBM] * 4,
        out_specs=HBM,
        scratch_shapes=[
            pltpu.VMEM((DIM, 4096), f32),
            pltpu.VMEM((RHS, 4096), f32),
            pltpu.VMEM((32, RIM_WIDTH), f32),
            pltpu.VMEM((32, 2048), f32),
            pltpu.VMEM((RHS, 56 * RANK), f32),
            pltpu.VMEM((DIM, 48 * 128), f32),
            pltpu.VMEM((RHS, 48 * 128), f32),
            pltpu.VMEM((96, 64, 128), bf16),
            pltpu.VMEM((4, 12, 2, 64, 128), bf16),
            pltpu.SemaphoreType.DMA((4,)),
        ],
        compiler_params=pltpu.CompilerParams(vmem_limit_bytes=VMEM_LIMIT),
        cost_estimate=pl.CostEstimate(flops=5 * 10**9, bytes_accessed=2**22, transcendentals=0),
        name="fine",
    )(*arguments)


COARSE_EMPTY = 30


def coarse_kernel(
    device,
    lists,
    top_lists,
    tables_hbm,
    anchors_hbm,
    moments_hbm,
    inner_hbm,
    outer_hbm,
    beyond_hbm,
    third_hbm,
    top_hbm,
    incoming_hbm,
    matrices_hbm,
    far_hbm,
    basis_hbm,
    near_hbm,
    out_hbm,
    tables,
    anchors,
    moments,
    inner,
    outer,
    beyond,
    third,
    top_anchors,
    incoming,
    matrices,
    far,
    basis,
    near,
    out,
    held_anchors,
    held_moments,
    factors,
    weights,
    expansion,
    staged,
    formed,
    semaphores,
):
    me = device[0]
    loads = started(
        semaphores,
        (anchors_hbm, anchors),
        (moments_hbm, moments),
        (inner_hbm.at[:, 1152:], inner),
        (outer_hbm.at[:, 1152:], outer),
        (beyond_hbm, beyond),
        (third_hbm, third),
        (top_hbm, top_anchors),
        (tables_hbm.at[me], tables),
        (incoming_hbm, incoming),
        (matrices_hbm, matrices),
        (far_hbm, far),
        (basis_hbm, basis),
        (near_hbm, near),
    )
    for copy in loads[:6]:
        copy.wait()
    odd = (me & 1) == 1

    def at(column):
        return slice(column, column + 128)

    def place(on_inner, source, column, low_place, high_place):
        below = odd if on_inner else jnp.logical_not(odd)
        target = pl.multiple_of(jnp.where(below, low_place, high_place) * 128, 128)
        held_anchors[:, pl.ds(target, 128)] = source[:DIM, column]
        held_moments[:, pl.ds(target, 128)] = source[DIM:, column]

    def nearest(on_inner, column):
        below = odd if on_inner else jnp.logical_not(odd)
        return pl.ds(pl.multiple_of(column + jnp.where(below, 128, 0), 128), 128)

    for on_inner, source in ((True, inner), (False, outer)):
        place(on_inner, source, at(0), 1, 5)
        place(on_inner, source, at(128), 2, 6)
        place(on_inner, source, at(256), 10, 12)
    place(False, outer, nearest(False, 512), 0, 7)
    place(False, outer, at(768), 9, 13)
    place(False, third, at(0), 8, 14)
    place(True, beyond, nearest(True, 0), 0, 7)
    place(True, beyond, at(256), 9, 13)
    place(True, beyond, at(768), 8, 14)
    for index, column in ((3, 3584), (4, 3712), (11, 3840)):
        held_anchors[:, at(128 * index)] = anchors[:, at(column)]
        held_moments[:, at(128 * index)] = moments[:, at(column)]
    held_anchors[:, at(128 * 15)] = jnp.zeros((DIM, 128), f32)
    held_moments[:, at(128 * 15)] = jnp.zeros((RHS, 128), f32)
    prepare_factors(held_anchors, factors, 4)
    prepare_weights(held_moments, weights, 4)

    def local_pair(height, q, base):
        number = LEAVES_DEV >> height
        located = []
        for cluster in range(2):
            for j in range(8):
                entry = lists[2 * LEAVES_DEV - 2 * number + 2 * q + cluster, j]
                located.append(
                    locate(entry, me * number - REACH, number + 2 * REACH - 1, base, COARSE_EMPTY)
                )
        return two_clusters(
            anchors[:, at(COLUMN[height] + 128 * q)], factors, weights, located
        )

    far_third = [local_pair(3, q, 0) for q in range(2)]
    far_fourth = local_pair(4, 0, 16)

    loads[8].wait()
    loads[9].wait()
    loads[7].wait()

    lane = lax.broadcasted_iota(jnp.int32, (8, 128), 1)

    def two_blocks(first, second):
        return rows(
            jnp.where(lane < RANK, first, pltpu.roll(second, RANK, 1)),
            jnp.where(lane < RANK, pltpu.roll(first, RANK, 1), second),
        )

    sixth = [
        jnp.sum(incoming[64 * c : 64 * (c + 1), 8 * (SLOTS - 1) : 8 * SLOTS, :], axis=0)
        for c in range(2)
    ]
    seventh = lifted(two_blocks(*sixth), matrices[RANK * (LOCAL + 7) : RANK * (LOCAL + 9), :])
    seventh = as_block(seventh)

    def held(kind, other):
        slot = tables[SENT // 128 + kind, other]
        return slot, incoming[other, pl.ds(pl.multiple_of((slot & 3) * 8, 8), 8), :]

    for index, shift in enumerate(FORMED):
        other = jnp.minimum(jnp.maximum(me + shift, 0), DEVICES - 1)
        value = two_blocks(held(1, other)[1], jnp.zeros((8, 128), f32))[:, :RANK]
        start = RANK * (LOCAL + 9 + index)
        formed[index] = as_block(lifted(value, matrices[start : start + RANK, :]))

    entries = [[lists[62, j] for j in range(8)]]
    for level in range(1, TOP + 1):
        row = DEVICES - (DEVICES >> (level - 1)) + (me >> level)
        entries.append([top_lists[row, j] for j in range(8)])

    def block(level, entry):
        if level == TOP:
            return jnp.where(entry == 0, seventh, 0.0)
        if level == SHARED:
            return jnp.where(entry == 0, sixth[0], jnp.where(entry == 1, sixth[1], 0.0))
        first = jnp.maximum(entry, 0) << level

        def add(i, total):
            slot, value = held(level, first + i)
            if level == 2:
                value = jnp.where(slot < SLOTS, value, formed[slot & 3])
            return total + value

        count = jnp.where(entry < 0, 0, 1 << level)
        return lax.fori_loop(0, count, add, jnp.zeros((8, 128), f32))

    wanted = [0] + [DEVICES - (DEVICES >> (level - 1)) + (me >> level) for level in range(1, TOP + 1)]
    for level in range(1, TOP + 1):
        first = DEVICES - (DEVICES >> (level - 1))
        wanted += [first + jnp.maximum(entry, 0) for entry in entries[level]]
    columns = []
    loads[6].wait()
    for group in range(8):
        part = wanted[8 * group : 8 * group + 8]
        regrouped(lambda c: top_anchors[pl.ds(part[c], 1), :], staged.at[group % 2], 8, 8)
        columns += eight_anchors([tile(staged.at[group % 2], c, 8) for c in range(8)])

    far_chain = []
    for unit in range(4):
        pairs = []
        for level in (2 * unit, 2 * unit + 1):
            sums = [block(level, entry) for entry in entries[level]]
            pairs += [two_blocks(sums[2 * j], sums[2 * j + 1]) for j in range(4)]
        weight = []
        for h in range(2):
            parts = []
            for slot in range(4):
                high = pairs[2 * slot + h].astype(bf16).astype(f32)
                parts += [high, pairs[2 * slot + h] - high]
            weight.append(rows(*parts).T.astype(bf16))
        own = columns[unit]
        sources = []
        for level in (2 * unit, 2 * unit + 1):
            for h in range(2):
                if level == 0:
                    found = [
                        held(SHARED, jnp.maximum(entry, 0))[1] for entry in entries[0][4 * h : 4 * h + 4]
                    ]
                    pair = lanes(two_blocks(found[0], found[1]), two_blocks(found[2], found[3]))
                else:
                    pair = lanes(*columns[4 * level + 2 * h : 4 * level + 2 * h + 2])
                sources.append(source_side(pair).astype(bf16))
        if unit == 0:
            own = halves(anchors[:, at(COLUMN[5])], own)
        result = cluster_sums(interact(two_targets(own), rows(*sources), rows(*weight)))
        far_chain += [result[:, :RANK], result[:, RANK:]]

    def pushed(value, matrix):
        high, low = split(matrix)
        return folded(dot_nt(narrow(value), lanes(high, low)))

    value = far_chain[TOP]
    for level in range(TOP - 1, -1, -1):
        value = far_chain[level] + pushed(value, matrices[RANK * (LOCAL + level) : RANK * (LOCAL + level + 1), :])

    def children(parent, height, q):
        start = (ROW[height] + 2 * q) * RANK
        return pushed(parent, matrices[start : start + 128, :])

    loads[10].wait()
    upper = [far_fourth + children(value, 4, 0)]
    for height in (3, 2, 1, 0):
        lower = []
        for q, slab in enumerate(upper):
            for side in range(2):
                parent = slab[:, RANK * side : RANK * (side + 1)]
                index = 2 * q + side
                if height == 3:
                    own = far_third[index]
                else:
                    own = far[:, at(COLUMN[height] + 128 * index)]
                lower.append(own + children(parent, height, index))
        upper = lower
    for q, slab in enumerate(upper):
        expansion[:, at(128 * q)] = slab

    def two_leaves(q, carry):
        slab = expansion[:, pl.ds(pl.multiple_of(q * 128, 128), 128)]
        for leaf in range(2):
            columns = pl.ds(pl.multiple_of(q * 256 + leaf * 128, 128), 128)
            high, low = split(basis[:, columns])
            own = slab[:, RANK * leaf : RANK * (leaf + 1)]
            out[:, columns] = near[:, columns] + folded(dot(narrow(own), rows(high, low)))
        return carry

    loads[11].wait()
    loads[12].wait()
    stores = []
    for part in range(2):
        lax.fori_loop(8 * part, 8 * part + 8, two_leaves, 0, unroll=8)
        own = slice(2048 * part, 2048 * part + 2048)
        stores += started(semaphores.at[13 + part :], (out.at[:, own], out_hbm.at[:, own]))
    for copy in stores:
        copy.wait()


def coarse_call(*arguments):
    return pl.pallas_call(
        coarse_kernel,
        out_shape=jax.ShapeDtypeStruct((RHS, LEAVES_DEV * LEAF), f32),
        in_specs=[SMEM] * 3 + [HBM] * 13,
        out_specs=HBM,
        scratch_shapes=[
            pltpu.SMEM((TABLE, 128), jnp.int32),
            pltpu.VMEM((DIM, 4096), f32),
            pltpu.VMEM((RHS, 4096), f32),
            pltpu.VMEM((32, 512), f32),
            pltpu.VMEM((32, 896), f32),
            pltpu.VMEM((32, 896), f32),
            pltpu.VMEM((32, 128), f32),
            pltpu.VMEM((127, RANK * DIM), f32),
            pltpu.VMEM((DEVICES, 8 * SLOTS, 128), f32),
            pltpu.VMEM((MATRICES * RANK, RANK), f32),
            pltpu.VMEM((RHS, 56 * RANK), f32),
            pltpu.VMEM((RANK, 4096), f32),
            pltpu.VMEM((RHS, 4096), f32),
            pltpu.VMEM((RHS, 4096), f32),
            pltpu.VMEM((DIM, 16 * 128), f32),
            pltpu.VMEM((RHS, 16 * 128), f32),
            pltpu.VMEM((32, 64, 128), bf16),
            pltpu.VMEM((4, 4, 2, 64, 128), bf16),
            pltpu.VMEM((RHS, 2048), f32),
            pltpu.VMEM((2, 64, 128), f32),
            pltpu.VMEM((4, 8, 128), f32),
            pltpu.SemaphoreType.DMA((15,)),
        ],
        compiler_params=pltpu.CompilerParams(vmem_limit_bytes=VMEM_LIMIT),
        cost_estimate=pl.CostEstimate(flops=10**9, bytes_accessed=2**23, transcendentals=0),
        name="coarse",
    )(*arguments)


def exchanged(value, mate):
    pairs = []
    for device in range(DEVICES):
        other = mate(device)
        pairs.append((device, other if 0 <= other < DEVICES else device))
    return lax.ppermute(value, "leaf", pairs)


def inner_mate(device):
    return device + 1 if device % 2 == 0 else device - 1


def outer_mate(device):
    return device - 1 if device % 2 == 0 else device + 1


def third_mate(device):
    return device - 3 if device % 2 == 0 else device + 3


def on_device(
    points,
    charges,
    leaf_basis,
    local_transfer,
    local_anchors,
    local_lists,
    near_blocks,
    top_transfer,
    top_anchors,
    top_lists,
):
    index = lax.axis_index("leaf")
    device = index.reshape(1)
    half = NREACH * LEAF
    lower = (index & 1) * half

    def edge(start):
        return jnp.concatenate(
            [lax.dynamic_slice_in_dim(array, start, half, 1) for array in (points, charges)], axis=0
        )

    inner_edge, outer_edge, device = lax.optimization_barrier(
        (edge(half - lower), edge(lower), device)
    )
    inner_leaves = exchanged(inner_edge, inner_mate)
    outer_leaves = exchanged(outer_edge, outer_mate)

    tables = jnp.asarray(slot_tables())
    moments, anchors, inner_rim, outer_rim, third, outgoing, matrices = moments_call(
        device, tables, leaf_basis, charges, local_transfer, local_anchors, top_transfer
    )
    outgoing, inner_leaves, outer_leaves = lax.optimization_barrier(
        (outgoing, inner_leaves, outer_leaves)
    )
    inner = exchanged(inner_rim, inner_mate)
    incoming = lax.all_to_all(outgoing, "leaf", 0, 0)
    outer = exchanged(
        jnp.concatenate([outer_rim, inner[:, RIM[3] : RIM[5]]], axis=1), outer_mate
    )
    third = exchanged(third, third_mate)
    near = near_call(device, near_blocks, points, charges, inner_leaves, outer_leaves)
    near, outer = lax.optimization_barrier((near, outer))
    beyond = exchanged(outer[:, RIM[3] :], inner_mate)
    far = fine_call(device, local_lists, anchors, moments, inner, outer)
    return coarse_call(
        device,
        local_lists,
        top_lists,
        tables,
        anchors,
        moments,
        inner,
        outer,
        beyond,
        third,
        top_anchors,
        incoming,
        matrices,
        far,
        leaf_basis,
        near,
    )


def solution(mesh):
    in_specs = (
        P(None, "leaf"),
        P(None, "leaf"),
        P(None, "leaf"),
        P("leaf", None),
        P("leaf", None),
        P("leaf", None),
        P("leaf", None),
        P(),
        P(),
        P(),
    )
    out_specs = P(None, "leaf")
    return jax.shard_map(
        on_device, mesh=mesh, in_specs=in_specs, out_specs=out_specs, check_vma=False
    )
```

time: 119 us -> 86.6 us (0.73)
  the two profiles are of different devices: /device:TPU:0 before, /device:TPU:32 now
where the time goes in v2:
time: 86.6 us; the launch traced here: 85.3 us
  Pallas kernels  54.1 us (62%)
  starting transfers between devices  24.3 us (28%)
  local copies, waits for them, and re-layouts  5.06 us (6%)
  waiting for transfers between devices  1.34 us (2%)
    ppermute x6, starting transfers between devices, exchanged(): return lax.ppermute(value, 'leaf', pairs)  18 us
    pallas_call x1, Pallas kernels, near_call(): pl.pallas_call(near_kernel, out_shape=jax.ShapeDtypeStruct((RHS, LEAVES_D...  16.3 us
    pallas_call x1, Pallas kernels, coarse_call(): pl.pallas_call(coarse_kernel, out_shape=jax.ShapeDtypeStruct((RHS, LEAVES...  14.7 us
    pallas_call x1, Pallas kernels, fine_call(): pl.pallas_call(fine_kernel, out_shape=jax.ShapeDtypeStruct((RHS, 56 * RAN...  13.7 us
    pallas_call x1, Pallas kernels, moments_call(): pl.pallas_call(moments_kernel, out_shape=(shape((16, 4096), f32), shape((...  9.48 us
    all_to_all x1, starting transfers between devices, on_device(): incoming = lax.all_to_all(outgoing, 'leaf', 0, 0)  6.32 us
    unnamed x29, local copies, waits for them, and re-layouts  3.91 us
  transfers between devices with their start and end apart: 7, of which 1 were waited for; matrix products, arithmetic and copies ran while one was open for 2% of the time, Pallas kernels for 46%

profile of v2, /device:TPU:32, one launch (start us, length us, event | category | flops | bytes accessed | tf_op | source)
XLA Modules:
  0.0 85.3 jit_solution(5511740084941092560)
XLA Ops:
  0.0 1.1 %constant_dynamic-slice_fusion = (f32[16,2048]{1,0:T(8,128)S(1)}, f32[16,2048]{1,0:T(8,128)S(1)}, f32[16,2048]{1,0:T(8,128)S(1)}, f32[16,2048]{1,0:T(8,128)S(1)}) fusion(f32[16,4096]{1,0:T(8,128)} %charges_hbm.3, s32[]{:T(128)S(6)} %select_n.9, s32[]{:T(128)S(6)} %select_n.8, f32[16,4096]{1,0:T(8,128)} %points_hbm.1), kind=kLoop, calls=%fused_computation.3 | loop fusion | bytes 1048584 | tf_op jit(solution)/shard_map/dynamic_slice | solution.py:1043
  1.2 0.1 collective-permute-start.1
  1.3 6.8 %collective-permute-start.2 = (f32[32,2048]{1,0:T(8,128)S(1)}, f32[32,2048]{1,0:T(8,128)S(1)}, u32[]{:S(2)}, u32[]{:S(2)}) collective-permute-start(f32[32,2048]{1,0:T(8,128)S(1)} %pad_maximum_fusion.1), channel_id=1, source_target_pairs={{0,0},{1,2},{2,1},{3,4},{4,3},{5,6},{6,5},{7,8},{8,7},{9,10},{10,9... | collective-permute-start | bytes 786440 | tf_op jit(solution)/shard_map/ppermute | solution.py:1009
  8.0 9.5 %moments.1 = (f32[16,4096]{1,0:T(8,128)}, f32[16,4096]{1,0:T(8,128)}, f32[32,1664]{1,0:T(8,128)}, f32[32,1664]{1,0:T(8,128)}, f32[32,128]{1,0:T(8,128)}, /*index=5*/f32[128,32,128]{2,1,0:T(8,128)}, f32[4800,64]{1,0:T(8,128)}) custom-call(s32[1]{0:T(128)} %bitcast.device, s32[128,11,128]{2,1,0:T(8,128)} %constant.16.clone.tables_hbm, f32[64,4096]{1,0:T(8,128)} %basis_hbm.3, ...), custom_call_target="tpu_custom_call" | custom-call | flops 1000000000 | bytes 4194304 | tf_op jit(solution)/shard_map/moments/pallas_call | solution.py:399
  17.5 0.0 copy-start.11
  17.5 0.0 copy-start.12
  17.5 0.0 copy-start.6
  17.6 0.0 copy-start.7
  17.6 0.0 copy-start.8
  17.6 0.0 collective-permute-done.1.inner_hbm
  17.6 0.0 copy-start.9
  17.6 0.0 collective-permute-done.2.outer_hbm
  17.6 6.3 %all-to-all-start = ((f32[128,32,128]{2,1,0:T(8,128)}), f32[128,32,128]{2,1,0:T(8,128)S(1)}, u32[]{:S(2)}, u32[]{:S(2)}) async-start(f32[128,32,128]{2,1,0:T(8,128)} %get-tuple-element.32), calls=%async_computation | async-start | bytes 4194304 | tf_op jit(solution)/shard_map/all_to_all | solution.py:1060
  24.0 0.2 collective-permute-start
  24.2 6.9 %collective-permute-start.5 = (f32[32,128]{1,0:T(8,128)S(1)}, f32[32,128]{1,0:T(8,128)S(1)}, u32[]{:S(2)}, u32[]{:S(2)}) collective-permute-start(f32[32,128]{1,0:T(8,128)S(1)} %copy-done.12), channel_id=1, source_target_pairs={{0,0},{1,4},{2,2},{3,6},{4,1},{5,8},{6,3},{7,10},{8,5},{9,12},{10,... | collective-permute-start | bytes 49160 | tf_op jit(solution)/shard_map/ppermute | solution.py:1009
  31.1 0.7 copy.12.near_blocks
  31.8 0.7 copy.14.lists
  32.5 0.7 copy.15.top_lists
  33.2 0.0 collective-permute-done.inner_hbm
  33.3 3.8 %collective-permute-start.3 = (f32[32,2048]{1,0:T(8,128)S(1)}, f32[32,2048]{1,0:T(8,128)S(1)}, u32[]{:S(2)}, u32[]{:S(2)}) collective-permute-start(f32[32,2048]{1,0:T(8,128)S(1)} %pad_maximum_fusion.2), channel_id=1, source_target_pairs={{0,0},{1,2},{2,1},{3,4},{4,3},{5,6},{6,5},{7,8},{8,7},{9,10},{10,9... | collective-permute-start | bytes 786440 | tf_op jit(solution)/shard_map/ppermute | solution.py:1009
  37.1 16.3 %near.1.near_hbm = f32[16,4096]{1,0:T(8,128)} custom-call(s32[1]{0:T(128)} %bitcast.device, s32[32,8]{1,0:T(8,128)} %copy.12.near_blocks, f32[16,4096]{1,0:T(8,128)} %points_hbm.1, f32[16,4096]{1,0:T(8,128)} %charges_hbm.3, f32[32,2048]{1,0:T(8,128)} %copy-done.9, f32[32,2048]{1,0:T(8,128)} %copy-done.10), custom_call_target="tpu_custom_call" | custom-call | flops 10000000000 | bytes 4194304 | tf_op jit(solution)/shard_map/near/pallas_call | solution.py:525
  53.4 1.3 %collective-permute-done.3.outer_hbm = f32[32,2048]{1,0:T(8,128)S(1)} collective-permute-done((f32[32,2048]{1,0:T(8,128)S(1)}, f32[32,2048]{1,0:T(8,128)S(1)}, u32[]{:S(2)}, u32[]{:S(2)}) %collective-permute-start.3) | collective-permute-done | bytes 262176 | tf_op jit(solution)/shard_map/ppermute | solution.py:1009
  54.7 0.3 collective-permute-start.4
  55.0 0.4 copy-done.1
  55.4 13.7 %fine.1.far_hbm = f32[16,3584]{1,0:T(8,128)} custom-call(s32[1]{0:T(128)} %bitcast.device, s32[63,8]{1,0:T(8,128)} %copy.14.lists, f32[16,4096]{1,0:T(8,128)} %get-tuple-element.21.anchors_hbm, f32[16,4096]{1,0:T(8,128)} %get-tuple-element.22.moments_hbm, f32[32,1664]{1,0:T(8,128)} %copy-done.2, f32[32,2048]{1,0:T(8,128)} %copy-done.1), custom_call_target="tpu_custom_call" | custom-call | flops 5000000000 | bytes 4194304 | tf_op jit(solution)/shard_map/fine/pallas_call | solution.py:693
  69.1 0.0 collective-permute-done.5.third_hbm
  69.1 0.0 collective-permute-done.4.beyond_hbm
  69.2 0.0 all-to-all-done.incoming_hbm
  69.2 0.5 copy-done.5
  69.7 0.1 copy-done.4
  69.8 0.7 copy-done
  70.5 14.7 %coarse.1 = f32[16,4096]{1,0:T(8,128)} custom-call(s32[1]{0:T(128)} %bitcast.device, s32[63,8]{1,0:T(8,128)} %copy.14.lists, s32[127,8]{1,0:T(8,128)} %copy.15.top_lists, s32[128,11,128]{2,1,0:T(8,128)} %constant.16.clone.tables_hbm, f32[16,4096]{1,0:T(8,128)} %get-tuple-element.21.anchors_hbm, f32[16,4096]{1,0:T(8,128)} %get-tuple-element.22.moments_hbm, ...), custom_call_target="tpu_custom_call" | custom-call | flops 1000000000 | bytes 8388608 | tf_op jit(solution)/shard_map/coarse/pallas_call | solution.py:969
  (21 shorter events, 0.1 us)
Async XLA Ops:
  1.2 16.4 %collective-permute-start.1 = (f32[32,2048]{1,0:T(8,128)S(1)}, f32[32,2048]{1,0:T(8,128)S(1)}, u32[]{:S(2)}, u32[]{:S(2)}) collective-permute-start(f32[32,2048]{1,0:T(8,128)S(1)} %pad_maximum_fusion), channel_id=1, source_target_pairs={{0,1},{1,0},{2,3},{3,2},{4,5},{5,4},{6,7},{7,6},{8,9},{9,8},{10,11... | collective-permute-start | bytes 786440 | tf_op jit(solution)/shard_map/ppermute | solution.py:1009
  1.3 16.3 %collective-permute-start.2 = (f32[32,2048]{1,0:T(8,128)S(1)}, f32[32,2048]{1,0:T(8,128)S(1)}, u32[]{:S(2)}, u32[]{:S(2)}) collective-permute-start(f32[32,2048]{1,0:T(8,128)S(1)} %pad_maximum_fusion.1), channel_id=1, source_target_pairs={{0,0},{1,2},{2,1},{3,4},{4,3},{5,6},{6,5},{7,8},{8,7},{9,10},{10,9... | collective-permute-start | bytes 786440 | tf_op jit(solution)/shard_map/ppermute | solution.py:1009
  17.5 6.4 %copy-start.11 = (f32[32,1664]{1,0:T(8,128)S(1)}, f32[32,1664]{1,0:T(8,128)}, u32[]{:S(2)}) copy-start(f32[32,1664]{1,0:T(8,128)} %get-tuple-element.23) | copy-start | bytes 638980
  17.5 6.7 %copy-start.12 = (f32[32,128]{1,0:T(8,128)S(1)}, f32[32,128]{1,0:T(8,128)}, u32[]{:S(2)}) copy-start(f32[32,128]{1,0:T(8,128)} %get-tuple-element.31) | copy-start | bytes 49156
  17.5 13.6 %copy-start.6 = (s32[32,8]{0,1:T(8,128)S(1)}, s32[32,8]{0,1:T(8,128)}, u32[]{:S(2)}) copy-start(s32[32,8]{0,1:T(8,128)} %param.17) | copy-start | bytes 3076
  17.6 14.3 %copy-start.7 = (s32[63,8]{0,1:T(8,128)S(1)}, s32[63,8]{0,1:T(8,128)}, u32[]{:S(2)}) copy-start(s32[63,8]{0,1:T(8,128)} %param.16) | copy-start | bytes 6052
  17.6 14.9 %copy-start.8 = (s32[127,8]{0,1:T(8,128)S(1)}, s32[127,8]{0,1:T(8,128)}, u32[]{:S(2)}) copy-start(s32[127,8]{0,1:T(8,128)} %param.20) | copy-start | bytes 12196
  17.6 15.7 %copy-start.3 = (f32[32,1664]{1,0:T(8,128)S(1)}, f32[32,1664]{1,0:T(8,128)}, u32[]{:S(2)}) copy-start(f32[32,1664]{1,0:T(8,128)} %get-tuple-element.29) | copy-start | bytes 638980
  17.6 15.7 %copy-start.9 = (f32[32,2048]{1,0:T(8,128)}, f32[32,2048]{1,0:T(8,128)S(1)}, u32[]{:S(2)}) copy-start(f32[32,2048]{1,0:T(8,128)S(1)} %collective-permute-done.1.inner_hbm) | copy-start | bytes 786436
  17.6 15.7 %copy-start.10 = (f32[32,2048]{1,0:T(8,128)}, f32[32,2048]{1,0:T(8,128)S(1)}, u32[]{:S(2)}) copy-start(f32[32,2048]{1,0:T(8,128)S(1)} %collective-permute-done.2.outer_hbm) | copy-start | bytes 786436
  17.6 51.5 %all-to-all-start = ((f32[128,32,128]{2,1,0:T(8,128)}), f32[128,32,128]{2,1,0:T(8,128)S(1)}, u32[]{:S(2)}, u32[]{:S(2)}) async-start(f32[128,32,128]{2,1,0:T(8,128)} %get-tuple-element.32), calls=%async_computation | async-start | bytes 4194304 | tf_op jit(solution)/shard_map/all_to_all | solution.py:1060
  24.0 9.3 %collective-permute-start = (f32[32,1664]{1,0:T(8,128)S(1)}, f32[32,1664]{1,0:T(8,128)S(1)}, u32[]{:S(2)}, u32[]{:S(2)}) collective-permute-start(f32[32,1664]{1,0:T(8,128)S(1)} %copy-done.11), channel_id=1, source_target_pairs={{0,1},{1,0},{2,3},{3,2},{4,5},{5,4},{6,7},{7,6},{8,9},{9,8},{10,11... | collective-permute-start | bytes 638984 | tf_op jit(solution)/shard_map/ppermute | solution.py:1009
  24.2 44.9 %collective-permute-start.5 = (f32[32,128]{1,0:T(8,128)S(1)}, f32[32,128]{1,0:T(8,128)S(1)}, u32[]{:S(2)}, u32[]{:S(2)}) collective-permute-start(f32[32,128]{1,0:T(8,128)S(1)} %copy-done.12), channel_id=1, source_target_pairs={{0,0},{1,4},{2,2},{3,6},{4,1},{5,8},{6,3},{7,10},{8,5},{9,12},{10,... | collective-permute-start | bytes 49160 | tf_op jit(solution)/shard_map/ppermute | solution.py:1009
  33.2 20.1 %copy-start.2 = (f32[32,1664]{1,0:T(8,128)}, f32[32,1664]{1,0:T(8,128)S(1)}, u32[]{:S(2)}) copy-start(f32[32,1664]{1,0:T(8,128)S(1)} %collective-permute-done.inner_hbm) | copy-start | bytes 638980
  33.3 21.4 %collective-permute-start.3 = (f32[32,2048]{1,0:T(8,128)S(1)}, f32[32,2048]{1,0:T(8,128)S(1)}, u32[]{:S(2)}, u32[]{:S(2)}) collective-permute-start(f32[32,2048]{1,0:T(8,128)S(1)} %pad_maximum_fusion.2), channel_id=1, source_target_pairs={{0,0},{1,2},{2,1},{3,4},{4,3},{5,6},{6,5},{7,8},{8,7},{9,10},{10,9... | collective-permute-start | bytes 786440 | tf_op jit(solution)/shard_map/ppermute | solution.py:1009
  54.7 0.7 copy-start.1
  54.7 14.4 %collective-permute-start.4 = (f32[32,896]{1,0:T(8,128)S(1)}, f32[32,896]{1,0:T(8,128)S(1)}, u32[]{:S(2)}, u32[]{:S(2)}) collective-permute-start(f32[32,896]{1,0:T(8,128)S(1)} %slice.7), channel_id=1, source_target_pairs={{0,1},{1,0},{2,3},{3,2},{4,5},{5,4},{6,7},{7,6},{8,9},{9,8},{10,11... | collective-permute-start | bytes 344072 | tf_op jit(solution)/shard_map/ppermute | solution.py:1009
  69.1 0.6 copy-start.5
  69.1 0.7 copy-start.4
  69.2 1.3 %copy-start = (f32[128,32,128]{2,1,0:T(8,128)}, f32[128,32,128]{2,1,0:T(8,128)S(1)}, u32[]{:S(2)}) copy-start(f32[128,32,128]{2,1,0:T(8,128)S(1)} %all-to-all-done.incoming_hbm) | copy-start | bytes 6291460

commit v3 on v2

--- a/solution.py
+++ b/solution.py
@@ -18,7 +18,8 @@
 DEVICES = 128
 TOP = 7
 SHARED = 6
-SLOTS = 4
+SLOTS = 3
+SUMMIT_ROW = 124
 NOTHING = 7
 ANCHORS = 8
 FORMED = (-6, -5, 5, 6)
@@ -48,7 +49,7 @@
 
 
 def slot_tables():
-    sent = np.full((DEVICES, DEVICES, SLOTS), NOTHING, np.int32)
+    sent = np.full((DEVICES, SLOTS, DEVICES), NOTHING, np.int32)
     held = np.zeros((DEVICES, SHARED + 1, DEVICES), np.int32)
     for first in range(DEVICES):
         for second in range(DEVICES):
@@ -56,18 +57,15 @@
             if levels and levels[0] == 0:
                 if len(levels) == 3:
                     levels.pop()
-                    held[first, 2, second] = SLOTS + FORMED.index(second - first)
+                    held[first, 2, second] = 4 + FORMED.index(second - first)
                 levels.append(ANCHORS)
             for slot, level in enumerate(levels):
-                sent[first, second, slot] = level
+                sent[first, slot, second] = level
                 held[first, SHARED if level == ANCHORS else level, second] = slot
-            sent[first, second, SLOTS - 1] = SHARED
-    tables = np.concatenate([sent.reshape(DEVICES, -1), held.reshape(DEVICES, -1)], axis=1)
-    return tables.reshape(DEVICES, -1, 128)
-
-
-SENT = DEVICES * SLOTS
-TABLE = (SENT + (SHARED + 1) * DEVICES) // 128
+    return np.concatenate([sent, held], axis=1)
+
+
+TABLE = SLOTS + SHARED + 1
 
 
 def started(semaphores, *pairs):
@@ -249,6 +247,7 @@
     inner_out,
     outer_out,
     third,
+    summit,
     outgoing_out,
     matrices_out,
     tables,
@@ -275,9 +274,20 @@
         (charges_hbm, charges),
         *[(basis_hbm.at[:, part], basis.at[:, part]) for part in quarters],
         (transfer_hbm, transfer),
-        (top_hbm, top_transfer),
         (anchors_hbm, anchor_rows),
         (tables_hbm.at[me], tables),
+    )
+    chain = [2 * DEVICES - (2 * DEVICES >> level) + (me >> level) for level in range(TOP)]
+    chain += [252, 253]
+    for shift in FORMED:
+        other = jnp.minimum(jnp.maximum(me + shift, 0), DEVICES - 1)
+        chain.append(DEVICES + (other >> 1))
+    chain_loads = started(
+        semaphores.at[18:],
+        *[
+            (top_hbm.at[pl.ds(row, 1), :], top_transfer.at[pl.ds(index, 1), :])
+            for index, row in enumerate(chain)
+        ],
     )
     loads[0].wait()
 
@@ -303,20 +313,19 @@
             ]
         for c in range(count):
             store_matrix(staged.at[group % 2], c, matrices, 8 * group + c)
-    loads[6].wait()
-    chain = [2 * DEVICES - (2 * DEVICES >> level) + (me >> level) for level in range(TOP)]
-    chain += [252, 253]
-    for shift in FORMED:
-        other = jnp.minimum(jnp.maximum(me + shift, 0), DEVICES - 1)
-        chain.append(DEVICES + (other >> 1))
+    for copy in chain_loads:
+        copy.wait()
     for group in range(2):
-        part = chain[8 * group : 8 * group + 8]
-        regrouped(lambda c: top_transfer[pl.ds(part[c], 1), :], staged.at[group], len(part), 32)
-        for c in range(len(part)):
+        count = min(8, 13 - 8 * group)
+        for i in range(32):
+            staged[group, 8 * i : 8 * i + count, :] = top_transfer[
+                8 * group : 8 * group + count, 128 * i : 128 * (i + 1)
+            ]
+        for c in range(count):
             store_matrix(staged.at[group], c, matrices, LOCAL + 8 * group + c)
     stores = started(semaphores.at[9:], (matrices, matrices_out))
 
-    loads[7].wait()
+    loads[6].wait()
     for group in range(8):
         count = min(8, 63 - 8 * group)
         for i in range(8):
@@ -376,16 +385,16 @@
             start = RANK * (LOCAL + level)
             value = lifted(value, matrices[start : start + RANK, :])
     blocks[NOTHING] = jnp.zeros((8, 128), f32)
+    for half in range(2):
+        summit[half] = jnp.where(me >> SHARED == half, blocks[SHARED], 0.0)
     blocks[ANCHORS] = as_block(anchors[:, COLUMN[5] : COLUMN[5] + RANK])
 
     def one_device(other, carry):
-        for slot in range(SLOTS - 1):
-            kind = tables[other // 32, (other % 32) * SLOTS + slot]
-            outgoing[other, 8 * slot : 8 * (slot + 1), :] = blocks[kind]
-        outgoing[other, 8 * (SLOTS - 1) : 8 * SLOTS, :] = blocks[SHARED]
+        for slot in range(SLOTS):
+            outgoing[other, 8 * slot : 8 * (slot + 1), :] = blocks[tables[slot, other]]
         return carry
 
-    loads[8].wait()
+    loads[7].wait()
     for part in range(4):
         lax.fori_loop(32 * part, 32 * part + 32, one_device, 0, unroll=8)
         own = slice(32 * part, 32 * part + 32)
@@ -404,18 +413,19 @@
             shape((32, RIM_WIDTH), f32),
             shape((32, RIM_WIDTH), f32),
             shape((32, 128), f32),
+            shape((2, 8, 128), f32),
             shape((DEVICES, 8 * SLOTS, 128), f32),
             shape((MATRICES * RANK, RANK), f32),
         ),
         in_specs=[SMEM] + [HBM] * 6,
-        out_specs=(HBM, HBM, HBM, HBM, VMEM, HBM, HBM),
+        out_specs=(HBM, HBM, HBM, HBM, VMEM, VMEM, HBM, HBM),
         scratch_shapes=[
             pltpu.SMEM((TABLE, 128), jnp.int32),
             pltpu.VMEM((RANK, 4096), f32),
             pltpu.VMEM((RHS, 4096), f32),
             pltpu.VMEM((LOCAL, RANK * RANK), f32),
             pltpu.VMEM((63, RANK * DIM), f32),
-            pltpu.VMEM((254, RANK * RANK), f32),
+            pltpu.VMEM((16, RANK * RANK), f32),
             pltpu.VMEM((RHS, 4096), f32),
             pltpu.VMEM((DIM, 4096), f32),
             pltpu.VMEM((32, RIM_WIDTH), f32),
@@ -425,7 +435,7 @@
             pltpu.VMEM((9, 8, 128), f32),
             pltpu.VMEM((2, 256, 128), f32),
             pltpu.VMEM((2, 64, 128), f32),
-            pltpu.SemaphoreType.DMA((18,)),
+            pltpu.SemaphoreType.DMA((31,)),
         ],
         compiler_params=pltpu.CompilerParams(vmem_limit_bytes=VMEM_LIMIT),
         cost_estimate=pl.CostEstimate(flops=10**9, bytes_accessed=2**22, transcendentals=0),
@@ -476,12 +486,12 @@
 
     loads[0].wait()
     loads[1].wait()
-    lax.fori_loop(0, 8, prepare(points, charges, 0, 4), 0, unroll=2)
+    lax.fori_loop(0, 8, prepare(points, charges, 0, 4), 0, unroll=8)
     side = (me & 1) * 12
     loads[2].wait()
-    lax.fori_loop(0, 4, prepare(inner, inner, DIM, 12 - side), 0, unroll=2)
+    lax.fori_loop(0, 4, prepare(inner, inner, DIM, 12 - side), 0, unroll=4)
     loads[3].wait()
-    lax.fori_loop(0, 4, prepare(outer, outer, DIM, side), 0, unroll=2)
+    lax.fori_loop(0, 4, prepare(outer, outer, DIM, side), 0, unroll=4)
     factors[64] = jnp.zeros((64, 128), bf16)
     for turn in range(4):
         weights[turn, 16] = jnp.zeros((128, 128), bf16)
@@ -496,7 +506,7 @@
         )
         located = []
         for j in range(8):
-            block = near_blocks[t, j]
+            block = near_blocks[j, t]
             inside = jnp.minimum(jnp.maximum(block - first_leaf, 0), 63)
             located.append(jnp.where(block < 0, 64, inside))
         sources = rows(
@@ -514,7 +524,7 @@
 
     stores = []
     for part in range(2):
-        lax.fori_loop(16 * part, 16 * part + 16, one_leaf, 0, unroll=8)
+        lax.fori_loop(16 * part, 16 * part + 16, one_leaf, 0, unroll=16)
         own = slice(2048 * part, 2048 * part + 2048)
         stores += started(semaphores.at[4 + part :], (out.at[:, own], out_hbm.at[:, own]))
     for copy in stores:
@@ -553,7 +563,7 @@
             factors[(i * 4 + m) * 2 + 1] = halves(turned, slab).astype(bf16)
         return carry
 
-    lax.fori_loop(0, groups, four_slabs, 0, unroll=2)
+    lax.fori_loop(0, groups, four_slabs, 0, unroll=True)
 
 
 def prepare_weights(moments, weights, groups):
@@ -565,7 +575,7 @@
             weights[turn, i, 1] = turns[turn][RANK:]
         return carry
 
-    lax.fori_loop(0, groups, four_slabs, 0, unroll=2)
+    lax.fori_loop(0, groups, four_slabs, 0, unroll=True)
 
 
 def two_targets(anchors):
@@ -676,7 +686,7 @@
             located = []
             for cluster in range(2):
                 for j in range(8):
-                    entry = lists[2 * LEAVES_DEV - 2 * number + 2 * q + cluster, j]
+                    entry = lists[j, 2 * LEAVES_DEV - 2 * number + 2 * q + cluster]
                     located.append(
                         locate(entry, first, number + 2 * REACH - 1, FINE_BASE[height], FINE_EMPTY)
                     )
@@ -684,7 +694,7 @@
             far[:, columns] = two_clusters(anchors[:, columns], factors, weights, located)
             return carry
 
-        lax.fori_loop(0, number // 2, one_pair, 0, unroll=4)
+        lax.fori_loop(0, number // 2, one_pair, 0, unroll=True)
     for copy in started(semaphores, (far, far_hbm)):
         copy.wait()
 
@@ -727,6 +737,7 @@
     outer_hbm,
     beyond_hbm,
     third_hbm,
+    summit,
     top_hbm,
     incoming_hbm,
     matrices_hbm,
@@ -814,7 +825,7 @@
         located = []
         for cluster in range(2):
             for j in range(8):
-                entry = lists[2 * LEAVES_DEV - 2 * number + 2 * q + cluster, j]
+                entry = lists[j, 2 * LEAVES_DEV - 2 * number + 2 * q + cluster]
                 located.append(
                     locate(entry, me * number - REACH, number + 2 * REACH - 1, base, COARSE_EMPTY)
                 )
@@ -837,16 +848,14 @@
             jnp.where(lane < RANK, pltpu.roll(first, RANK, 1), second),
         )
 
-    sixth = [
-        jnp.sum(incoming[64 * c : 64 * (c + 1), 8 * (SLOTS - 1) : 8 * SLOTS, :], axis=0)
-        for c in range(2)
-    ]
+    sixth = [summit[0], summit[1]]
     seventh = lifted(two_blocks(*sixth), matrices[RANK * (LOCAL + 7) : RANK * (LOCAL + 9), :])
     seventh = as_block(seventh)
 
     def held(kind, other):
-        slot = tables[SENT // 128 + kind, other]
-        return slot, incoming[other, pl.ds(pl.multiple_of((slot & 3) * 8, 8), 8), :]
+        slot = tables[SLOTS + kind, other]
+        place = jnp.minimum(slot, SLOTS - 1)
+        return slot, incoming[other, pl.ds(pl.multiple_of(place * 8, 8), 8), :]
 
     for index, shift in enumerate(FORMED):
         other = jnp.minimum(jnp.maximum(me + shift, 0), DEVICES - 1)
@@ -854,10 +863,10 @@
         start = RANK * (LOCAL + 9 + index)
         formed[index] = as_block(lifted(value, matrices[start : start + RANK, :]))
 
-    entries = [[lists[62, j] for j in range(8)]]
+    entries = [[lists[j, 62] for j in range(8)]]
     for level in range(1, TOP + 1):
         row = DEVICES - (DEVICES >> (level - 1)) + (me >> level)
-        entries.append([top_lists[row, j] for j in range(8)])
+        entries.append([top_lists[j, row] for j in range(8)])
 
     def block(level, entry):
         if level == TOP:
@@ -867,13 +876,17 @@
         first = jnp.maximum(entry, 0) << level
 
         def add(i, total):
-            slot, value = held(level, first + i)
-            if level == 2:
-                value = jnp.where(slot < SLOTS, value, formed[slot & 3])
-            return total + value
-
-        count = jnp.where(entry < 0, 0, 1 << level)
-        return lax.fori_loop(0, count, add, jnp.zeros((8, 128), f32))
+            for step in range(min(8, 1 << level)):
+                slot, value = held(level, first + min(8, 1 << level) * i + step)
+                if level == 2:
+                    value = jnp.where(slot < SLOTS, value, formed[slot & 3])
+                total = total + value
+            return total
+
+        nothing = jnp.zeros((8, 128), f32)
+        if level <= 3:
+            return jnp.where(entry < 0, nothing, add(0, nothing))
+        return lax.fori_loop(0, jnp.where(entry < 0, 0, 1 << (level - 3)), add, nothing)
 
     wanted = [0] + [DEVICES - (DEVICES >> (level - 1)) + (me >> level) for level in range(1, TOP + 1)]
     for level in range(1, TOP + 1):
@@ -969,7 +982,7 @@
     return pl.pallas_call(
         coarse_kernel,
         out_shape=jax.ShapeDtypeStruct((RHS, LEAVES_DEV * LEAF), f32),
-        in_specs=[SMEM] * 3 + [HBM] * 13,
+        in_specs=[SMEM] * 3 + [HBM] * 7 + [VMEM] + [HBM] * 6,
         out_specs=HBM,
         scratch_shapes=[
             pltpu.SMEM((TABLE, 128), jnp.int32),
@@ -1050,7 +1063,7 @@
     outer_leaves = exchanged(outer_edge, outer_mate)
 
     tables = jnp.asarray(slot_tables())
-    moments, anchors, inner_rim, outer_rim, third, outgoing, matrices = moments_call(
+    moments, anchors, inner_rim, outer_rim, third, summit, outgoing, matrices = moments_call(
         device, tables, leaf_basis, charges, local_transfer, local_anchors, top_transfer
     )
     outgoing, inner_leaves, outer_leaves = lax.optimization_barrier(
@@ -1058,18 +1071,26 @@
     )
     inner = exchanged(inner_rim, inner_mate)
     incoming = lax.all_to_all(outgoing, "leaf", 0, 0)
+    summit = lax.cond(
+        jnp.any(top_lists[SUMMIT_ROW:] >= 0),
+        lambda value: lax.psum(value, "leaf"),
+        lambda value: jnp.zeros_like(value),
+        summit,
+    )
     outer = exchanged(
         jnp.concatenate([outer_rim, inner[:, RIM[3] : RIM[5]]], axis=1), outer_mate
     )
+    near = near_call(device, near_blocks.T, points, charges, inner_leaves, outer_leaves)
+    near, third = lax.optimization_barrier((near, third))
     third = exchanged(third, third_mate)
-    near = near_call(device, near_blocks, points, charges, inner_leaves, outer_leaves)
     near, outer = lax.optimization_barrier((near, outer))
     beyond = exchanged(outer[:, RIM[3] :], inner_mate)
+    local_lists = local_lists.T
     far = fine_call(device, local_lists, anchors, moments, inner, outer)
     return coarse_call(
         device,
         local_lists,
-        top_lists,
+        top_lists.T,
         tables,
         anchors,
         moments,
@@ -1077,6 +1098,7 @@
         outer,
         beyond,
         third,
+        summit,
         top_anchors,
         incoming,
         matrices,

time: 86.6 us -> 73.4 us (0.85)
  Pallas kernels: 54.1 us -> 43.6 us
  local copies, waits for them, and re-layouts: 5.06 us -> 2.92 us
  waiting for transfers between devices: 1.34 us -> 0.22 us
    pallas_call x1, Pallas kernels: 13.7 us -> 9.98 us  [fine_call(): pl.pallas_call(fine_kernel, out_shape=jax.ShapeDtypeStruct((RHS, 56 * RAN...]
    pallas_call x1, Pallas kernels: 14.7 us -> 11.1 us  [coarse_call(): pl.pallas_call(coarse_kernel, out_shape=jax.ShapeDtypeStruct((RHS, LEAVES...]
    unnamed x29 -> x20, local copies, waits for them, and re-layouts: 3.91 us -> 1.78 us
    pallas_call x1, Pallas kernels: 16.3 us -> 14.5 us  [near_call(): pl.pallas_call(near_kernel, out_shape=jax.ShapeDtypeStruct((RHS, LEAVES_D...]
    pallas_call x1, Pallas kernels: 9.48 us -> 8.04 us  [moments_call(): pl.pallas_call(moments_kernel, out_shape=(shape((16, 4096), f32), shape((...]
    ppermute x6, waiting for transfers between devices: 1.34 us -> 0.21 us  [exchanged(): return lax.ppermute(value, 'leaf', pairs)]
  transfers between devices with their start and end apart: 7 -> 7, of which waited for: 1 -> 2; matrix products, arithmetic and copies ran while one was open for 2% -> 1% of each run, Pallas kernels for 46% -> 45%
where the time goes in v3:
time: 73.4 us; the launch traced here: 72.5 us
  Pallas kernels  43.6 us (59%)
  starting transfers between devices  23.8 us (32%)
  local copies, waits for them, and re-layouts  2.92 us (4%)
  between operations  1.15 us (2%)
  other arithmetic  0.84 us (1%)
    ppermute x6, starting transfers between devices, exchanged(): return lax.ppermute(value, 'leaf', pairs)  17.2 us
    pallas_call x1, Pallas kernels, near_call(): pl.pallas_call(near_kernel, out_shape=jax.ShapeDtypeStruct((RHS, LEAVES_D...  14.5 us
    pallas_call x1, Pallas kernels, coarse_call(): pl.pallas_call(coarse_kernel, out_shape=jax.ShapeDtypeStruct((RHS, LEAVES...  11.1 us
    pallas_call x1, Pallas kernels, fine_call(): pl.pallas_call(fine_kernel, out_shape=jax.ShapeDtypeStruct((RHS, 56 * RAN...  9.98 us
    pallas_call x1, Pallas kernels, moments_call(): pl.pallas_call(moments_kernel, out_shape=(shape((16, 4096), f32), shape((...  8.04 us
    all_to_all x1, starting transfers between devices, on_device(): incoming = lax.all_to_all(outgoing, 'leaf', 0, 0)  6.59 us
    unnamed x20, local copies, waits for them, and re-layouts  1.78 us
  transfers between devices with their start and end apart: 7, of which 2 were waited for; matrix products, arithmetic and copies ran while one was open for 1% of the time, Pallas kernels for 45%

profile of v3, /device:TPU:32, one launch (start us, length us, event | category | flops | bytes accessed | tf_op | source)
XLA Modules:
  0.0 72.5 jit_solution(612759439509373786)
XLA Ops:
  0.0 1.1 %constant_dynamic-slice_fusion = (f32[16,2048]{1,0:T(8,128)S(1)}, f32[16,2048]{1,0:T(8,128)S(1)}, f32[16,2048]{1,0:T(8,128)S(1)}, f32[16,2048]{1,0:T(8,128)S(1)}) fusion(f32[16,4096]{1,0:T(8,128)} %charges_hbm.3, s32[]{:T(128)S(6)} %select_n.9, s32[]{:T(128)S(6)} %select_n.8, f32[16,4096]{1,0:T(8,128)} %points_hbm.1), kind=kLoop, calls=%fused_computation.5 | loop fusion | bytes 1048584 | tf_op jit(solution)/shard_map/dynamic_slice | solution.py:1056
  1.2 0.0 copy-start.6
  1.2 0.1 collective-permute-start.1
  1.3 6.8 %collective-permute-start.2 = (f32[32,2048]{1,0:T(8,128)S(1)}, f32[32,2048]{1,0:T(8,128)S(1)}, u32[]{:S(2)}, u32[]{:S(2)}) collective-permute-start(f32[32,2048]{1,0:T(8,128)S(1)} %pad_maximum_fusion.1), channel_id=1, source_target_pairs={{0,0},{1,2},{2,1},{3,4},{4,3},{5,6},{6,5},{7,8},{8,7},{9,10},{10,9... | collective-permute-start | bytes 786440 | tf_op jit(solution)/shard_map/ppermute | solution.py:1022
  8.1 8.0 %moments.1 = (f32[16,4096]{1,0:T(8,128)}, f32[16,4096]{1,0:T(8,128)}, f32[32,1664]{1,0:T(8,128)}, f32[32,1664]{1,0:T(8,128)}, f32[32,128]{1,0:T(8,128)}, /*index...) custom-call(s32[1]{0:T(128)} %bitcast.device, s32[128,10,128]{2,1,0:T(8,128)} %constant.21.clone.tables_hbm, ...), custom_call_target="tpu_custom_call" | custom-call | flops 1000000000 | bytes 4194304 | tf_op jit(solution)/shard_map/moments/pallas_call | solution.py:408
  16.1 0.0 copy-start.3
  16.1 0.1 collective-permute-start
  16.2 0.0 copy-done.6
  16.2 0.8 %fusion = pred[]{:T(512)} fusion(s32[127,8]{0,1:T(8,128)S(1)} %copy-done.6), kind=kLoop, calls=%fused_computation.4 | loop fusion | flops 47 | bytes 97 | tf_op jit(solution)/shard_map/reduce_or | solution.py:1075
  17.7 0.1 collective-permute-done.inner_hbm
  17.9 0.0 collective-permute-done.1.inner_hbm
  17.9 0.0 copy-start.7
  17.9 0.0 collective-permute-done.2.outer_hbm
  17.9 0.0 copy-start.8
  17.9 6.6 %all-to-all-start = ((f32[128,24,128]{2,1,0:T(8,128)}), f32[128,24,128]{2,1,0:T(8,128)S(1)}, u32[]{:S(2)}, u32[]{:S(2)}) async-start(f32[128,24,128]{2,1,0:T(8,128)} %get-tuple-element.42), calls=%async_computation | async-start | bytes 3145728 | tf_op jit(solution)/shard_map/all_to_all | solution.py:1073
  24.5 0.0 copy-done.3
  24.6 6.6 %collective-permute-start.3 = (f32[32,2048]{1,0:T(8,128)S(1)}, f32[32,2048]{1,0:T(8,128)S(1)}, u32[]{:S(2)}, u32[]{:S(2)}) collective-permute-start(f32[32,2048]{1,0:T(8,128)S(1)} %pad_maximum_fusion.2), channel_id=1, source_target_pairs={{0,0},{1,2},{2,1},{3,4},{4,3},{5,6},{6,5},{7,8},{8,7},{9,10},{10,9... | collective-permute-start | bytes 786440 | tf_op jit(solution)/shard_map/ppermute | solution.py:1022
  31.2 0.0 copy-done.7
  31.2 14.5 %near.1.near_hbm = f32[16,4096]{1,0:T(8,128)} custom-call(s32[1]{0:T(128)} %bitcast.device, s32[8,32]{1,0:T(8,128)} %bitcast.7, f32[16,4096]{1,0:T(8,128)} %points_hbm.1, f32[16,4096]{1,0:T(8,128)} %charges_hbm.3, f32[32,2048]{1,0:T(8,128)} %copy-done.7, f32[32,2048]{1,0:T(8,128)} %copy-done.8), custom_call_target="tpu_custom_call" | custom-call | flops 10000000000 | bytes 4194304 | tf_op jit(solution)/shard_map/near/pallas_call | solution.py:535
  45.7 3.6 %collective-permute-start.5 = (f32[32,128]{1,0:T(8,128)S(1)}, f32[32,128]{1,0:T(8,128)S(1)}, u32[]{:S(2)}, u32[]{:S(2)}) collective-permute-start(f32[32,128]{1,0:T(8,128)S(1)} %copy-done.9), channel_id=1, source_target_pairs={{0,0},{1,4},{2,2},{3,6},{4,1},{5,8},{6,3},{7,10},{8,5},{9,12},{10,... | collective-permute-start | bytes 49160 | tf_op jit(solution)/shard_map/ppermute | solution.py:1022
  49.3 0.1 collective-permute-done.3.outer_hbm
  49.4 0.1 collective-permute-start.4
  49.5 0.6 copy-done.1
  50.1 10.0 %fine.1.far_hbm = f32[16,3584]{1,0:T(8,128)} custom-call(s32[1]{0:T(128)} %bitcast.device, s32[8,63]{1,0:T(8,128)} %bitcast.5, f32[16,4096]{1,0:T(8,128)} %get-tuple-element.28.anchors_hbm, f32[16,4096]{1,0:T(8,128)} %get-tuple-element.29.moments_hbm, f32[32,1664]{1,0:T(8,128)} %copy-done.2, f32[32,2048]{1,0:T(8,128)} %copy-done.1), custom_call_target="tpu_custom_call" | custom-call | flops 5000000000 | bytes 4194304 | tf_op jit(solution)/shard_map/fine/pallas_call | solution.py:703
  60.1 0.0 collective-permute-done.5.third_hbm
  60.1 0.0 collective-permute-done.4.beyond_hbm
  60.1 0.0 copy-start.4
  60.1 0.0 all-to-all-done.incoming_hbm
  60.1 0.5 copy-done.5
  60.7 0.1 copy-done.4
  60.7 0.5 copy-done
  61.3 11.1 %coarse.1 = f32[16,4096]{1,0:T(8,128)} custom-call(s32[1]{0:T(128)} %bitcast.device, s32[8,63]{1,0:T(8,128)} %bitcast.6, s32[8,127]{1,0:T(8,128)} %bitcast.4, s32[128,10,128]{2,1,0:T(8,128)} %constant.21.clone.tables_hbm, f32[16,4096]{1,0:T(8,128)} %get-tuple-element.28.anchors_hbm, f32[16,4096]{1,0:T(8,128)} %get-tuple-element.29.moments_hbm, ...), custom_call_target="tpu_custom_call" | custom-call | flops 1000000000 | bytes 8388608 | tf_op jit(solution)/shard_map/coarse/pallas_call | solution.py:982
  (15 shorter events, 0.1 us)
Async XLA Ops:
  1.2 15.0 %copy-start.6 = (s32[127,8]{0,1:T(8,128)S(1)}, s32[127,8]{0,1:T(8,128)}, u32[]{:S(2)}) copy-start(s32[127,8]{0,1:T(8,128)} %param.22) | copy-start | bytes 12196
  1.2 16.7 %collective-permute-start.1 = (f32[32,2048]{1,0:T(8,128)S(1)}, f32[32,2048]{1,0:T(8,128)S(1)}, u32[]{:S(2)}, u32[]{:S(2)}) collective-permute-start(f32[32,2048]{1,0:T(8,128)S(1)} %pad_maximum_fusion), channel_id=1, source_target_pairs={{0,1},{1,0},{2,3},{3,2},{4,5},{5,4},{6,7},{7,6},{8,9},{9,8},{10,11... | collective-permute-start | bytes 786440 | tf_op jit(solution)/shard_map/ppermute | solution.py:1022
  1.3 16.6 %collective-permute-start.2 = (f32[32,2048]{1,0:T(8,128)S(1)}, f32[32,2048]{1,0:T(8,128)S(1)}, u32[]{:S(2)}, u32[]{:S(2)}) collective-permute-start(f32[32,2048]{1,0:T(8,128)S(1)} %pad_maximum_fusion.1), channel_id=1, source_target_pairs={{0,0},{1,2},{2,1},{3,4},{4,3},{5,6},{6,5},{7,8},{8,7},{9,10},{10,9... | collective-permute-start | bytes 786440 | tf_op jit(solution)/shard_map/ppermute | solution.py:1022
  16.1 8.4 %copy-start.3 = (f32[32,1664]{1,0:T(8,128)S(1)}, f32[32,1664]{1,0:T(8,128)}, u32[]{:S(2)}) copy-start(f32[32,1664]{1,0:T(8,128)} %get-tuple-element.38) | copy-start | bytes 638980
  16.1 1.8 %collective-permute-start = (f32[32,1664]{1,0:T(8,128)}, f32[32,1664]{1,0:T(8,128)S(1)}, u32[]{:S(2)}, u32[]{:S(2)}) collective-permute-start(f32[32,1664]{1,0:T(8,128)} %get-tuple-element.30), channel_id=1, source_target_pairs={{0,1},{1,0},{2,3},{3,2},{4,5},{5,4},{6,7},{7,6},{8,9},{9,8},{10,11... | collective-permute-start | bytes 638984 | tf_op jit(solution)/shard_map/ppermute | solution.py:1022
  17.9 27.8 %copy-start.2 = (f32[32,1664]{1,0:T(8,128)}, f32[32,1664]{1,0:T(8,128)S(1)}, u32[]{:S(2)}) copy-start(f32[32,1664]{1,0:T(8,128)S(1)} %collective-permute-done.inner_hbm) | copy-start | bytes 638980
  17.9 13.3 %copy-start.7 = (f32[32,2048]{1,0:T(8,128)}, f32[32,2048]{1,0:T(8,128)S(1)}, u32[]{:S(2)}) copy-start(f32[32,2048]{1,0:T(8,128)S(1)} %collective-permute-done.1.inner_hbm) | copy-start | bytes 786436
  17.9 13.3 %copy-start.8 = (f32[32,2048]{1,0:T(8,128)}, f32[32,2048]{1,0:T(8,128)S(1)}, u32[]{:S(2)}) copy-start(f32[32,2048]{1,0:T(8,128)S(1)} %collective-permute-done.2.outer_hbm) | copy-start | bytes 786436
  17.9 42.2 %all-to-all-start = ((f32[128,24,128]{2,1,0:T(8,128)}), f32[128,24,128]{2,1,0:T(8,128)S(1)}, u32[]{:S(2)}, u32[]{:S(2)}) async-start(f32[128,24,128]{2,1,0:T(8,128)} %get-tuple-element.42), calls=%async_computation | async-start | bytes 3145728 | tf_op jit(solution)/shard_map/all_to_all | solution.py:1073
  24.6 24.8 %collective-permute-start.3 = (f32[32,2048]{1,0:T(8,128)S(1)}, f32[32,2048]{1,0:T(8,128)S(1)}, u32[]{:S(2)}, u32[]{:S(2)}) collective-permute-start(f32[32,2048]{1,0:T(8,128)S(1)} %pad_maximum_fusion.2), channel_id=1, source_target_pairs={{0,0},{1,2},{2,1},{3,4},{4,3},{5,6},{6,5},{7,8},{8,7},{9,10},{10,9... | collective-permute-start | bytes 786440 | tf_op jit(solution)/shard_map/ppermute | solution.py:1022
  31.2 14.5 %copy-start.9 = (f32[32,128]{1,0:T(8,128)S(1)}, f32[32,128]{1,0:T(8,128)}, u32[]{:S(2)}) copy-start(f32[32,128]{1,0:T(8,128)} %get-tuple-element.40) | copy-start | bytes 49156
  45.7 14.3 %collective-permute-start.5 = (f32[32,128]{1,0:T(8,128)S(1)}, f32[32,128]{1,0:T(8,128)S(1)}, u32[]{:S(2)}, u32[]{:S(2)}) collective-permute-start(f32[32,128]{1,0:T(8,128)S(1)} %copy-done.9), channel_id=1, source_target_pairs={{0,0},{1,4},{2,2},{3,6},{4,1},{5,8},{6,3},{7,10},{8,5},{9,12},{10,... | collective-permute-start | bytes 49160 | tf_op jit(solution)/shard_map/ppermute | solution.py:1022
  49.4 0.7 copy-start.1
  49.4 10.7 %collective-permute-start.4 = (f32[32,896]{1,0:T(8,128)S(1)}, f32[32,896]{1,0:T(8,128)S(1)}, u32[]{:S(2)}, u32[]{:S(2)}) collective-permute-start(f32[32,896]{1,0:T(8,128)S(1)} %slice.10), channel_id=1, source_target_pairs={{0,1},{1,0},{2,3},{3,2},{4,5},{5,4},{6,7},{7,6},{8,9},{9,8},{10,11... | collective-permute-start | bytes 344072 | tf_op jit(solution)/shard_map/ppermute | solution.py:1022
  60.1 0.6 copy-start.5
  60.1 0.7 copy-start.4
  60.1 1.2 %copy-start = (f32[128,24,128]{2,1,0:T(8,128)}, f32[128,24,128]{2,1,0:T(8,128)S(1)}, u32[]{:S(2)}) copy-start(f32[128,24,128]{2,1,0:T(8,128)S(1)} %all-to-all-done.incoming_hbm) | copy-start | bytes 4718596

commit v4 on v3

--- a/solution.py
+++ b/solution.py
@@ -836,57 +836,10 @@
     far_third = [local_pair(3, q, 0) for q in range(2)]
     far_fourth = local_pair(4, 0, 16)
 
-    loads[8].wait()
-    loads[9].wait()
-    loads[7].wait()
-
-    lane = lax.broadcasted_iota(jnp.int32, (8, 128), 1)
-
-    def two_blocks(first, second):
-        return rows(
-            jnp.where(lane < RANK, first, pltpu.roll(second, RANK, 1)),
-            jnp.where(lane < RANK, pltpu.roll(first, RANK, 1), second),
-        )
-
-    sixth = [summit[0], summit[1]]
-    seventh = lifted(two_blocks(*sixth), matrices[RANK * (LOCAL + 7) : RANK * (LOCAL + 9), :])
-    seventh = as_block(seventh)
-
-    def held(kind, other):
-        slot = tables[SLOTS + kind, other]
-        place = jnp.minimum(slot, SLOTS - 1)
-        return slot, incoming[other, pl.ds(pl.multiple_of(place * 8, 8), 8), :]
-
-    for index, shift in enumerate(FORMED):
-        other = jnp.minimum(jnp.maximum(me + shift, 0), DEVICES - 1)
-        value = two_blocks(held(1, other)[1], jnp.zeros((8, 128), f32))[:, :RANK]
-        start = RANK * (LOCAL + 9 + index)
-        formed[index] = as_block(lifted(value, matrices[start : start + RANK, :]))
-
     entries = [[lists[j, 62] for j in range(8)]]
     for level in range(1, TOP + 1):
         row = DEVICES - (DEVICES >> (level - 1)) + (me >> level)
         entries.append([top_lists[j, row] for j in range(8)])
-
-    def block(level, entry):
-        if level == TOP:
-            return jnp.where(entry == 0, seventh, 0.0)
-        if level == SHARED:
-            return jnp.where(entry == 0, sixth[0], jnp.where(entry == 1, sixth[1], 0.0))
-        first = jnp.maximum(entry, 0) << level
-
-        def add(i, total):
-            for step in range(min(8, 1 << level)):
-                slot, value = held(level, first + min(8, 1 << level) * i + step)
-                if level == 2:
-                    value = jnp.where(slot < SLOTS, value, formed[slot & 3])
-                total = total + value
-            return total
-
-        nothing = jnp.zeros((8, 128), f32)
-        if level <= 3:
-            return jnp.where(entry < 0, nothing, add(0, nothing))
-        return lax.fori_loop(0, jnp.where(entry < 0, 0, 1 << (level - 3)), add, nothing)
 
     wanted = [0] + [DEVICES - (DEVICES >> (level - 1)) + (me >> level) for level in range(1, TOP + 1)]
     for level in range(1, TOP + 1):
@@ -899,12 +852,64 @@
         regrouped(lambda c: top_anchors[pl.ds(part[c], 1), :], staged.at[group % 2], 8, 8)
         columns += eight_anchors([tile(staged.at[group % 2], c, 8) for c in range(8)])
 
+    loads[8].wait()
+    loads[9].wait()
+    loads[7].wait()
+
+    lane = lax.broadcasted_iota(jnp.int32, (8, 128), 1)
+
+    def two_blocks(first, second):
+        return rows(
+            jnp.where(lane < RANK, first, pltpu.roll(second, RANK, 1)),
+            jnp.where(lane < RANK, pltpu.roll(first, RANK, 1), second),
+        )
+
+    sixth = [summit[0], summit[1]]
+    seventh = lifted(two_blocks(*sixth), matrices[RANK * (LOCAL + 7) : RANK * (LOCAL + 9), :])
+    seventh = as_block(seventh)
+
+    def held(kind, other):
+        slot = tables[SLOTS + kind, other]
+        place = jnp.minimum(slot, SLOTS - 1)
+        return slot, incoming[other, pl.ds(pl.multiple_of(place * 8, 8), 8), :]
+
+    for index, shift in enumerate(FORMED):
+        other = jnp.minimum(jnp.maximum(me + shift, 0), DEVICES - 1)
+        value = two_blocks(held(1, other)[1], jnp.zeros((8, 128), f32))[:, :RANK]
+        start = RANK * (LOCAL + 9 + index)
+        formed[index] = as_block(lifted(value, matrices[start : start + RANK, :]))
+
+    def block(level, entry):
+        if level == TOP:
+            return jnp.where(entry == 0, seventh, 0.0)
+        if level == SHARED:
+            return jnp.where(entry == 0, sixth[0], jnp.where(entry == 1, sixth[1], 0.0))
+        first = jnp.maximum(entry, 0) << level
+
+        def add(i, total):
+            for step in range(min(8, 1 << level)):
+                slot, value = held(level, first + min(8, 1 << level) * i + step)
+                if level == 2:
+                    value = jnp.where(slot < SLOTS, value, formed[slot & 3])
+                total = total + value
+            return total
+
+        nothing = jnp.zeros((8, 128), f32)
+        if level <= 4:
+            total = nothing
+            for i in range(max(1, (1 << level) // 8)):
+                total = add(i, total)
+            return jnp.where(entry < 0, nothing, total)
+        return lax.fori_loop(0, jnp.where(entry < 0, 0, 1 << (level - 3)), add, nothing)
+
+    found_pairs = []
+    for level in range(TOP + 1):
+        sums = [block(level, entry) for entry in entries[level]]
+        found_pairs += [two_blocks(sums[2 * j], sums[2 * j + 1]) for j in range(4)]
+
     far_chain = []
     for unit in range(4):
-        pairs = []
-        for level in (2 * unit, 2 * unit + 1):
-            sums = [block(level, entry) for entry in entries[level]]
-            pairs += [two_blocks(sums[2 * j], sums[2 * j + 1]) for j in range(4)]
+        pairs = found_pairs[8 * unit : 8 * unit + 8]
         weight = []
         for h in range(2):
             parts = []

time: 73.4 us -> 73.1 us (level)
  no operation moved by 1% of the time
where the time goes in v4:
time: 73.1 us; the launch traced here: 72.3 us
  Pallas kernels  43.4 us (59%)
  starting transfers between devices  23.8 us (33%)
  local copies, waits for them, and re-layouts  2.92 us (4%)
  between operations  1.15 us (2%)
  other arithmetic  0.84 us (1%)
    ppermute x6, starting transfers between devices, exchanged(): return lax.ppermute(value, 'leaf', pairs)  17.2 us
    pallas_call x1, Pallas kernels, near_call(): pl.pallas_call(near_kernel, out_shape=jax.ShapeDtypeStruct((RHS, LEAVES_D...  14.5 us
    pallas_call x1, Pallas kernels, coarse_call(): pl.pallas_call(coarse_kernel, out_shape=jax.ShapeDtypeStruct((RHS, LEAVES...  10.8 us
    pallas_call x1, Pallas kernels, fine_call(): pl.pallas_call(fine_kernel, out_shape=jax.ShapeDtypeStruct((RHS, 56 * RAN...  9.98 us
    pallas_call x1, Pallas kernels, moments_call(): pl.pallas_call(moments_kernel, out_shape=(shape((16, 4096), f32), shape((...  8.04 us
    all_to_all x1, starting transfers between devices, on_device(): incoming = lax.all_to_all(outgoing, 'leaf', 0, 0)  6.59 us
    unnamed x20, local copies, waits for them, and re-layouts  1.78 us
  transfers between devices with their start and end apart: 7, of which 2 were waited for; matrix products, arithmetic and copies ran while one was open for 1% of the time, Pallas kernels for 45%

profile of v4, /device:TPU:32, one launch (start us, length us, event | category | flops | bytes accessed | tf_op | source)
XLA Modules:
  0.0 72.3 jit_solution(8819897949068639651)
XLA Ops:
  0.0 1.1 %constant_dynamic-slice_fusion = (f32[16,2048]{1,0:T(8,128)S(1)}, f32[16,2048]{1,0:T(8,128)S(1)}, f32[16,2048]{1,0:T(8,128)S(1)}, f32[16,2048]{1,0:T(8,128)S(1)}) fusion(f32[16,4096]{1,0:T(8,128)} %charges_hbm.3, s32[]{:T(128)S(6)} %select_n.9, s32[]{:T(128)S(6)} %select_n.8, f32[16,4096]{1,0:T(8,128)} %points_hbm.1), kind=kLoop, calls=%fused_computation.5 | loop fusion | bytes 1048584 | tf_op jit(solution)/shard_map/dynamic_slice | solution.py:1061
  1.2 0.0 copy-start.6
  1.2 0.1 collective-permute-start.1
  1.3 6.8 %collective-permute-start.2 = (f32[32,2048]{1,0:T(8,128)S(1)}, f32[32,2048]{1,0:T(8,128)S(1)}, u32[]{:S(2)}, u32[]{:S(2)}) collective-permute-start(f32[32,2048]{1,0:T(8,128)S(1)} %pad_maximum_fusion.1), channel_id=1, source_target_pairs={{0,0},{1,2},{2,1},{3,4},{4,3},{5,6},{6,5},{7,8},{8,7},{9,10},{10,9... | collective-permute-start | bytes 786440 | tf_op jit(solution)/shard_map/ppermute | solution.py:1027
  8.1 8.0 %moments.1 = (f32[16,4096]{1,0:T(8,128)}, f32[16,4096]{1,0:T(8,128)}, f32[32,1664]{1,0:T(8,128)}, f32[32,1664]{1,0:T(8,128)}, f32[32,128]{1,0:T(8,128)}, /*index...) custom-call(s32[1]{0:T(128)} %bitcast.device, s32[128,10,128]{2,1,0:T(8,128)} %constant.21.clone.tables_hbm, ...), custom_call_target="tpu_custom_call" | custom-call | flops 1000000000 | bytes 4194304 | tf_op jit(solution)/shard_map/moments/pallas_call | solution.py:408
  16.1 0.0 copy-start.3
  16.1 0.1 collective-permute-start
  16.2 0.0 copy-done.6
  16.2 0.8 %fusion = pred[]{:T(512)} fusion(s32[127,8]{0,1:T(8,128)S(1)} %copy-done.6), kind=kLoop, calls=%fused_computation.4 | loop fusion | flops 47 | bytes 97 | tf_op jit(solution)/shard_map/reduce_or | solution.py:1080
  17.7 0.1 collective-permute-done.inner_hbm
  17.9 0.0 collective-permute-done.1.inner_hbm
  17.9 0.0 copy-start.7
  17.9 0.0 collective-permute-done.2.outer_hbm
  17.9 0.0 copy-start.8
  17.9 6.6 %all-to-all-start = ((f32[128,24,128]{2,1,0:T(8,128)}), f32[128,24,128]{2,1,0:T(8,128)S(1)}, u32[]{:S(2)}, u32[]{:S(2)}) async-start(f32[128,24,128]{2,1,0:T(8,128)} %get-tuple-element.42), calls=%async_computation | async-start | bytes 3145728 | tf_op jit(solution)/shard_map/all_to_all | solution.py:1078
  24.5 0.0 copy-done.3
  24.6 6.6 %collective-permute-start.3 = (f32[32,2048]{1,0:T(8,128)S(1)}, f32[32,2048]{1,0:T(8,128)S(1)}, u32[]{:S(2)}, u32[]{:S(2)}) collective-permute-start(f32[32,2048]{1,0:T(8,128)S(1)} %pad_maximum_fusion.2), channel_id=1, source_target_pairs={{0,0},{1,2},{2,1},{3,4},{4,3},{5,6},{6,5},{7,8},{8,7},{9,10},{10,9... | collective-permute-start | bytes 786440 | tf_op jit(solution)/shard_map/ppermute | solution.py:1027
  31.2 0.0 copy-done.7
  31.2 14.5 %near.1.near_hbm = f32[16,4096]{1,0:T(8,128)} custom-call(s32[1]{0:T(128)} %bitcast.device, s32[8,32]{1,0:T(8,128)} %bitcast.7, f32[16,4096]{1,0:T(8,128)} %points_hbm.1, f32[16,4096]{1,0:T(8,128)} %charges_hbm.3, f32[32,2048]{1,0:T(8,128)} %copy-done.7, f32[32,2048]{1,0:T(8,128)} %copy-done.8), custom_call_target="tpu_custom_call" | custom-call | flops 10000000000 | bytes 4194304 | tf_op jit(solution)/shard_map/near/pallas_call | solution.py:535
  45.7 3.6 %collective-permute-start.5 = (f32[32,128]{1,0:T(8,128)S(1)}, f32[32,128]{1,0:T(8,128)S(1)}, u32[]{:S(2)}, u32[]{:S(2)}) collective-permute-start(f32[32,128]{1,0:T(8,128)S(1)} %copy-done.9), channel_id=1, source_target_pairs={{0,0},{1,4},{2,2},{3,6},{4,1},{5,8},{6,3},{7,10},{8,5},{9,12},{10,... | collective-permute-start | bytes 49160 | tf_op jit(solution)/shard_map/ppermute | solution.py:1027
  49.3 0.1 collective-permute-done.3.outer_hbm
  49.4 0.1 collective-permute-start.4
  49.5 0.6 copy-done.1
  50.1 10.0 %fine.1.far_hbm = f32[16,3584]{1,0:T(8,128)} custom-call(s32[1]{0:T(128)} %bitcast.device, s32[8,63]{1,0:T(8,128)} %bitcast.5, f32[16,4096]{1,0:T(8,128)} %get-tuple-element.28.anchors_hbm, f32[16,4096]{1,0:T(8,128)} %get-tuple-element.29.moments_hbm, f32[32,1664]{1,0:T(8,128)} %copy-done.2, f32[32,2048]{1,0:T(8,128)} %copy-done.1), custom_call_target="tpu_custom_call" | custom-call | flops 5000000000 | bytes 4194304 | tf_op jit(solution)/shard_map/fine/pallas_call | solution.py:703
  60.1 0.0 collective-permute-done.5.third_hbm
  60.1 0.0 collective-permute-done.4.beyond_hbm
  60.1 0.0 copy-start.4
  60.1 0.0 all-to-all-done.incoming_hbm
  60.1 0.5 copy-done.5
  60.7 0.1 copy-done.4
  60.7 0.5 copy-done
  61.3 10.8 %coarse.1 = f32[16,4096]{1,0:T(8,128)} custom-call(s32[1]{0:T(128)} %bitcast.device, s32[8,63]{1,0:T(8,128)} %bitcast.6, s32[8,127]{1,0:T(8,128)} %bitcast.4, s32[128,10,128]{2,1,0:T(8,128)} %constant.21.clone.tables_hbm, f32[16,4096]{1,0:T(8,128)} %get-tuple-element.28.anchors_hbm, f32[16,4096]{1,0:T(8,128)} %get-tuple-element.29.moments_hbm, ...), custom_call_target="tpu_custom_call" | custom-call | flops 1000000000 | bytes 8388608 | tf_op jit(solution)/shard_map/coarse/pallas_call | solution.py:987
  (15 shorter events, 0.1 us)
Async XLA Ops:
  1.2 15.0 %copy-start.6 = (s32[127,8]{0,1:T(8,128)S(1)}, s32[127,8]{0,1:T(8,128)}, u32[]{:S(2)}) copy-start(s32[127,8]{0,1:T(8,128)} %param.22) | copy-start | bytes 12196
  1.2 16.7 %collective-permute-start.1 = (f32[32,2048]{1,0:T(8,128)S(1)}, f32[32,2048]{1,0:T(8,128)S(1)}, u32[]{:S(2)}, u32[]{:S(2)}) collective-permute-start(f32[32,2048]{1,0:T(8,128)S(1)} %pad_maximum_fusion), channel_id=1, source_target_pairs={{0,1},{1,0},{2,3},{3,2},{4,5},{5,4},{6,7},{7,6},{8,9},{9,8},{10,11... | collective-permute-start | bytes 786440 | tf_op jit(solution)/shard_map/ppermute | solution.py:1027
  1.3 16.6 %collective-permute-start.2 = (f32[32,2048]{1,0:T(8,128)S(1)}, f32[32,2048]{1,0:T(8,128)S(1)}, u32[]{:S(2)}, u32[]{:S(2)}) collective-permute-start(f32[32,2048]{1,0:T(8,128)S(1)} %pad_maximum_fusion.1), channel_id=1, source_target_pairs={{0,0},{1,2},{2,1},{3,4},{4,3},{5,6},{6,5},{7,8},{8,7},{9,10},{10,9... | collective-permute-start | bytes 786440 | tf_op jit(solution)/shard_map/ppermute | solution.py:1027
  16.1 8.4 %copy-start.3 = (f32[32,1664]{1,0:T(8,128)S(1)}, f32[32,1664]{1,0:T(8,128)}, u32[]{:S(2)}) copy-start(f32[32,1664]{1,0:T(8,128)} %get-tuple-element.38) | copy-start | bytes 638980
  16.1 1.8 %collective-permute-start = (f32[32,1664]{1,0:T(8,128)}, f32[32,1664]{1,0:T(8,128)S(1)}, u32[]{:S(2)}, u32[]{:S(2)}) collective-permute-start(f32[32,1664]{1,0:T(8,128)} %get-tuple-element.30), channel_id=1, source_target_pairs={{0,1},{1,0},{2,3},{3,2},{4,5},{5,4},{6,7},{7,6},{8,9},{9,8},{10,11... | collective-permute-start | bytes 638984 | tf_op jit(solution)/shard_map/ppermute | solution.py:1027
  17.9 27.8 %copy-start.2 = (f32[32,1664]{1,0:T(8,128)}, f32[32,1664]{1,0:T(8,128)S(1)}, u32[]{:S(2)}) copy-start(f32[32,1664]{1,0:T(8,128)S(1)} %collective-permute-done.inner_hbm) | copy-start | bytes 638980
  17.9 13.3 %copy-start.7 = (f32[32,2048]{1,0:T(8,128)}, f32[32,2048]{1,0:T(8,128)S(1)}, u32[]{:S(2)}) copy-start(f32[32,2048]{1,0:T(8,128)S(1)} %collective-permute-done.1.inner_hbm) | copy-start | bytes 786436
  17.9 13.3 %copy-start.8 = (f32[32,2048]{1,0:T(8,128)}, f32[32,2048]{1,0:T(8,128)S(1)}, u32[]{:S(2)}) copy-start(f32[32,2048]{1,0:T(8,128)S(1)} %collective-permute-done.2.outer_hbm) | copy-start | bytes 786436
  17.9 42.2 %all-to-all-start = ((f32[128,24,128]{2,1,0:T(8,128)}), f32[128,24,128]{2,1,0:T(8,128)S(1)}, u32[]{:S(2)}, u32[]{:S(2)}) async-start(f32[128,24,128]{2,1,0:T(8,128)} %get-tuple-element.42), calls=%async_computation | async-start | bytes 3145728 | tf_op jit(solution)/shard_map/all_to_all | solution.py:1078
  24.6 24.8 %collective-permute-start.3 = (f32[32,2048]{1,0:T(8,128)S(1)}, f32[32,2048]{1,0:T(8,128)S(1)}, u32[]{:S(2)}, u32[]{:S(2)}) collective-permute-start(f32[32,2048]{1,0:T(8,128)S(1)} %pad_maximum_fusion.2), channel_id=1, source_target_pairs={{0,0},{1,2},{2,1},{3,4},{4,3},{5,6},{6,5},{7,8},{8,7},{9,10},{10,9... | collective-permute-start | bytes 786440 | tf_op jit(solution)/shard_map/ppermute | solution.py:1027
  31.2 14.5 %copy-start.9 = (f32[32,128]{1,0:T(8,128)S(1)}, f32[32,128]{1,0:T(8,128)}, u32[]{:S(2)}) copy-start(f32[32,128]{1,0:T(8,128)} %get-tuple-element.40) | copy-start | bytes 49156
  45.7 14.3 %collective-permute-start.5 = (f32[32,128]{1,0:T(8,128)S(1)}, f32[32,128]{1,0:T(8,128)S(1)}, u32[]{:S(2)}, u32[]{:S(2)}) collective-permute-start(f32[32,128]{1,0:T(8,128)S(1)} %copy-done.9), channel_id=1, source_target_pairs={{0,0},{1,4},{2,2},{3,6},{4,1},{5,8},{6,3},{7,10},{8,5},{9,12},{10,... | collective-permute-start | bytes 49160 | tf_op jit(solution)/shard_map/ppermute | solution.py:1027
  49.4 0.7 copy-start.1
  49.4 10.7 %collective-permute-start.4 = (f32[32,896]{1,0:T(8,128)S(1)}, f32[32,896]{1,0:T(8,128)S(1)}, u32[]{:S(2)}, u32[]{:S(2)}) collective-permute-start(f32[32,896]{1,0:T(8,128)S(1)} %slice.10), channel_id=1, source_target_pairs={{0,1},{1,0},{2,3},{3,2},{4,5},{5,4},{6,7},{7,6},{8,9},{9,8},{10,11... | collective-permute-start | bytes 344072 | tf_op jit(solution)/shard_map/ppermute | solution.py:1027
  60.1 0.6 copy-start.5
  60.1 0.7 copy-start.4
  60.1 1.2 %copy-start = (f32[128,24,128]{2,1,0:T(8,128)}, f32[128,24,128]{2,1,0:T(8,128)S(1)}, u32[]{:S(2)}) copy-start(f32[128,24,128]{2,1,0:T(8,128)S(1)} %all-to-all-done.incoming_hbm) | copy-start | bytes 4718596

commit v5 on v4

--- a/solution.py
+++ b/solution.py
@@ -302,7 +302,7 @@
 
     for part in range(4):
         loads[1 + part].wait()
-        lax.fori_loop(4 * part, 4 * part + 4, two_leaves, 0, unroll=4)
+    lax.fori_loop(0, LEAVES_DEV // 2, two_leaves, 0, unroll=16)
 
     loads[5].wait()
     for group in range(8):
@@ -396,7 +396,7 @@
 
     loads[7].wait()
     for part in range(4):
-        lax.fori_loop(32 * part, 32 * part + 32, one_device, 0, unroll=8)
+        lax.fori_loop(32 * part, 32 * part + 32, one_device, 0, unroll=32)
         own = slice(32 * part, 32 * part + 32)
         stores += started(semaphores.at[14 + part :], (outgoing.at[own], outgoing_out.at[own]))
     for copy in stores:

time: 73.1 us -> 72.5 us (level)
  transfers between devices with their start and end apart: 7 -> 7, of which waited for: 2 -> 1; matrix products, arithmetic and copies ran while one was open for 1% -> 1% of each run, Pallas kernels for 45% -> 45%
where the time goes in v5:
time: 72.5 us; the launch traced here: 71.7 us
  Pallas kernels  42.8 us (59%)
  starting transfers between devices  23.8 us (33%)
  local copies, waits for them, and re-layouts  2.92 us (4%)
  between operations  1.15 us (2%)
  other arithmetic  0.84 us (1%)
    ppermute x6, starting transfers between devices, exchanged(): return lax.ppermute(value, 'leaf', pairs)  17.2 us
    pallas_call x1, Pallas kernels, near_call(): pl.pallas_call(near_kernel, out_shape=jax.ShapeDtypeStruct((RHS, LEAVES_D...  14.5 us
    pallas_call x1, Pallas kernels, coarse_call(): pl.pallas_call(coarse_kernel, out_shape=jax.ShapeDtypeStruct((RHS, LEAVES...  10.9 us
    pallas_call x1, Pallas kernels, fine_call(): pl.pallas_call(fine_kernel, out_shape=jax.ShapeDtypeStruct((RHS, 56 * RAN...  9.98 us
    pallas_call x1, Pallas kernels, moments_call(): pl.pallas_call(moments_kernel, out_shape=(shape((16, 4096), f32), shape((...  7.48 us
    all_to_all x1, starting transfers between devices, on_device(): incoming = lax.all_to_all(outgoing, 'leaf', 0, 0)  6.58 us
    unnamed x20, local copies, waits for them, and re-layouts  1.78 us
  transfers between devices with their start and end apart: 7, of which 1 were waited for; matrix products, arithmetic and copies ran while one was open for 1% of the time, Pallas kernels for 45%

profile of v5, /device:TPU:32, one launch (start us, length us, event | category | flops | bytes accessed | tf_op | source)
XLA Modules:
  0.0 71.7 jit_solution(16372574078905463158)
XLA Ops:
  0.0 1.1 %constant_dynamic-slice_fusion = (f32[16,2048]{1,0:T(8,128)S(1)}, f32[16,2048]{1,0:T(8,128)S(1)}, f32[16,2048]{1,0:T(8,128)S(1)}, f32[16,2048]{1,0:T(8,128)S(1)}) fusion(f32[16,4096]{1,0:T(8,128)} %charges_hbm.3, s32[]{:T(128)S(6)} %select_n.9, s32[]{:T(128)S(6)} %select_n.8, f32[16,4096]{1,0:T(8,128)} %points_hbm.1), kind=kLoop, calls=%fused_computation.5 | loop fusion | bytes 1048584 | tf_op jit(solution)/shard_map/dynamic_slice | solution.py:1061
  1.2 0.0 copy-start.6
  1.2 0.1 collective-permute-start.1
  1.3 6.8 %collective-permute-start.2 = (f32[32,2048]{1,0:T(8,128)S(1)}, f32[32,2048]{1,0:T(8,128)S(1)}, u32[]{:S(2)}, u32[]{:S(2)}) collective-permute-start(f32[32,2048]{1,0:T(8,128)S(1)} %pad_maximum_fusion.1), channel_id=1, source_target_pairs={{0,0},{1,2},{2,1},{3,4},{4,3},{5,6},{6,5},{7,8},{8,7},{9,10},{10,9... | collective-permute-start | bytes 786440 | tf_op jit(solution)/shard_map/ppermute | solution.py:1027
  8.1 7.5 %moments.1 = (f32[16,4096]{1,0:T(8,128)}, f32[16,4096]{1,0:T(8,128)}, f32[32,1664]{1,0:T(8,128)}, f32[32,1664]{1,0:T(8,128)}, f32[32,128]{1,0:T(8,128)}, /*index...) custom-call(s32[1]{0:T(128)} %bitcast.device, s32[128,10,128]{2,1,0:T(8,128)} %constant.21.clone.tables_hbm, ...), custom_call_target="tpu_custom_call" | custom-call | flops 1000000000 | bytes 4194304 | tf_op jit(solution)/shard_map/moments/pallas_call | solution.py:408
  15.5 0.0 copy-start.3
  15.6 0.1 collective-permute-start
  15.6 0.0 copy-done.6
  15.7 0.8 %fusion = pred[]{:T(512)} fusion(s32[127,8]{0,1:T(8,128)S(1)} %copy-done.6), kind=kLoop, calls=%fused_computation.4 | loop fusion | flops 47 | bytes 97 | tf_op jit(solution)/shard_map/reduce_or | solution.py:1080
  17.2 0.1 collective-permute-done.inner_hbm
  17.3 0.0 collective-permute-done.1.inner_hbm
  17.3 0.0 copy-start.7
  17.3 0.0 collective-permute-done.2.outer_hbm
  17.3 0.0 copy-start.8
  17.4 6.6 %all-to-all-start = ((f32[128,24,128]{2,1,0:T(8,128)}), f32[128,24,128]{2,1,0:T(8,128)S(1)}, u32[]{:S(2)}, u32[]{:S(2)}) async-start(f32[128,24,128]{2,1,0:T(8,128)} %get-tuple-element.42), calls=%async_computation | async-start | bytes 3145728 | tf_op jit(solution)/shard_map/all_to_all | solution.py:1078
  23.9 0.0 copy-done.3
  24.0 6.6 %collective-permute-start.3 = (f32[32,2048]{1,0:T(8,128)S(1)}, f32[32,2048]{1,0:T(8,128)S(1)}, u32[]{:S(2)}, u32[]{:S(2)}) collective-permute-start(f32[32,2048]{1,0:T(8,128)S(1)} %pad_maximum_fusion.2), channel_id=1, source_target_pairs={{0,0},{1,2},{2,1},{3,4},{4,3},{5,6},{6,5},{7,8},{8,7},{9,10},{10,9... | collective-permute-start | bytes 786440 | tf_op jit(solution)/shard_map/ppermute | solution.py:1027
  30.6 0.0 copy-done.7
  30.6 0.0 copy-done.8
  30.6 14.5 %near.1.near_hbm = f32[16,4096]{1,0:T(8,128)} custom-call(s32[1]{0:T(128)} %bitcast.device, s32[8,32]{1,0:T(8,128)} %bitcast.7, f32[16,4096]{1,0:T(8,128)} %points_hbm.1, f32[16,4096]{1,0:T(8,128)} %charges_hbm.3, f32[32,2048]{1,0:T(8,128)} %copy-done.7, f32[32,2048]{1,0:T(8,128)} %copy-done.8), custom_call_target="tpu_custom_call" | custom-call | flops 10000000000 | bytes 4194304 | tf_op jit(solution)/shard_map/near/pallas_call | solution.py:535
  45.2 3.6 %collective-permute-start.5 = (f32[32,128]{1,0:T(8,128)S(1)}, f32[32,128]{1,0:T(8,128)S(1)}, u32[]{:S(2)}, u32[]{:S(2)}) collective-permute-start(f32[32,128]{1,0:T(8,128)S(1)} %copy-done.9), channel_id=1, source_target_pairs={{0,0},{1,4},{2,2},{3,6},{4,1},{5,8},{6,3},{7,10},{8,5},{9,12},{10,... | collective-permute-start | bytes 49160 | tf_op jit(solution)/shard_map/ppermute | solution.py:1027
  48.7 0.0 collective-permute-done.3.outer_hbm
  48.8 0.1 collective-permute-start.4
  48.9 0.6 copy-done.1
  49.5 10.0 %fine.1.far_hbm = f32[16,3584]{1,0:T(8,128)} custom-call(s32[1]{0:T(128)} %bitcast.device, s32[8,63]{1,0:T(8,128)} %bitcast.5, f32[16,4096]{1,0:T(8,128)} %get-tuple-element.28.anchors_hbm, f32[16,4096]{1,0:T(8,128)} %get-tuple-element.29.moments_hbm, f32[32,1664]{1,0:T(8,128)} %copy-done.2, f32[32,2048]{1,0:T(8,128)} %copy-done.1), custom_call_target="tpu_custom_call" | custom-call | flops 5000000000 | bytes 4194304 | tf_op jit(solution)/shard_map/fine/pallas_call | solution.py:703
  59.5 0.0 collective-permute-done.5.third_hbm
  59.5 0.0 collective-permute-done.4.beyond_hbm
  59.5 0.0 all-to-all-done.incoming_hbm
  59.6 0.5 copy-done.5
  60.1 0.1 copy-done.4
  60.2 0.5 copy-done
  60.7 10.9 %coarse.1 = f32[16,4096]{1,0:T(8,128)} custom-call(s32[1]{0:T(128)} %bitcast.device, s32[8,63]{1,0:T(8,128)} %bitcast.6, s32[8,127]{1,0:T(8,128)} %bitcast.4, s32[128,10,128]{2,1,0:T(8,128)} %constant.21.clone.tables_hbm, f32[16,4096]{1,0:T(8,128)} %get-tuple-element.28.anchors_hbm, f32[16,4096]{1,0:T(8,128)} %get-tuple-element.29.moments_hbm, ...), custom_call_target="tpu_custom_call" | custom-call | flops 1000000000 | bytes 8388608 | tf_op jit(solution)/shard_map/coarse/pallas_call | solution.py:987
  (15 shorter events, 0.1 us)
Async XLA Ops:
  1.2 14.5 %copy-start.6 = (s32[127,8]{0,1:T(8,128)S(1)}, s32[127,8]{0,1:T(8,128)}, u32[]{:S(2)}) copy-start(s32[127,8]{0,1:T(8,128)} %param.22) | copy-start | bytes 12196
  1.2 16.1 %collective-permute-start.1 = (f32[32,2048]{1,0:T(8,128)S(1)}, f32[32,2048]{1,0:T(8,128)S(1)}, u32[]{:S(2)}, u32[]{:S(2)}) collective-permute-start(f32[32,2048]{1,0:T(8,128)S(1)} %pad_maximum_fusion), channel_id=1, source_target_pairs={{0,1},{1,0},{2,3},{3,2},{4,5},{5,4},{6,7},{7,6},{8,9},{9,8},{10,11... | collective-permute-start | bytes 786440 | tf_op jit(solution)/shard_map/ppermute | solution.py:1027
  1.3 16.0 %collective-permute-start.2 = (f32[32,2048]{1,0:T(8,128)S(1)}, f32[32,2048]{1,0:T(8,128)S(1)}, u32[]{:S(2)}, u32[]{:S(2)}) collective-permute-start(f32[32,2048]{1,0:T(8,128)S(1)} %pad_maximum_fusion.1), channel_id=1, source_target_pairs={{0,0},{1,2},{2,1},{3,4},{4,3},{5,6},{6,5},{7,8},{8,7},{9,10},{10,9... | collective-permute-start | bytes 786440 | tf_op jit(solution)/shard_map/ppermute | solution.py:1027
  15.5 8.4 %copy-start.3 = (f32[32,1664]{1,0:T(8,128)S(1)}, f32[32,1664]{1,0:T(8,128)}, u32[]{:S(2)}) copy-start(f32[32,1664]{1,0:T(8,128)} %get-tuple-element.38) | copy-start | bytes 638980
  15.6 1.8 %collective-permute-start = (f32[32,1664]{1,0:T(8,128)}, f32[32,1664]{1,0:T(8,128)S(1)}, u32[]{:S(2)}, u32[]{:S(2)}) collective-permute-start(f32[32,1664]{1,0:T(8,128)} %get-tuple-element.30), channel_id=1, source_target_pairs={{0,1},{1,0},{2,3},{3,2},{4,5},{5,4},{6,7},{7,6},{8,9},{9,8},{10,11... | collective-permute-start | bytes 638984 | tf_op jit(solution)/shard_map/ppermute | solution.py:1027
  17.3 27.8 %copy-start.2 = (f32[32,1664]{1,0:T(8,128)}, f32[32,1664]{1,0:T(8,128)S(1)}, u32[]{:S(2)}) copy-start(f32[32,1664]{1,0:T(8,128)S(1)} %collective-permute-done.inner_hbm) | copy-start | bytes 638980
  17.3 13.3 %copy-start.7 = (f32[32,2048]{1,0:T(8,128)}, f32[32,2048]{1,0:T(8,128)S(1)}, u32[]{:S(2)}) copy-start(f32[32,2048]{1,0:T(8,128)S(1)} %collective-permute-done.1.inner_hbm) | copy-start | bytes 786436
  17.3 13.3 %copy-start.8 = (f32[32,2048]{1,0:T(8,128)}, f32[32,2048]{1,0:T(8,128)S(1)}, u32[]{:S(2)}) copy-start(f32[32,2048]{1,0:T(8,128)S(1)} %collective-permute-done.2.outer_hbm) | copy-start | bytes 786436
  17.4 42.2 %all-to-all-start = ((f32[128,24,128]{2,1,0:T(8,128)}), f32[128,24,128]{2,1,0:T(8,128)S(1)}, u32[]{:S(2)}, u32[]{:S(2)}) async-start(f32[128,24,128]{2,1,0:T(8,128)} %get-tuple-element.42), calls=%async_computation | async-start | bytes 3145728 | tf_op jit(solution)/shard_map/all_to_all | solution.py:1078
  24.0 24.8 %collective-permute-start.3 = (f32[32,2048]{1,0:T(8,128)S(1)}, f32[32,2048]{1,0:T(8,128)S(1)}, u32[]{:S(2)}, u32[]{:S(2)}) collective-permute-start(f32[32,2048]{1,0:T(8,128)S(1)} %pad_maximum_fusion.2), channel_id=1, source_target_pairs={{0,0},{1,2},{2,1},{3,4},{4,3},{5,6},{6,5},{7,8},{8,7},{9,10},{10,9... | collective-permute-start | bytes 786440 | tf_op jit(solution)/shard_map/ppermute | solution.py:1027
  30.6 14.5 %copy-start.9 = (f32[32,128]{1,0:T(8,128)S(1)}, f32[32,128]{1,0:T(8,128)}, u32[]{:S(2)}) copy-start(f32[32,128]{1,0:T(8,128)} %get-tuple-element.40) | copy-start | bytes 49156
  45.2 14.3 %collective-permute-start.5 = (f32[32,128]{1,0:T(8,128)S(1)}, f32[32,128]{1,0:T(8,128)S(1)}, u32[]{:S(2)}, u32[]{:S(2)}) collective-permute-start(f32[32,128]{1,0:T(8,128)S(1)} %copy-done.9), channel_id=1, source_target_pairs={{0,0},{1,4},{2,2},{3,6},{4,1},{5,8},{6,3},{7,10},{8,5},{9,12},{10,... | collective-permute-start | bytes 49160 | tf_op jit(solution)/shard_map/ppermute | solution.py:1027
  48.8 0.7 copy-start.1
  48.8 10.7 %collective-permute-start.4 = (f32[32,896]{1,0:T(8,128)S(1)}, f32[32,896]{1,0:T(8,128)S(1)}, u32[]{:S(2)}, u32[]{:S(2)}) collective-permute-start(f32[32,896]{1,0:T(8,128)S(1)} %slice.10), channel_id=1, source_target_pairs={{0,1},{1,0},{2,3},{3,2},{4,5},{5,4},{6,7},{7,6},{8,9},{9,8},{10,11... | collective-permute-start | bytes 344072 | tf_op jit(solution)/shard_map/ppermute | solution.py:1027
  59.5 0.6 copy-start.5
  59.5 0.7 copy-start.4
  59.5 1.2 %copy-start = (f32[128,24,128]{2,1,0:T(8,128)}, f32[128,24,128]{2,1,0:T(8,128)S(1)}, u32[]{:S(2)}) copy-start(f32[128,24,128]{2,1,0:T(8,128)S(1)} %all-to-all-done.incoming_hbm) | copy-start | bytes 4718596
